TPU v7x, 32 devices: a whole 2x2x4 slice. The times are simulated.
32 devices in a mesh: dp: 8 (over z, x), fsdp: 4 (over y, core).
Axes of the slice: x: 2, y: 2, z: 4, core: 2. Of those that a mesh axis runs over, the one named last changes fastest.
Arguments:
- chars: int32 [64, 256], P(('dp', 'fsdp')), may hold values from 0 to 26
- steps: int32 [64], P(('dp', 'fsdp')), may hold values from 0 to 999
- embed: bfloat16 [13824], P(('dp', 'fsdp')), may hold values from -4 to 4
- layer_params: bfloat16 [2, 3216384], P(None, ('dp', 'fsdp')), may hold values from -2 to 2, as said below
- cotangent: bfloat16 [64, 256, 512], P(('dp', 'fsdp')), may hold values from -6 to 6
Outputs:
- out_act: bfloat16 [64, 256, 512], P(('dp', 'fsdp'))
- grad_embed: float32 [13824], P(('dp', 'fsdp'))
- grad_params: float32 [2, 3216384], P(None, ('dp', 'fsdp'))
Inputs may be any that keep to these rules, and one draw needn't show every extreme that they name: `layer_params`: parameters of 2 layers in the layout of the steps.
All inputs are finite; a program needn't handle non-finite values.
Results may differ from a plain program's by a relative error of at most 0.01.
Values may be sent and summed in bfloat16 or wider, within the bound.
No kernel may reach another device: no remote copies, remote signals or barrier semaphores. Data moves between devices by JAX's collectives and lax.ppermute only.
A program may use at most 256 MiB of HBM per device.

v0:
```python
import math

import jax
import jax.numpy as jnp
from jax import lax
from jax.sharding import PartitionSpec as P

D = 512
HEADS = 8
FF = 2048
VOCAB = 27
TD = 128
HD = 64


EPSILON = 1e-05


def timestep_embed(step_ids):
    half_dim = TD // 2
    freq_base = jnp.exp(jnp.arange(half_dim, dtype=jnp.float32) * (-math.log(10000.0) / half_dim))
    angle_grid = step_ids.astype(jnp.float32)[:, None] * freq_base[None, :]
    return jnp.concatenate([jnp.sin(angle_grid), jnp.cos(angle_grid)], axis=1)


def split_params(flat_vec):
    piece_shapes = (
        (D,),
        (D,),
        (TD, D),
        (D,),
        (D, 3 * D),
        (D, D),
        (D,),
        (D,),
        (D, FF),
        (FF,),
        (FF, D),
        (D,),
    )
    pieces_out = []
    offset_now = 0
    for piece_shape in piece_shapes:
        piece_size = math.prod(piece_shape)
        pieces_out.append(flat_vec[offset_now : offset_now + piece_size].reshape(piece_shape))
        offset_now = offset_now + piece_size
    return pieces_out


def normalize(values, gain_vec, bias_vec):
    mean_val = jnp.mean(values, -1, keepdims=True)
    centered = values - mean_val
    variance = jnp.mean(centered * centered, -1, keepdims=True)
    return centered * lax.rsqrt(variance + EPSILON) * gain_vec + bias_vec


def gelu_tanh(values):
    return jax.nn.gelu(values, approximate=True)


def dot_plain(left, right):
    return jnp.dot(left, right, preferred_element_type=jnp.float32)


def contract_rows(left, right):
    return lax.dot_general(
        left, right, (((0,), (0,)), ((), ())), preferred_element_type=jnp.float32
    )


def contract_cols(left, right):
    return lax.dot_general(
        left, right, (((1,), (1,)), ((), ())), preferred_element_type=jnp.float32
    )


def fetch_forward(shard_vec):
    return lax.all_gather(shard_vec[None, :], ("dp", "fsdp"), axis=0, tiled=True)


def fetch_backward(shard_vec):
    return lax.all_gather(shard_vec[None, :], ("dp", "fsdp"), axis=0, tiled=True)


def reduce_rows(grad_rows):
    return lax.psum_scatter(grad_rows, ("dp", "fsdp"), scatter_dimension=0, tiled=True)[0]


def split_heads(qkv_low, seq_count, seq_length):
    queries = qkv_low[:, :D].reshape(seq_count, seq_length, HEADS, HD)
    key_rows = qkv_low[:, D : 2 * D].reshape(seq_count, seq_length, HEADS, HD)
    values = qkv_low[:, 2 * D :].reshape(seq_count, seq_length, HEADS, HD)
    return (queries, key_rows, values)


def attend(queries, key_rows, values):
    head_scale = 1.0 / math.sqrt(HD)
    scores = (
        jnp.einsum("bqhe,bkhe->bhqk", queries, key_rows, preferred_element_type=jnp.float32)
        * head_scale
    )
    top_score = jnp.max(scores, -1, keepdims=True)
    log_total = top_score + jnp.log(jnp.sum(jnp.exp(scores - top_score), -1, keepdims=True))
    probs_low = jnp.exp(scores - log_total).astype(jnp.bfloat16)
    mixed = jnp.einsum("bhqk,bkhe->bqhe", probs_low, values, preferred_element_type=jnp.float32)
    return (mixed, log_total)


def attend_back(queries, key_rows, values, log_total, heads_grad_low):
    head_scale = 1.0 / math.sqrt(HD)
    scores = (
        jnp.einsum("bqhe,bkhe->bhqk", queries, key_rows, preferred_element_type=jnp.float32)
        * head_scale
    )
    prob_full = jnp.exp(scores - log_total)
    probs_low = prob_full.astype(jnp.bfloat16)
    probs_grad = jnp.einsum(
        "bqhe,bkhe->bhqk", heads_grad_low, values, preferred_element_type=jnp.float32
    )
    row_dot = jnp.sum(prob_full * probs_grad, -1, keepdims=True)
    score_grad_low = (prob_full * (probs_grad - row_dot)).astype(jnp.bfloat16)
    grad_queries = (
        jnp.einsum("bhqk,bkhe->bqhe", score_grad_low, key_rows, preferred_element_type=jnp.float32)
        * head_scale
    )
    grad_keys = (
        jnp.einsum("bhqk,bqhe->bkhe", score_grad_low, queries, preferred_element_type=jnp.float32)
        * head_scale
    )
    grad_values = jnp.einsum(
        "bhqk,bqhe->bkhe", probs_low, heads_grad_low, preferred_element_type=jnp.float32
    )
    return (grad_queries, grad_keys, grad_values)


def forward_layer(stream, emb_low, weights):
    (
        gain_one,
        bias_one,
        w_time,
        b_time,
        w_qkv,
        w_out,
        gain_two,
        bias_two,
        w_up,
        b_up,
        w_down,
        b_down,
    ) = weights
    seq_count = emb_low.shape[0]
    tok_rows = stream.shape[0]
    seq_length = tok_rows // seq_count
    time_vec = dot_plain(emb_low, w_time) + b_time.astype(jnp.float32)
    mixed_in = (stream.reshape(seq_count, seq_length, D) + time_vec[:, None, :]).reshape(
        tok_rows, D
    )
    normed_low = normalize(
        mixed_in, gain_one.astype(jnp.float32), bias_one.astype(jnp.float32)
    ).astype(jnp.bfloat16)
    qkv_low = dot_plain(normed_low, w_qkv).astype(jnp.bfloat16)
    queries, key_rows, values = split_heads(qkv_low, seq_count, seq_length)
    heads_out, log_total = attend(queries, key_rows, values)
    attn_low = heads_out.reshape(tok_rows, D).astype(jnp.bfloat16)
    after_attn = mixed_in + dot_plain(attn_low, w_out)
    normed_two = normalize(
        after_attn, gain_two.astype(jnp.float32), bias_two.astype(jnp.float32)
    ).astype(jnp.bfloat16)
    up_proj = dot_plain(normed_two, w_up) + b_up.astype(jnp.float32)
    hidden_low = gelu_tanh(up_proj).astype(jnp.bfloat16)
    result = after_attn + (dot_plain(hidden_low, w_down) + b_down.astype(jnp.float32))
    kept_state = (
        mixed_in,
        normed_low,
        queries,
        key_rows,
        values,
        log_total,
        attn_low,
        after_attn,
        normed_two,
        up_proj,
        hidden_low,
    )
    return (result, kept_state)


def backward_layer(stream_grad, emb_low, weights, kept_state):
    (
        gain_one,
        bias_one,
        w_time,
        b_time,
        w_qkv,
        w_out,
        gain_two,
        bias_two,
        w_up,
        b_up,
        w_down,
        b_down,
    ) = weights
    (
        mixed_in,
        normed_low,
        queries,
        key_rows,
        values,
        log_total,
        attn_low,
        after_attn,
        normed_two,
        up_proj,
        hidden_low,
    ) = kept_state
    seq_count = emb_low.shape[0]
    tok_rows = stream_grad.shape[0]
    seq_length = tok_rows // seq_count
    ffn_grad_low = stream_grad.astype(jnp.bfloat16)
    grad_b_down = jnp.sum(ffn_grad_low.astype(jnp.float32), 0)
    grad_w_down = contract_rows(hidden_low, ffn_grad_low)
    hidden_grad = contract_cols(ffn_grad_low, w_down)
    unused_gelu, gelu_back = jax.vjp(gelu_tanh, up_proj)
    up_grad_low = gelu_back(hidden_grad)[0].astype(jnp.bfloat16)
    grad_b_up = jnp.sum(up_grad_low.astype(jnp.float32), 0)
    grad_w_up = contract_rows(normed_two, up_grad_low)
    normed_two_grad = contract_cols(up_grad_low, w_up)
    unused_norm, second_back = jax.vjp(
        normalize, after_attn, gain_two.astype(jnp.float32), bias_two.astype(jnp.float32)
    )
    second_input_grad, grad_gain_two, grad_bias_two = second_back(normed_two_grad)
    after_grad = stream_grad + second_input_grad
    attn_grad_low = after_grad.astype(jnp.bfloat16)
    grad_w_out = contract_rows(attn_low, attn_grad_low)
    heads_grad_low = (
        contract_cols(attn_grad_low, w_out)
        .astype(jnp.bfloat16)
        .reshape(seq_count, seq_length, HEADS, HD)
    )
    grad_queries, grad_keys, grad_values = attend_back(
        queries, key_rows, values, log_total, heads_grad_low
    )
    qkv_grad_low = jnp.concatenate(
        [
            grad_queries.reshape(tok_rows, D),
            grad_keys.reshape(tok_rows, D),
            grad_values.reshape(tok_rows, D),
        ],
        1,
    ).astype(jnp.bfloat16)
    grad_w_qkv = contract_rows(normed_low, qkv_grad_low)
    normed_grad = contract_cols(qkv_grad_low, w_qkv)
    unused_first, first_back = jax.vjp(
        normalize, mixed_in, gain_one.astype(jnp.float32), bias_one.astype(jnp.float32)
    )
    first_input_grad, grad_gain_one, grad_bias_one = first_back(normed_grad)
    mixed_grad = after_grad + first_input_grad
    time_grad_low = jnp.sum(mixed_grad.reshape(seq_count, seq_length, D), 1).astype(jnp.bfloat16)
    grad_b_time = jnp.sum(time_grad_low.astype(jnp.float32), 0)
    grad_w_time = contract_rows(emb_low, time_grad_low)
    weight_grads = [
        grad_gain_one,
        grad_bias_one,
        grad_w_time,
        grad_b_time,
        grad_w_qkv,
        grad_w_out,
        grad_gain_two,
        grad_bias_two,
        grad_w_up,
        grad_b_up,
        grad_w_down,
        grad_b_down,
    ]
    return (mixed_grad, weight_grads)


def body(chars, steps, embed, layer_params, cotangent):
    seq_count, seq_length = chars.shape
    tok_rows = seq_count * seq_length
    layer_count = layer_params.shape[0]
    devices = lax.axis_size(("dp", "fsdp"))
    param_cols = layer_params.shape[1]
    embed_cols = embed.shape[0]
    emb_low = timestep_embed(steps).astype(jnp.bfloat16)
    one_hot = (chars.reshape(tok_rows, 1) == jnp.arange(VOCAB, dtype=jnp.int32)[None, :]).astype(
        jnp.bfloat16
    )
    first_rows = fetch_forward(jnp.concatenate([layer_params[0], embed]))
    char_table = first_rows[:, param_cols:].reshape(VOCAB, D)
    stream = dot_plain(one_hot, char_table)
    saved_state = []
    whole_weights = []
    for layer_index in range(layer_count):
        if layer_index == 0:
            gathered = first_rows[:, :param_cols].reshape(-1)
        else:
            gathered = fetch_forward(layer_params[layer_index]).reshape(-1)
        stream, kept_state = forward_layer(stream, emb_low, split_params(gathered))
        saved_state.append(kept_state)
        whole_weights.append(gathered)
    output = stream.astype(jnp.bfloat16).reshape(seq_count, seq_length, D)
    stream_grad = cotangent.astype(jnp.float32).reshape(tok_rows, D)
    reduced = [None] * layer_count
    for layer_index in reversed(range(layer_count)):
        gathered = fetch_backward(layer_params[layer_index]).reshape(-1)
        stream_grad, weight_grads = backward_layer(
            stream_grad, emb_low, split_params(gathered), saved_state[layer_index]
        )
        grad_rows = jnp.concatenate(
            [grad_piece.reshape(-1) for grad_piece in weight_grads]
        ).reshape(devices, param_cols)
        if layer_index == 0:
            table_grad = contract_rows(one_hot, stream_grad.astype(jnp.bfloat16))
            grad_rows = jnp.concatenate([grad_rows, table_grad.reshape(devices, embed_cols)], 1)
        reduced[layer_index] = reduce_rows(grad_rows)
    grad_embed = reduced[0][param_cols:]
    grad_params = jnp.stack([reduced[0][:param_cols]] + [reduced[1]])
    return (output, grad_embed, grad_params)


def solution(mesh):
    placed = (
        P(("dp", "fsdp"), None),
        P(("dp", "fsdp")),
        P(("dp", "fsdp")),
        P(None, ("dp", "fsdp")),
        P(("dp", "fsdp"), None, None),
    )
    return jax.shard_map(
        body,
        mesh=mesh,
        in_specs=placed,
        out_specs=(P(("dp", "fsdp"), None, None), P(("dp", "fsdp")), P(None, ("dp", "fsdp"))),
        check_vma=False,
    )
```

profile of v0, /device:TPU:0, one launch (start us, length us, event | category | flops | bytes accessed | tf_op | source)
XLA Modules:
  0.0 1291.8 jit_solution(16181139200639155183)
XLA Ops:
  14.1 4.4 dynamic-update-slice
  21.9 157.8 %all-reduce.7.cloned.1.call-done = bf16[3230208]{0:T(1024)(128)(2,1)} async-done(((bf16[3230208]{0:T(1024)(128)(2,1)}), bf16[3230208]{0:T(1024)(128)(2,1)}) %all-reduce.7.cloned.1.call-update) | async-done | bytes 6460432
  179.7 13.8 %reshape.447 = bf16[32,100944]{1,0:T(8,128)(2,1)} reshape(bf16[3230208]{0:T(1024)(128)(2,1)} %all-reduce.7.cloned.1.call-done) | data formatting | bytes 12920832 | tf_op jit(solution)/shard_map/all_gather | solution.py:78
  193.5 6.1 slice.199
  199.5 15.0 %reshape.475 = bf16[3216384]{0:T(1024)(128)(2,1)} reshape(bf16[32,100512]{1,0:T(8,128)(2,1)} %slice.199) | data formatting | bytes 12865536
  214.6 11.1 slice.155
  232.2 4.3 reshape.408
  245.2 3.4 slice.211
  256.1 4.6 reshape.412
  263.5 3.3 fusion.93
  266.8 14.2 %all-gather.6.cloned.1.call-done = bf16[32,1,100512]{2,1,0:T(2,128)(2,1)} async-done(((bf16[1,1,100512]{2,1,0:T(2,128)(2,1)}), bf16[32,1,100512]{2,1,0:T(2,128)(2,1)}) %all-gather.6.cloned.1.call-update) | async-done | bytes 6432784 | tf_op jit(solution)/shard_map/all_gather | solution.py:78
  281.0 39.5 %reduce.4 = bf16[32,100512]{1,0:T(8,128)(2,1)} reduce(bf16[32,1,100512]{2,1,0:T(2,128)(2,1)} %all-gather.6.cloned.1.call-done, bf16[]{:T(256)} %constant.58), dimensions={1}, to_apply=%all-gather.1.reduce_sub_computation | reduce | bytes 12865538 | tf_op jit(solution)/shard_map/all_gather | solution.py:78
  320.4 14.7 %reshape.473 = bf16[3216384]{0:T(1024)(128)(2,1)} reshape(bf16[32,100512]{1,0:T(8,128)(2,1)} %reduce.4) | data formatting | bytes 12865536
  335.1 11.4 slice.172
  349.5 3.4 slice.226
  352.9 4.6 reshape.414
  360.1 5.4 fusion.104
  384.7 4.3 reshape.418
  393.6 7.7 convert_reduce_fusion
  412.6 3.8 multiply_reduce_fusion.1
  422.1 39.8 %reduce.6 = bf16[32,100512]{1,0:T(8,128)(2,1)} reduce(bf16[32,1,100512]{2,1,0:T(2,128)(2,1)} %all-gather.8.cloned.1.call-done, bf16[]{:T(256)} %constant.58), dimensions={1}, to_apply=%all-gather.2.reduce_sub_computation | reduce | bytes 12865538 | tf_op jit(solution)/shard_map/all_gather | solution.py:82
  461.9 14.7 %reshape.477 = bf16[3216384]{0:T(1024)(128)(2,1)} reshape(bf16[32,100512]{1,0:T(8,128)(2,1)} %reduce.6) | data formatting | bytes 12865536
  477.3 11.5 slice.188
  488.8 3.5 slice.231
  498.6 4.2 reshape.426
  504.7 7.2 convert_reduce_fusion.1
  522.7 3.8 multiply_reduce_fusion
  537.0 4.5 reshape.431
  552.4 3.5 convolution_bitcast_fusion.3
  555.9 4.3 convolution_bitcast_fusion.2
  563.9 3.4 convolution_bitcast_fusion.1
  567.3 4.2 convolution_bitcast_fusion
  572.8 4.1 fusion.106
  576.9 4.4 reshape.434
  582.6 5.2 copy.188
  595.6 27.9 %dynamic-update-slice.17 = f32[3216384]{0:T(1024)} dynamic-update-slice(f32[3216384]{0:T(1024)} %constant_dynamic-update-slice_fusion.22, f32[786432]{0:T(1024)} %reshape.434, s32[]{} %constant.68) | dynamic-update-slice | bytes 6291460
  628.4 36.6 %dynamic-update-slice.21 = f32[3216384]{0:T(1024)} dynamic-update-slice(f32[3216384]{0:T(1024)} %constant_dynamic-update-slice_fusion.16, f32[1048576]{0:T(1024)} %bitcast.176, s32[]{} %constant.72) | dynamic-update-slice | bytes 8388612
  666.3 36.7 %dynamic-update-slice.23 = f32[3216384]{0:T(1024)} dynamic-update-slice(f32[3216384]{0:T(1024)} %constant_dynamic-update-slice_fusion.14, f32[1048576]{0:T(1024)} %bitcast.175, s32[]{} %constant.74) | dynamic-update-slice | bytes 8388612
  704.3 18.4 %reshape.438 = f32[32,100512]{1,0:T(8,128)} reshape(f32[3216384]{0:T(1024)} %constant_dynamic-update-slice_fusion.12) | data formatting | bytes 25731072 | tf_op jit(solution)/shard_map/reshape | solution.py:312
  723.4 4.4 reshape.442
  728.1 5.3 copy.193
  739.8 28.0 %dynamic-update-slice.5 = f32[3216384]{0:T(1024)} dynamic-update-slice(f32[3216384]{0:T(1024)} %constant_dynamic-update-slice_fusion.23, f32[786432]{0:T(1024)} %reshape.442, s32[]{} %constant.68) | dynamic-update-slice | bytes 6291460
  772.7 36.6 %dynamic-update-slice.9 = f32[3216384]{0:T(1024)} dynamic-update-slice(f32[3216384]{0:T(1024)} %constant_dynamic-update-slice_fusion.17, f32[1048576]{0:T(1024)} %bitcast.177, s32[]{} %constant.72) | dynamic-update-slice | bytes 8388612
  810.6 36.4 %dynamic-update-slice.11 = f32[3216384]{0:T(1024)} dynamic-update-slice(f32[3216384]{0:T(1024)} %constant_dynamic-update-slice_fusion.15, f32[1048576]{0:T(1024)} %bitcast.174, s32[]{} %constant.74) | dynamic-update-slice | bytes 8388612
  848.3 18.4 %reshape.446 = f32[32,100512]{1,0:T(8,128)} reshape(f32[3216384]{0:T(1024)} %constant_dynamic-update-slice_fusion.13) | data formatting | bytes 25731072 | tf_op jit(solution)/shard_map/reshape | solution.py:312
  866.7 12.0 pad_maximum_fusion
  879.4 5.7 fusion.43
  885.1 392.6 %all-reduce.9.cloned.1.call-done = (f32[32,100944]{1,0:T(8,128)}, f32[32,100512]{1,0:T(8,128)}) async-done(((f32[32,100944]{1,0:T(8,128)}, f32[32,100512]{1,0:T(8,128)}), (f32[32,100944]{1,0:T(8,128)}, f32[32,100512]{1,0:T(8,128)})) %all-reduce.9.cloned.1.call-update) | async-done | bytes 25786384
  (290 shorter events, 166.5 us)
Async XLA Ops:
  7.2 172.5 %all-reduce.7.cloned.1.call-start = ((), (), s32[]{:S(2)}) async-start(), calls=%async_computation | async-start | bytes 12922880
  14.1 6.2 copy-start.60
  14.1 6.2 copy-start.16
  18.5 2.6 copy-start.57
  18.6 262.4 %all-gather.6.cloned.1.call-start = ((), (), s32[]{:S(2)}) async-start(), calls=%async_computation.1 | async-start | bytes 13280256 | tf_op jit(solution)/shard_map/all_gather | solution.py:78
  19.3 402.7 %all-gather.8.cloned.1.call-start = ((), (), s32[]{:S(2)}) async-start(), calls=%async_computation.2 | async-start | bytes 13280256 | tf_op jit(solution)/shard_map/all_gather | solution.py:82
  20.1 1257.6 %all-reduce.9.cloned.1.call-start = ((), (), s32[]{:S(2)}) async-start(), calls=%async_computation.3 | async-start | bytes 51609600
  241.2 4.0 copy-start.18
  242.3 6.3 copy-start.20
  250.8 4.6 copy-start.12
  250.9 3.7 copy-start
  256.1 6.7 copy-start.25
  260.7 2.8 copy-start.11
  360.1 5.7 copy-start.50
  371.1 10.9 copy-start.13
  374.3 6.9 copy-start.22
  389.0 3.3 copy-start.10
  393.6 7.7 copy-start.30
  401.3 3.0 copy-start.17
  412.6 3.8 copy-start.3
  416.4 2.4 copy-start.23
  417.5 2.8 copy-start.14
  488.8 3.6 copy-start.45
  488.8 4.3 copy-start.44
  488.8 4.9 copy-start.40
  504.7 9.3 copy-start.28
  504.7 7.3 copy-start.41
  522.7 3.8 copy-start.1
  548.5 2.5 copy-start.26
  548.5 3.9 copy-start.49
  552.4 3.5 copy-start.29
  552.4 3.5 copy-start.32
  555.9 4.6 copy-start.8
  555.9 4.6 copy-start.39
  560.2 3.2 copy-start.27
  560.2 3.2 copy-start.43
  560.2 3.7 copy-start.47
  563.8 3.5 copy-start.31
  563.9 3.5 copy-start.56
  567.3 4.2 copy-start.58
  567.3 4.7 copy-start.52
  567.3 5.5 copy-start.37
  576.9 4.5 copy-start.35
  582.6 5.2 copy-start.34
  587.9 5.7 copy-start.53
  590.9 32.6 %copy-start.36 = (f32[64,4,8,128]{3,1,2,0:T(4,128)S(1)}, f32[64,4,8,128]{3,1,2,0:T(4,128)}, u32[]{:S(2)}) copy-start(f32[64,4,8,128]{3,1,2,0:T(4,128)} %copy.187) | copy-start | bytes 3145732
  728.1 5.3 copy-start.33
  733.4 4.4 copy-start.54
  (17 other events, 24.2 us)
Sparse Core Ops, SparseCore 0:
  18.7 160.9 all-reduce.6
  183.6 97.2 all-gather.5
  284.3 95.7 all-gather.7
  878.9 398.7 all-reduce.8
where the time goes:
time: 1310 us; the launch traced here: 1290 us
  waiting for transfers between devices  566 us (43%)
  local copies, waits for them, and re-layouts  497 us (38%)
  other arithmetic  114 us (9%)
  matrix products  99.5 us (8%)
  between operations  15.1 us (1%)
    unnamed x6, waiting for transfers between devices  552 us
    unnamed x173, local copies, waits for them, and re-layouts  311 us
    slice x9, local copies, waits for them, and re-layouts, split_params(): flat_vec[offset_now:offset_now + piece_size].reshape(piece_shape)  53.2 us
    all_gather x1, other arithmetic, fetch_backward(): lax.all_gather(shard_vec[None, :], ('dp', 'fsdp'), axis=0, tiled=True)  39.8 us
    all_gather x1, other arithmetic, fetch_forward(): lax.all_gather(shard_vec[None, :], ('dp', 'fsdp'), axis=0, tiled=True)  39.5 us
    reshape x2, local copies, waits for them, and re-layouts, body(): grad_rows = jnp.concatenate([grad_piece.reshape(-1) for grad_piece in wei...  36.8 us
    dot_general x8, matrix products, contract_cols(): lax.dot_general(left, right, (((1,), (1,)), ((), ())), preferred_element_...  27.1 us
    reshape x6, local copies, waits for them, and re-layouts, split_params(): flat_vec[offset_now:offset_now + piece_size].reshape(piece_shape)  26.5 us
  transfers between devices with their start and end apart: 4, of which 3 were waited for; matrix products, arithmetic and copies ran while one was open for 18% of the time, Pallas kernels for 0%

commit v1 on v0

v1 whole, which is shorter than its diff:
```python
import functools
import math

import jax
import jax.numpy as jnp
from jax import lax
from jax.experimental import pallas as pl
from jax.experimental.pallas import tpu as pltpu
from jax.sharding import PartitionSpec as P

D = 512
HEADS = 8
FF = 2048
VOCAB = 27
TD = 128
HD = 64
LANES = 128
EPSILON = 1e-05
AXES = ("dp", "fsdp")
F32 = jnp.float32
BF16 = jnp.bfloat16
VMEM_BYTES = 52 * 2**20

ROW_GAIN_ONE, ROW_BIAS_ONE, ROW_W_TIME, ROW_B_TIME = 0, 4, 8, 520
ROW_QKV, ROW_OUT, ROW_GAIN_TWO, ROW_BIAS_TWO = 524, 6668, 8716, 8720
ROW_UP, ROW_B_UP, ROW_DOWN, ROW_B_DOWN, ROW_END = 8724, 16916, 16932, 25124, 25128
CHUNK_PAD = 832


def ceil_to(value, step):
    return -(-value // step) * step


class Geometry:
    def __init__(self, devices, shard, embed_shard):
        self.devices, self.shard, self.embed_shard = devices, shard, embed_shard
        self.param_rows = max(self.count(d, shard) for d in range(devices))
        self.embed_rows = max(self.count(d, embed_shard) for d in range(devices))
        self.embed_at = ceil_to(self.param_rows, 8)
        self.rows = ceil_to(self.embed_at + 8, 16)

    @staticmethod
    def first(d, size):
        return d * size // LANES

    @staticmethod
    def count(d, size):
        return -(-(d + 1) * size // LANES) - d * size // LANES


def params(flops, nbytes):
    return dict(
        compiler_params=pltpu.CompilerParams(vmem_limit_bytes=VMEM_BYTES),
        cost_estimate=pl.CostEstimate(flops=flops, bytes_accessed=nbytes, transcendentals=0),
    )


VM = pl.BlockSpec(memory_space=pltpu.VMEM)
SM = pl.BlockSpec(memory_space=pltpu.SMEM)
ANY = pl.BlockSpec(memory_space=pl.ANY)


def nn(left, right):
    return lax.dot_general(left, right, (((1,), (0,)), ((), ())), preferred_element_type=F32)


def nt(left, right):
    return lax.dot_general(left, right, (((1,), (1,)), ((), ())), preferred_element_type=F32)


def tn(left, right):
    return nn(left.T, right)


def shift_in(flat, offset):
    rolled = pltpu.roll(flat, offset, 1)
    above = jnp.concatenate([jnp.zeros((1, LANES), F32), rolled[:-1]], 0)
    lane = lax.broadcasted_iota(jnp.int32, flat.shape, 1)
    return jnp.where(lane >= offset, rolled, above)


def shift_out(flat, offset):
    rolled = pltpu.roll(flat, lax.rem(LANES - offset, LANES), 1)
    below = jnp.concatenate([rolled[1:], jnp.zeros((1, LANES), F32)], 0)
    lane = lax.broadcasted_iota(jnp.int32, flat.shape, 1)
    return jnp.where(lane < LANES - offset, rolled, below)


def pack_kernel(geo, place_ref, layers_ref, embed_ref, first_ref, second_ref):
    main = geo.embed_at
    for layer, out_ref in ((0, first_ref), (1, second_ref)):
        moved = shift_in(layers_ref[layer].astype(F32), place_ref[1])
        if layer == 0:
            tail = shift_in(embed_ref[...].astype(F32), place_ref[2])
            parts = [moved[:main], tail] + ([moved[main + 8 :]] if geo.rows > main + 8 else [])
            moved = jnp.concatenate(parts, 0)
        out_ref[...] = moved.astype(BF16)


def pack_shards(geo, place, layer_params, embed):
    layers = jnp.pad(layer_params, ((0, 0), (0, geo.rows * LANES - geo.shard)))
    table = jnp.pad(embed, (0, 8 * LANES - geo.embed_shard))
    out = jax.ShapeDtypeStruct((geo.rows, LANES), BF16)
    return pl.pallas_call(
        functools.partial(pack_kernel, geo),
        out_shape=(out, out),
        in_specs=[SM, VM, VM],
        out_specs=(VM, VM),
        **params(10**6, geo.rows * 1024),
    )(place, layers.reshape(2, geo.rows, LANES), table.reshape(8, LANES))


def finish_kernel(geo, place_ref, *refs):
    n_param, n_embed = 4, 4
    firsts, seconds, tables = refs[:n_param], refs[n_param : 2 * n_param], refs[2 * n_param : 2 * n_param + n_embed]
    grads_ref, embed_ref = refs[-2:]
    for layer, parts in ((0, firsts), (1, seconds)):
        total = parts[0][...].astype(F32)
        for part in parts[1:]:
            total = total + part[...].astype(F32)
        grads_ref[layer] = shift_out(total, place_ref[1])
    total = tables[0][...].astype(F32)
    for part in tables[1:]:
        total = total + part[...].astype(F32)
    embed_ref[...] = shift_out(total, place_ref[2])


def finish(geo, place, firsts, seconds, tables):
    operands = list(firsts) + list(seconds) + list(tables)
    grads, table = pl.pallas_call(
        functools.partial(finish_kernel, geo),
        out_shape=(
            jax.ShapeDtypeStruct((2, geo.rows, LANES), F32),
            jax.ShapeDtypeStruct((8, LANES), F32),
        ),
        in_specs=[SM] + [VM] * len(operands),
        out_specs=(VM, VM),
        **params(10**6, geo.rows * 4096),
    )(place, *operands)
    grads = grads.reshape(2, geo.rows * LANES)[:, : geo.shard]
    return grads, table.reshape(-1)[: geo.embed_shard]


def unpack_kernel(geo, layer, plan, place_ref, *refs):
    n_in = len(plan)
    chunk_refs = refs[:n_in]
    w_time, w_qkv, w_out, w_up, w_down, vectors = refs[n_in : n_in + 6]
    table = refs[n_in + 6] if layer == 0 else None
    held, flat, flat_table, sems = refs[-4:]
    me = place_ref[0]
    copies = []
    for source, pieces in zip(chunk_refs, plan):
        for src_at, relative, absolute, dst_at, count in pieces:
            if absolute is None:
                target = held.at[lax.bitwise_xor(me, relative), pl.ds(dst_at, count)]
                origin = source.at[pl.ds(src_at, count)]
            else:
                target, origin = held, source
            copies.append(pltpu.make_async_copy(origin, target, sems.at[len(copies)]))
    for copy in copies:
        copy.start()
    for copy in copies:
        copy.wait()
    for d in range(geo.devices):
        block = held[d].astype(F32)
        start, rows = geo.first(d, geo.shard), geo.count(d, geo.shard)
        split = (d * geo.shard) % LANES != 0
        if split:
            shared = flat[pl.ds(start, 1), :] + block[:1]
        flat[pl.ds(start, rows), :] = block[:rows]
        if split:
            flat[pl.ds(start, 1), :] = shared
        if layer == 0:
            tail = block[geo.embed_at : geo.embed_at + 8]
            start, rows = geo.first(d, geo.embed_shard), geo.count(d, geo.embed_shard)
            split = (d * geo.embed_shard) % LANES != 0
            if split:
                shared = flat_table[pl.ds(start, 1), :] + tail[:1]
            flat_table[pl.ds(start, rows), :] = tail[:rows]
            if split:
                flat_table[pl.ds(start, 1), :] = shared
    for out, start, rows, width in (
        (w_time, ROW_W_TIME, TD, 4),
        (w_qkv, ROW_QKV, D, 12),
        (w_out, ROW_OUT, D, 4),
        (w_up, ROW_UP, D, 16),
        (w_down, ROW_DOWN, FF, 4),
    ):
        for c in range(width):
            out[:, c * LANES : (c + 1) * LANES] = flat[pl.ds(start + c, rows, stride=width), :].astype(BF16)
    for row, start, width in (
        (0, ROW_GAIN_ONE, 4),
        (1, ROW_BIAS_ONE, 4),
        (2, ROW_B_TIME, 4),
        (3, ROW_GAIN_TWO, 4),
        (4, ROW_BIAS_TWO, 4),
        (5, ROW_B_DOWN, 4),
        (6, ROW_B_UP, 16),
    ):
        for c in range(width):
            vectors[row : row + 1, c * LANES : (c + 1) * LANES] = flat[pl.ds(start + c, 1), :]
    if layer == 0:
        table[...] = jnp.zeros(table.shape, BF16)
        for c in range(4):
            table[0:VOCAB, c * LANES : (c + 1) * LANES] = flat_table[pl.ds(c, VOCAB, stride=4), :].astype(BF16)


def unpack(geo, layer, place, gathered):
    arrays = [array for array, pieces in gathered]
    plan = tuple(tuple(pieces) for array, pieces in gathered)
    shapes = [
        jax.ShapeDtypeStruct((TD, D), BF16),
        jax.ShapeDtypeStruct((D, 3 * D), BF16),
        jax.ShapeDtypeStruct((D, D), BF16),
        jax.ShapeDtypeStruct((D, FF), BF16),
        jax.ShapeDtypeStruct((FF, D), BF16),
        jax.ShapeDtypeStruct((8, FF), F32),
    ]
    if layer == 0:
        shapes.append(jax.ShapeDtypeStruct((32, D), BF16))
    return pl.pallas_call(
        functools.partial(unpack_kernel, geo, layer, plan),
        out_shape=tuple(shapes),
        in_specs=[SM] + [ANY] * len(arrays),
        out_specs=(VM,) * len(shapes),
        scratch_shapes=[
            pltpu.VMEM((geo.devices, geo.rows, LANES), BF16),
            pltpu.VMEM((ROW_END + 8, LANES), F32),
            pltpu.VMEM((4 * 32, LANES), F32),
            pltpu.SemaphoreType.DMA((sum(len(pieces) for pieces in plan),)),
        ],
        **params(10**7, 4 * 6432768),
    )(place, *arrays)


def norm_stats(values):
    mean = jnp.mean(values, -1, keepdims=True)
    centered = values - mean
    variance = jnp.mean(centered * centered, -1, keepdims=True)
    scale = lax.rsqrt(variance + EPSILON)
    return centered * scale, scale


def norm_back(grad, values, gain):
    unit, scale = norm_stats(values)
    grad_gain = jnp.sum(grad * unit, 0, keepdims=True)
    grad_bias = jnp.sum(grad, 0, keepdims=True)
    inner = grad * gain
    shifted = inner - jnp.mean(inner, -1, keepdims=True)
    return scale * (shifted - unit * jnp.mean(inner * unit, -1, keepdims=True)), grad_gain, grad_bias


def gelu_both(u):
    root = math.sqrt(2.0 / math.pi)
    square = u * u
    t = jnp.tanh(root * (u + 0.044715 * (square * u)))
    half = 0.5 * (1.0 + t)
    slope = half + 0.5 * u * (1.0 - t * t) * (root * (1.0 + 3.0 * 0.044715 * square))
    return u * half, slope


def head_masks(shape, scale):
    lane = lax.broadcasted_iota(jnp.int32, shape, 1)
    one = jnp.where(lane < HD, scale, 0.0).astype(BF16)
    two = jnp.where(lane < HD, 0.0, scale).astype(BF16)
    return one, two


def forward_kernel(layer, seqs, *refs):
    if layer == 0:
        chars, table = refs[:2]
        refs = refs[2:]
    else:
        stream_in = refs[0]
        refs = refs[1:]
    emb, w_time, w_qkv, w_out, w_up, w_down, vectors = refs[:7]
    stream_out, x_out, a_out, qkv_out, prob_out, o_out, x2_out, a2_out, gl_out, slope_out = refs[7:]
    tokens = x_out.shape[0]
    length = tokens // seqs
    time_vec = nn(emb[...], w_time[...]) + vectors[2:3, :D]
    if layer == 0:
        lane = lax.broadcasted_iota(jnp.int32, (tokens, 32), 1)
        stream = nn((chars[...] == lane).astype(BF16), table[...])
    else:
        stream = stream_in[...]
    for s in range(seqs):
        x_out[s * length : (s + 1) * length, :] = stream[s * length : (s + 1) * length] + time_vec[s : s + 1]
    unit, _ = norm_stats(x_out[...])
    a_out[...] = (unit * vectors[0:1, :D] + vectors[1:2, :D]).astype(BF16)
    for c in range(3):
        part = slice(c * D, (c + 1) * D)
        qkv_out[:, part] = nn(a_out[...], w_qkv[:, part]).astype(BF16)
    masks = head_masks((length, LANES), 1.0 / math.sqrt(HD))
    for s in range(seqs):
        rows = slice(s * length, (s + 1) * length)
        for pair in range(HEADS // 2):
            cols = slice(pair * LANES, (pair + 1) * LANES)
            q = qkv_out[rows, pair * LANES : (pair + 1) * LANES]
            k = qkv_out[rows, D + pair * LANES : D + (pair + 1) * LANES]
            v_t = qkv_out[rows, 2 * D + pair * LANES : 2 * D + (pair + 1) * LANES].T
            mixed = []
            for h in range(2):
                scores = nt(k * masks[h], q)
                top = jnp.max(scores, 0, keepdims=True)
                expd = jnp.exp(scores - top)
                prob = (expd / jnp.sum(expd, 0, keepdims=True)).astype(BF16)
                prob_out[s * HEADS + 2 * pair + h] = prob
                mixed.append(nn(v_t[h * HD : (h + 1) * HD], prob))
            o_out[rows, cols] = jnp.concatenate(mixed, 0).T.astype(BF16)
    x2_out[...] = x_out[...] + nn(o_out[...], w_out[...])
    unit, _ = norm_stats(x2_out[...])
    a2_out[...] = (unit * vectors[3:4, :D] + vectors[4:5, :D]).astype(BF16)
    total = x2_out[...] + vectors[5:6, :D]
    for c in range(4):
        part = slice(c * D, (c + 1) * D)
        u = nn(a2_out[...], w_up[:, part]) + vectors[6:7, part]
        gl, slope = gelu_both(u)
        gl_out[:, part] = gl.astype(BF16)
        slope_out[:, part] = slope.astype(BF16)
        total = total + nn(gl_out[:, part], w_down[part, :])
    stream_out[...] = total.astype(stream_out.dtype)


def forward(layer, seqs, tokens, first_inputs, emb, weights, out_dtype):
    length = tokens // seqs
    shapes = (
        jax.ShapeDtypeStruct((tokens, D), out_dtype),
        jax.ShapeDtypeStruct((tokens, D), F32),
        jax.ShapeDtypeStruct((tokens, D), BF16),
        jax.ShapeDtypeStruct((tokens, 3 * D), BF16),
        jax.ShapeDtypeStruct((seqs * HEADS, length, length), BF16),
        jax.ShapeDtypeStruct((tokens, D), BF16),
        jax.ShapeDtypeStruct((tokens, D), F32),
        jax.ShapeDtypeStruct((tokens, D), BF16),
        jax.ShapeDtypeStruct((tokens, FF), BF16),
        jax.ShapeDtypeStruct((tokens, FF), BF16),
    )
    operands = list(first_inputs) + [emb] + list(weights)
    return pl.pallas_call(
        functools.partial(forward_kernel, layer, seqs),
        out_shape=shapes,
        in_specs=[VM] * len(operands),
        out_specs=(VM,) * len(shapes),
        **params(2 * tokens * 3216384 * 2, 3 * 10**7),
    )(*operands)


def place_chunks(geo, owners, flat, base, me, outs, fast):
    for d in owners:
        block = flat[pl.ds(geo.first(d, geo.shard) - base, geo.rows), :].astype(BF16)
        if fast:
            keep, send = outs
            relative = lax.bitwise_xor(me, d)
            row = lax.bitwise_and(relative, 4) + lax.bitwise_and(relative, 2)
            row = row + lax.bitwise_and(lax.shift_right_logical(relative, 3), 1)
            core = lax.bitwise_and(relative, 1)

            @pl.when(core == 0)
            def _():
                keep[row] = block

            @pl.when(core == 1)
            def _():
                send[row] = block
        else:
            outs[0][d - owners[0]] = block


def back_mlp_kernel(geo, layer, fast, place_ref, grad, x2, a2, gl, slope, w_up, w_down, vectors, *refs):
    grad_out, rest_out = refs[:2]
    outs = refs[2:-1]
    flat = refs[-1]
    base = ROW_GAIN_TWO
    tokens = x2.shape[0]
    grad_in = grad[...].astype(F32)
    grad_low = grad_in.astype(BF16)
    flat[pl.ds(ROW_END - base, CHUNK_PAD), :] = jnp.zeros((CHUNK_PAD, LANES), F32)
    grad_bias = jnp.sum(grad_low.astype(F32), 0, keepdims=True)
    for c in range(4):
        flat[pl.ds(ROW_B_DOWN - base + c, 1), :] = grad_bias[:, c * LANES : (c + 1) * LANES]
    normed_grad = jnp.zeros((tokens, D), F32)
    for j in range(4):
        part = slice(j * D, (j + 1) * D)
        hidden = nt(grad_low, w_down[part, :])
        up_grad = (hidden * slope[:, part].astype(F32)).astype(BF16)
        bias_grad = jnp.sum(up_grad.astype(F32), 0, keepdims=True)
        down = tn(gl[:, part], grad_low)
        up = tn(a2[...], up_grad)
        for c in range(4):
            cols = slice(c * LANES, (c + 1) * LANES)
            flat[pl.ds(ROW_B_UP - base + 4 * j + c, 1), :] = bias_grad[:, cols]
            flat[pl.ds(ROW_DOWN - base + 4 * D * j + c, D, stride=4), :] = down[:, cols]
            flat[pl.ds(ROW_UP - base + 4 * j + c, D, stride=16), :] = up[:, cols]
        normed_grad = normed_grad + nt(up_grad, w_up[:, part])
    back, grad_gain, grad_bias = norm_back(normed_grad, x2[...], vectors[3:4, :D])
    grad_out[...] = grad_in + back
    for c in range(4):
        cols = slice(c * LANES, (c + 1) * LANES)
        flat[pl.ds(ROW_GAIN_TWO - base + c, 1), :] = grad_gain[:, cols]
        flat[pl.ds(ROW_BIAS_TWO - base + c, 1), :] = grad_bias[:, cols]
    rest_out[...] = flat[pl.ds(0, rest_out.shape[0]), :]
    owners = list(range(geo.devices // 2, geo.devices))
    place_chunks(geo, owners, flat, base, place_ref[0], outs, fast)


def chunk_shapes(geo, fast):
    if fast:
        shape = jax.ShapeDtypeStruct((geo.devices // 4, geo.rows, LANES), BF16)
        return (shape, shape)
    return (jax.ShapeDtypeStruct((geo.devices // 2, geo.rows, LANES), BF16),)


def rest_rows(geo):
    middle = geo.first(geo.devices // 2, geo.shard)
    return ceil_to(middle + geo.rows - ROW_GAIN_TWO, 8)


def back_mlp(geo, layer, fast, place, grad, kept, weights):
    x2, a2, gl, slope = kept
    w_up, w_down, vectors = weights
    tokens = x2.shape[0]
    chunks = chunk_shapes(geo, fast)
    return pl.pallas_call(
        functools.partial(back_mlp_kernel, geo, layer, fast),
        out_shape=(
            jax.ShapeDtypeStruct((tokens, D), F32),
            jax.ShapeDtypeStruct((rest_rows(geo), LANES), F32),
        )
        + chunks,
        in_specs=[SM] + [VM] * 8,
        out_specs=(VM,) * (2 + len(chunks)),
        scratch_shapes=[pltpu.VMEM((ROW_END - ROW_GAIN_TWO + CHUNK_PAD, LANES), F32)],
        **params(4 * tokens * 2100000 * 2, 2 * 10**7),
    )(place, grad, x2, a2, gl, slope, w_up, w_down, vectors)


def back_attn_kernel(geo, layer, fast, seqs, place_ref, grad, x, a, qkv, prob, o, w_qkv, w_out, vectors, emb_t, rest, *refs):
    if layer == 0:
        chars = refs[0]
        refs = refs[1:]
    n_chunks = 2 if fast else 1
    if layer == 0:
        outs, embed_outs = refs[:n_chunks], refs[n_chunks : 2 * n_chunks]
        flat, qkv_grad, heads_grad, flat_table = refs[2 * n_chunks :]
    else:
        grad_out = refs[0]
        outs = refs[1 : 1 + n_chunks]
        flat, qkv_grad, heads_grad = refs[1 + n_chunks :]
    tokens = x.shape[0]
    length = tokens // seqs
    me = place_ref[0]
    flat[pl.ds(ROW_GAIN_TWO, rest.shape[0]), :] = rest[...]
    grad_in = grad[...]
    grad_low = grad_in.astype(BF16)
    out_grad = tn(o[...], grad_low)
    for c in range(4):
        flat[pl.ds(ROW_OUT + c, D, stride=4), :] = out_grad[:, c * LANES : (c + 1) * LANES]
    heads_grad[...] = nt(grad_low, w_out[...]).astype(BF16)
    masks = head_masks((length, LANES), 1.0)
    scale = 1.0 / math.sqrt(HD)
    lane = lax.broadcasted_iota(jnp.int32, (length, LANES), 1)
    for s in range(seqs):
        rows = slice(s * length, (s + 1) * length)
        for pair in range(HEADS // 2):
            cols = [slice(c * D + pair * LANES, c * D + (pair + 1) * LANES) for c in range(3)]
            q, k, v = qkv[rows, cols[0]], qkv[rows, cols[1]], qkv[rows, cols[2]]
            go = heads_grad[rows, cols[0]]
            k_t = k.T
            to_q, to_k, to_v = [], [], []
            for h in range(2):
                prob_low = prob[s * HEADS + 2 * pair + h]
                prob_full = prob_low.astype(F32)
                prob_grad = nt(v * masks[h], go)
                weighted = prob_full * prob_grad
                row_dot = jnp.sum(weighted, 0, keepdims=True)
                score_grad = (weighted - prob_full * row_dot).astype(BF16)
                to_q.append(nn(k_t[h * HD : (h + 1) * HD], score_grad))
                to_k.append(nn(score_grad, q))
                to_v.append(nn(prob_low, go))
            qkv_grad[rows, cols[0]] = (jnp.concatenate(to_q, 0).T * scale).astype(BF16)
            qkv_grad[rows, cols[1]] = (jnp.where(lane < HD, to_k[0], to_k[1]) * scale).astype(BF16)
            qkv_grad[rows, cols[2]] = jnp.where(lane < HD, to_v[0], to_v[1]).astype(BF16)
    normed_grad = jnp.zeros((tokens, D), F32)
    a_t = a[...].T
    for part in range(3):
        cols = slice(part * D, (part + 1) * D)
        piece = nn(a_t, qkv_grad[:, cols])
        for c in range(4):
            flat[pl.ds(ROW_QKV + 4 * part + c, D, stride=12), :] = piece[:, c * LANES : (c + 1) * LANES]
        normed_grad = normed_grad + nt(qkv_grad[:, cols], w_qkv[:, cols])
    back, grad_gain, grad_bias = norm_back(normed_grad, x[...], vectors[0:1, :D])
    total = grad_in + back
    if layer != 0:
        grad_out[...] = total
    time_grad = [
        jnp.sum(total[s * length : (s + 1) * length], 0, keepdims=True).astype(BF16).astype(F32) for s in range(seqs)
    ]
    bias_grad = sum(time_grad[1:], time_grad[0])
    weight_grad = sum(emb_t[:, s : s + 1] * time_grad[s] for s in range(seqs))
    for c in range(4):
        cols = slice(c * LANES, (c + 1) * LANES)
        flat[pl.ds(ROW_GAIN_ONE + c, 1), :] = grad_gain[:, cols]
        flat[pl.ds(ROW_BIAS_ONE + c, 1), :] = grad_bias[:, cols]
        flat[pl.ds(ROW_B_TIME + c, 1), :] = bias_grad[:, cols]
        flat[pl.ds(ROW_W_TIME + c, TD, stride=4), :] = weight_grad[:, cols]
    place_chunks(geo, list(range(geo.devices // 2)), flat, 0, me, outs, fast)
    if layer == 0:
        kind = lax.broadcasted_iota(jnp.int32, (32, tokens), 0)
        table_grad = nn((chars[...] == kind).astype(BF16), total.astype(BF16))
        for c in range(4):
            flat_table[pl.ds(c, 32, stride=4), :] = table_grad[:, c * LANES : (c + 1) * LANES]
        for d in range(geo.devices):
            block = flat_table[pl.ds(geo.first(d, geo.embed_shard), 8), :]
            if fast:
                relative = lax.bitwise_xor(me, d)
                row = lax.shift_right_logical(relative, 1)
                core = lax.bitwise_and(relative, 1)

                @pl.when(core == 0)
                def _():
                    embed_outs[0][row] = block

                @pl.when(core == 1)
                def _():
                    embed_outs[1][row] = block
            else:
                embed_outs[0][d] = block


def back_attn(geo, layer, fast, seqs, place, grad, kept, weights, emb_t, rest, chars_row):
    x, a, qkv, prob, o = kept
    w_qkv, w_out, vectors = weights
    tokens = x.shape[0]
    chunks = chunk_shapes(geo, fast)
    shapes = () if layer == 0 else (jax.ShapeDtypeStruct((tokens, D), F32),)
    shapes = shapes + chunks
    operands = [grad, x, a, qkv, prob, o, w_qkv, w_out, vectors, emb_t, rest]
    scratch = [
        pltpu.VMEM((ROW_GAIN_TWO + rest.shape[0], LANES), F32),
        pltpu.VMEM((tokens, 3 * D), BF16),
        pltpu.VMEM((tokens, D), BF16),
    ]
    if layer == 0:
        operands.append(chars_row)
        if fast:
            tables = (jax.ShapeDtypeStruct((geo.devices // 2, 8, LANES), F32),) * 2
        else:
            tables = (jax.ShapeDtypeStruct((geo.devices, 8, LANES), F32),)
        shapes = shapes + tables
        scratch.append(pltpu.VMEM((4 * 32, LANES), F32))
    return pl.pallas_call(
        functools.partial(back_attn_kernel, geo, layer, fast, seqs),
        out_shape=shapes,
        in_specs=[SM] + [VM] * len(operands),
        out_specs=(VM,) * len(shapes),
        scratch_shapes=scratch,
        **params(4 * tokens * 1100000 * 2, 2 * 10**7),
    )(place, *operands)


def permute(value, distance, devices):
    return lax.ppermute(value, AXES, [(d, d ^ distance) for d in range(devices)])


Z1, Z2, Z3, X, Y, CORE = 8, 16, 24, 4, 2, 1


def gather_fast(geo, chunk):
    n, rows = geo.devices, geo.rows
    half = ceil_to(rows // 2, 16)
    column = jnp.concatenate([chunk] + [permute(chunk, k, n) for k in (Z1, Z2, Z3)], 0)
    over_x, over_y = permute(column, X, n), permute(column, Y, n)
    cut_x = over_x.reshape(4, rows, LANES)[:, :half].reshape(-1, LANES)
    cut_y = over_y.reshape(4, rows, LANES)[:, half:].reshape(-1, LANES)
    corner_one, corner_two = permute(cut_x, Y, n), permute(cut_y, X, n)
    found = []
    for array, relative, at, count in (
        (column, 0, 0, rows),
        (over_x, X, 0, rows),
        (over_y, Y, 0, rows),
        (corner_one, X + Y, 0, half),
        (corner_two, X + Y, half, rows - half),
    ):
        for core in (0, CORE):
            held = permute(array, core, n) if core else array
            pieces = [(z * count, relative + core + 8 * z, None, at, count) for z in range(4)]
            found.append((held, pieces))
    return found


def gather_any(geo, chunk):
    gathered = lax.all_gather(chunk, AXES, axis=0)
    return [(gathered, [(0, 0, 0, 0, 0)])]


def add(*values):
    total = values[0].astype(F32)
    for value in values[1:]:
        total = total + value.astype(F32)
    return total


def plane_sum(geo, keep, send):
    n, rows = geo.devices, geo.rows
    half = ceil_to(rows // 2, 16)
    keep = keep.reshape(2, 2, 2, rows, LANES)
    came = permute(send, CORE, n).reshape(2, 2, 2, rows, LANES)
    one = add(keep[:, :, :, :half], came[:, :, :, :half])
    two = add(keep[:, :, :, half:], came[:, :, :, half:])
    from_x = permute(one[1].astype(BF16), X, n)
    from_y = permute(two[:, 1].astype(BF16), Y, n)
    one = add(one[0], from_x)
    two = add(two[:, 0], from_y)
    from_y = permute(one[1].astype(BF16), Y, n)
    from_x = permute(two[1].astype(BF16), X, n)
    return jnp.concatenate([add(one[0], from_y), add(two[0], from_x)], 1)


def column_sum(geo, place, upper, lower):
    n = geo.devices
    is_upper = place[3] >= 2
    near = jnp.where(is_upper, upper, lower)
    far = jnp.where(is_upper, lower, upper).astype(BF16)
    return [near[0], permute(near[1].astype(BF16), Z1, n), permute(far[0], Z2, n), permute(far[1], Z3, n)]


def table_sum(geo, keep, send):
    n = geo.devices
    total = add(keep, permute(send.astype(BF16), CORE, n)).reshape(4, 2, 2, 8, LANES)
    total = add(total[:, 0], permute(total[:, 1].astype(BF16), X, n))
    total = add(total[:, 0], permute(total[:, 1].astype(BF16), Y, n))
    low = total.astype(BF16)
    return [total[0]] + [permute(low[k], 8 * k, n) for k in (1, 2, 3)]


def sum_any(chunks):
    total = lax.psum_scatter(chunks.astype(F32), AXES, scatter_dimension=0, tiled=True)[0]
    zero = jnp.zeros_like(total)
    return [total, zero, zero, zero]


def timestep_embed(step_ids):
    half_dim = TD // 2
    freq_base = jnp.exp(jnp.arange(half_dim, dtype=F32) * (-math.log(10000.0) / half_dim))
    angle_grid = step_ids.astype(F32)[:, None] * freq_base[None, :]
    return jnp.concatenate([jnp.sin(angle_grid), jnp.cos(angle_grid)], axis=1)


def body(fast, chars, steps, embed, layer_params, cotangent):
    seqs, length = chars.shape
    tokens = seqs * length
    geo = Geometry(lax.axis_size(AXES), layer_params.shape[1], embed.shape[0])
    index = lax.axis_index(AXES).astype(jnp.int32)
    place = jnp.stack(
        [index, index * geo.shard % LANES, index * geo.embed_shard % LANES, index // 8]
    ).astype(jnp.int32)
    gather = gather_fast if fast else gather_any
    chunks = pack_shards(geo, place, layer_params, embed)
    emb = timestep_embed(steps).astype(BF16)
    emb_rows = jnp.concatenate([emb, jnp.zeros((8 - seqs, TD), BF16)], 0) if seqs < 8 else emb
    emb_t = emb.astype(F32).T
    gathered = [gather(geo, chunk) for chunk in chunks]

    stream = None
    kept, weights = [], []
    for layer in range(2):
        got = unpack(geo, layer, place, gathered[layer])
        if layer == 0:
            first_inputs = [chars.reshape(tokens, 1), got[6]]
        else:
            first_inputs = [stream]
        stream, *saved = forward(
            layer, seqs, tokens, first_inputs, emb_rows, got[:6], F32 if layer == 0 else BF16
        )
        kept.append(saved)
        weights.append(got[:6])
    output = stream.reshape(seqs, length, D)

    grad = cotangent.reshape(tokens, D)
    sums = [None, None]
    for layer in (1, 0):
        x, a, qkv, prob, o, x2, a2, gl, slope = kept[layer]
        w_time, w_qkv, w_out, w_up, w_down, vectors = weights[layer]
        grad, rest, *upper = back_mlp(
            geo, layer, fast, place, grad, (x2, a2, gl, slope), (w_up, w_down, vectors)
        )
        if fast:
            upper = plane_sum(geo, *upper)
        got = back_attn(
            geo,
            layer,
            fast,
            seqs,
            place,
            grad,
            (x, a, qkv, prob, o),
            (w_qkv, w_out, vectors),
            emb_t,
            rest,
            chars.reshape(1, tokens),
        )
        if layer == 0:
            lower, tables = (got[:2], got[2:]) if fast else (got[:1], got[1:])
        else:
            grad, *lower = got
        if fast:
            sums[layer] = column_sum(geo, place, upper, plane_sum(geo, *lower))
        else:
            sums[layer] = sum_any(jnp.concatenate([lower[0], upper[0]], 0))
    tables = table_sum(geo, *tables) if fast else sum_any(tables[0])
    grad_params, grad_embed = finish(geo, place, sums[0], sums[1], tables)
    return (output, grad_embed, grad_params)


def solution(mesh):
    both = P(AXES)
    fast = dict(mesh.shape) == {"dp": 8, "fsdp": 4}
    return jax.shard_map(
        functools.partial(body, fast),
        mesh=mesh,
        in_specs=(P(AXES, None), both, both, P(None, AXES), P(AXES, None, None)),
        out_specs=(P(AXES, None, None), both, P(None, AXES)),
        check_vma=False,
    )
```

time: 1310 us -> 337 us (0.26); the launches traced: 1290 us -> 333 us
  local copies, waits for them, and re-layouts: 497 us -> 16 us
  waiting for transfers between devices: 566 us -> 119 us
  Pallas kernels: 0 us -> 113 us
  other arithmetic: 114 us -> 8.01 us
  matrix products: 99.5 us -> 0 us
  starting transfers between devices: 0.33 us -> 76.4 us
  between operations: 15.1 us -> 1.61 us
    unnamed x6 -> x0, waiting for transfers between devices: 552 us -> none
    unnamed x173 -> x39, local copies, waits for them, and re-layouts: 311 us -> 7.94 us
    ppermute x0 -> x56, waiting for transfers between devices: none -> 119 us  [permute(): lax.ppermute(value, AXES, [(d, d ^ distance) for d in range(devices)])]
    pallas_call x0 -> x10, Pallas kernels: none -> 113 us  [the longest x2 34.9 us: forward(): pl.pallas_call(functools.partial(forward_kernel, layer, seqs), out_shape=...]
    dot_general x42 -> x0, matrix products: 99.5 us -> none  [the longest x8 27.1 us: contract_cols(): lax.dot_general(left, right, (((1,), (1,)), ((), ())), preferred_element_...]
    reshape x28 -> x1, local copies, waits for them, and re-layouts: 98.4 us -> 0.01 us  [pack_shards(): table.reshape(8, LANES)]
    all_gather x2 -> x0, other arithmetic: 79.3 us -> none  [the longest x1 39.8 us: fetch_backward(): lax.all_gather(shard_vec[None, :], ('dp', 'fsdp'), axis=0, tiled=True)]
    ppermute x0 -> x56, starting transfers between devices: none -> 76.4 us  [permute(): lax.ppermute(value, AXES, [(d, d ^ distance) for d in range(devices)])]
  transfers between devices with their start and end apart: 4 -> 56, of which waited for: 3 -> 27; matrix products, arithmetic and copies ran while one was open for 18% -> 5% of each run, Pallas kernels for 0% -> 12%
where the time goes in v1:
time: 337 us; the launch traced here: 333 us
  waiting for transfers between devices  119 us (35%)
  Pallas kernels  113 us (34%)
  starting transfers between devices  76.4 us (23%)
  local copies, waits for them, and re-layouts  16 us (5%)
  other arithmetic  8.01 us (2%)
    ppermute x56, waiting for transfers between devices, permute(): lax.ppermute(value, AXES, [(d, d ^ distance) for d in range(devices)])  119 us
    ppermute x56, starting transfers between devices, permute(): lax.ppermute(value, AXES, [(d, d ^ distance) for d in range(devices)])  76.4 us
    pallas_call x2, Pallas kernels, forward(): pl.pallas_call(functools.partial(forward_kernel, layer, seqs), out_shape=...  34.9 us
    pallas_call x2, Pallas kernels, back_attn(): pl.pallas_call(functools.partial(back_attn_kernel, geo, layer, fast, seqs...  30.3 us
    pallas_call x2, Pallas kernels, back_mlp(): pl.pallas_call(functools.partial(back_mlp_kernel, geo, layer, fast), out_...  26.9 us
    pallas_call x2, Pallas kernels, unpack(): pl.pallas_call(functools.partial(unpack_kernel, geo, layer, plan), out_sh...  17.8 us
    unnamed x39, local copies, waits for them, and re-layouts  7.94 us
    add x26, other arithmetic, add(): total = total + value.astype(F32)  7.3 us
  transfers between devices with their start and end apart: 56, of which 27 were waited for; matrix products, arithmetic and copies ran while one was open for 5% of the time, Pallas kernels for 12%

profile of v1, /device:TPU:0, one launch (start us, length us, event | category | flops | bytes accessed | tf_op | source)
XLA Modules:
  0.0 333.5 jit_solution(3692262183314879806)
XLA Ops:
  3.0 3.1 collective-permute-start.12
  6.1 2.6 collective-permute-start.13
  9.6 3.5 %collective-permute-start.1 = (bf16[800,128]{1,0:T(8,128)(2,1)S(1)}, bf16[800,128]{1,0:T(8,128)(2,1)S(1)}, u32[]{:S(2)}, u32[]{:S(2)}) collective-permute-start(bf16[800,128]{1,0:T(8,128)(2,1)S(1)} %get-tuple-element.55), channel_id=1, source_target_pairs={{0,16},{1,17},{2,18},{3,19},{4,20},{5,21},{6,22},{7,23},{8,24},{9,... | collective-permute-start | bytes 614408 | tf_op jit(solution)/shard_map/ppermute | solution.py:562
  13.8 1.8 collective-permute-done.12
  15.6 4.6 %collective-permute-start.2 = (bf16[800,128]{1,0:T(8,128)(2,1)S(1)}, bf16[800,128]{1,0:T(8,128)(2,1)S(1)}, u32[]{:S(2)}, u32[]{:S(2)}) collective-permute-start(bf16[800,128]{1,0:T(8,128)(2,1)S(1)} %get-tuple-element.55), channel_id=1, source_target_pairs={{0,24},{1,25},{2,26},{3,27},{4,28},{5,29},{6,30},{7,31},{8,16},{9,... | collective-permute-start | bytes 614408 | tf_op jit(solution)/shard_map/ppermute | solution.py:562
  20.9 2.9 collective-permute-done.13
  26.7 14.6 %collective-permute-done.1 = bf16[800,128]{1,0:T(8,128)(2,1)S(1)} collective-permute-done((bf16[800,128]{1,0:T(8,128)(2,1)S(1)}, bf16[800,128]{1,0:T(8,128)(2,1)S(1)}, u32[]{:S(2)}, u32[]{:S(2)}) %collective-permute-start.1) | collective-permute-done | bytes 204832 | tf_op jit(solution)/shard_map/ppermute | solution.py:562
  41.4 1.6 collective-permute-start.6
  46.1 1.6 collective-permute-start.20
  47.7 15.1 %collective-permute-done.6.refs_4_ = bf16[3200,128]{1,0:T(8,128)(2,1)} collective-permute-done((bf16[3200,128]{1,0:T(8,128)(2,1)S(1)}, bf16[3200,128]{1,0:T(8,128)(2,1)}, u32[]{:S(2)}, u32[]{:S(2)}) %collective-permute-start.6) | collective-permute-done | bytes 819232 | tf_op jit(solution)/shard_map/ppermute | solution.py:562
  66.4 1.6 collective-permute-start.8
  68.0 12.3 %collective-permute-done.18.refs_4_ = bf16[3200,128]{1,0:T(8,128)(2,1)} collective-permute-done((bf16[3200,128]{1,0:T(8,128)(2,1)}, bf16[3200,128]{1,0:T(8,128)(2,1)}, u32[]{:S(2)}, u32[]{:S(2)}) %collective-permute-start.18) | collective-permute-done | bytes 819232 | tf_op jit(solution)/shard_map/ppermute | solution.py:562
  81.9 7.1 %collective-permute-done.20.refs_6_ = bf16[1600,128]{1,0:T(8,128)(2,1)S(1)} collective-permute-done((bf16[1600,128]{1,0:T(8,128)(2,1)S(1)}, bf16[1600,128]{1,0:T(8,128)(2,1)S(1)}, u32[]{:S(2)}, u32[]{:S(2)}) %collective-permute-start.20) | collective-permute-done | bytes 409632 | tf_op jit(solution)/shard_map/ppermute | solution.py:562
  90.5 3.5 %collective-permute-done.8.refs_6_ = bf16[1600,128]{1,0:T(8,128)(2,1)S(1)} collective-permute-done((bf16[1600,128]{1,0:T(8,128)(2,1)S(1)}, bf16[1600,128]{1,0:T(8,128)(2,1)S(1)}, u32[]{:S(2)}, u32[]{:S(2)}) %collective-permute-start.8) | collective-permute-done | bytes 409632 | tf_op jit(solution)/shard_map/ppermute | solution.py:562
  94.0 2.9 collective-permute-done.22.refs_8_
  98.7 9.1 %shard_map.77 = (bf16[128,512]{1,0:T(8,128)(2,1)S(1)}, bf16[512,1536]{1,0:T(8,128)(2,1)}, bf16[512,512]{1,0:T(8,128)(2,1)}, bf16[512,2048]{1,0:T(8,128)(2,1)}, b...) custom-call(s32[4]{0:T(128)S(1)} %pad_add_fusion.place_ref, ...), custom_call_target="tpu_custom_call" | custom-call | flops 10000000 | bytes 25731072 | tf_op jit(solution)/shard_map/pallas_call | solution.py:221
  107.8 17.2 %shard_map.78 = (f32[512,512]{1,0:T(8,128)}, f32[512,512]{1,0:T(8,128)}, bf16[512,512]{1,0:T(8,128)(2,1)S(1)}, bf16[512,1536]{1,0:T(8,128)(2,1)}, bf16[16,256,25...) custom-call(s32[512,1]{1,0:T(8,128)S(1)} %bitcast.177, ...), custom_call_target="tpu_custom_call" | custom-call | flops 6587154432 | bytes 30000000 | tf_op jit(solution)/shard_map/pallas_call | solution.py:339
  125.0 8.6 %shard_map.79 = (bf16[128,512]{1,0:T(8,128)(2,1)S(1)}, bf16[512,1536]{1,0:T(8,128)(2,1)}, bf16[512,512]{1,0:T(8,128)(2,1)}, bf16[512,2048]{1,0:T(8,128)(2,1)}, b...) custom-call(s32[4]{0:T(128)S(1)} %pad_add_fusion.place_ref, ...), custom_call_target="tpu_custom_call" | custom-call | flops 10000000 | bytes 25731072 | tf_op jit(solution)/shard_map/pallas_call | solution.py:221
  133.7 17.7 %shard_map.80 = (bf16[512,512]{1,0:T(8,128)(2,1)}, f32[512,512]{1,0:T(8,128)}, bf16[512,512]{1,0:T(8,128)(2,1)S(1)}, bf16[512,1536]{1,0:T(8,128)(2,1)}, bf16[16,...) custom-call(f32[512,512]{1,0:T(8,128)} %get-tuple-element.63.refs_0_, ...), custom_call_target="tpu_custom_call" | custom-call | flops 6587154432 | bytes 30000000 | tf_op jit(solution)/shard_map/pallas_call | solution.py:339
  151.4 13.5 %shard_map.81 = (f32[512,512]{1,0:T(8,128)}, f32[4648,128]{1,0:T(8,128)}, bf16[8,800,128]{2,1,0:T(8,128)(2,1)}, bf16[8,800,128]{2,1,0:T(8,128)(2,1)}) custom-call(s32[4]{0:T(128)S(1)} %pad_add_fusion.place_ref, bf16[512,512]{1,0:T(8,128)(2,1)S(1)} %bitcast.183, f32[512,512]{1,0:T(8,128)} %get-tuple-element.72.x2, bf16[512,512]{1,0:T(8,128)(2,1)S(1)} %get-tuple-element.73.a2, ...), custom_call_target="tpu_custom_call" | custom-call | flops 8601600000 | bytes 20000000 | tf_op jit(solution)/shard_map/pallas_call | solution.py:423
  164.9 14.9 %shard_map.82 = (f32[512,512]{1,0:T(8,128)}, bf16[8,800,128]{2,1,0:T(8,128)(2,1)}, bf16[8,800,128]{2,1,0:T(8,128)(2,1)}) custom-call(s32[4]{0:T(128)S(1)} %pad_add_fusion.place_ref, f32[512,512]{1,0:T(8,128)} %get-tuple-element.76.grad, f32[512,512]{1,0:T(8,128)} %get-tuple-element.77.x, bf16[512,512]{1,0:T(8,128)(2,1)S(1)} %get-tuple-element.78.a, ...), custom_call_target="tpu_custom_call" | custom-call | flops 4505600000 | bytes 20000000 | tf_op jit(solution)/shard_map/pallas_call | solution.py:551
  179.9 13.4 %shard_map.83 = (f32[512,512]{1,0:T(8,128)S(1)}, f32[4648,128]{1,0:T(8,128)}, bf16[8,800,128]{2,1,0:T(8,128)(2,1)}, bf16[8,800,128]{2,1,0:T(8,128)(2,1)}) custom-call(s32[4]{0:T(128)S(1)} %pad_add_fusion.place_ref, f32[512,512]{1,0:T(8,128)} %get-tuple-element.83.grad, f32[512,512]{1,0:T(8,128)} %get-tuple-element.84.x2, bf16[512,512]{1,0:T(8,128)(2,1)S(1)} %copy-done.4, ...), custom_call_target="tpu_custom_call" | custom-call | flops 8601600000 | bytes 20000000 | tf_op jit(solution)/shard_map/pallas_call | solution.py:423
  194.7 15.3 %shard_map.84 = (bf16[8,800,128]{2,1,0:T(8,128)(2,1)}, bf16[8,800,128]{2,1,0:T(8,128)(2,1)}, f32[16,8,128]{2,1,0:T(8,128)S(1)}, f32[16,8,128]{2,1,0:T(8,128)S(1)}) custom-call(s32[4]{0:T(128)S(1)} %pad_add_fusion.place_ref, f32[512,512]{1,0:T(8,128)} %copy-done.3, f32[512,512]{1,0:T(8,128)} %get-tuple-element.91.x, ...), custom_call_target="tpu_custom_call" | custom-call | flops 4505600000 | bytes 20000000 | tf_op jit(solution)/shard_map/pallas_call | solution.py:551
  212.9 2.3 collective-permute-done.51
  217.2 1.6 collective-permute-done.52
  218.9 3.5 %collective-permute-start.53 = (bf16[8,128]{1,0:T(8,128)(2,1)S(1)}, bf16[8,128]{1,0:T(8,128)(2,1)S(1)}, u32[]{:S(2)}, u32[]{:S(2)}) collective-permute-start(bf16[8,128]{1,0:T(8,128)(2,1)S(1)} %get-tuple-element.115), channel_id=1, source_target_pairs={{0,8},{1,9},{2,10},{3,11},{4,12},{5,13},{6,14},{7,15},{8,0},{9,1},... | collective-permute-start | bytes 6152 | tf_op jit(solution)/shard_map/ppermute | solution.py:562
  236.4 6.1 %collective-permute-done.25 = bf16[2,2,400,128]{3,2,1,0:T(8,128)(2,1)S(1)} collective-permute-done((bf16[2,2,400,128]{3,2,1,0:T(8,128)(2,1)S(1)}, bf16[2,2,400,128]{3,2,1,0:T(8,128)(2,1)S(1)}, u32[]{:S(2)}, u32[]{:S(2)}) %collective-permute-start.25) | collective-permute-done | bytes 409632 | tf_op jit(solution)/shard_map/ppermute | solution.py:562
  244.2 1.6 collective-permute-start.32
  245.8 6.3 %collective-permute-done.30 = bf16[2,2,400,128]{3,2,1,0:T(8,128)(2,1)S(1)} collective-permute-done((bf16[2,2,400,128]{3,2,1,0:T(8,128)(2,1)S(1)}, bf16[2,2,400,128]{3,2,1,0:T(8,128)(2,1)S(1)}, u32[]{:S(2)}, u32[]{:S(2)}) %collective-permute-start.30) | collective-permute-done | bytes 409632 | tf_op jit(solution)/shard_map/ppermute | solution.py:562
  253.8 1.9 collective-permute-start.40
  255.9 6.6 %collective-permute-done.38 = bf16[2,2,400,128]{3,2,1,0:T(8,128)(2,1)S(1)} collective-permute-done((bf16[2,2,400,128]{3,2,1,0:T(8,128)(2,1)S(1)}, bf16[2,2,400,128]{3,2,1,0:T(8,128)(2,1)S(1)}, u32[]{:S(2)}, u32[]{:S(2)}) %collective-permute-start.38) | collective-permute-done | bytes 409632 | tf_op jit(solution)/shard_map/ppermute | solution.py:562
  264.3 2.6 collective-permute-start.45
  267.0 4.8 %collective-permute-done.43 = bf16[2,2,400,128]{3,2,1,0:T(8,128)(2,1)S(1)} collective-permute-done((bf16[2,2,400,128]{3,2,1,0:T(8,128)(2,1)S(1)}, bf16[2,2,400,128]{3,2,1,0:T(8,128)(2,1)S(1)}, u32[]{:S(2)}, u32[]{:S(2)}) %collective-permute-start.43) | collective-permute-done | bytes 409632 | tf_op jit(solution)/shard_map/ppermute | solution.py:562
  271.8 3.6 %collective-permute-start.26 = (bf16[2,400,128]{2,1,0:T(8,128)(2,1)S(1)}, bf16[2,400,128]{2,1,0:T(8,128)(2,1)S(1)}, u32[]{:S(2)}, u32[]{:S(2)}) collective-permute-start(bf16[2,400,128]{2,1,0:T(8,128)(2,1)S(1)} %fusion.26), channel_id=1, source_target_pairs={{0,2},{1,3},{2,0},{3,1},{4,6},{5,7},{6,4},{7,5},{8,10},{9,11},{10,... | collective-permute-start | bytes 614408 | tf_op jit(solution)/shard_map/ppermute | solution.py:562
  277.2 2.3 collective-permute-done.26
  279.5 2.3 collective-permute-start.31
  283.9 3.3 collective-permute-done.31
  287.2 2.3 collective-permute-start.39
  290.0 1.8 collective-permute-start.41
  293.2 2.0 collective-permute-start.44
  295.7 1.8 collective-permute-start.46
  299.0 2.5 collective-permute-done.46
  301.9 3.0 collective-permute-start.35
  306.6 2.4 collective-permute-start.49
  309.9 9.8 %collective-permute-done.35.refs_2_ = bf16[800,128]{1,0:T(8,128)(2,1)S(1)} collective-permute-done((bf16[800,128]{1,0:T(8,128)(2,1)S(1)}, bf16[800,128]{1,0:T(8,128)(2,1)S(1)}, u32[]{:S(2)}, u32[]{:S(2)}) %collective-permute-start.35) | collective-permute-done | bytes 204832 | tf_op jit(solution)/shard_map/ppermute | solution.py:562
  320.5 6.6 %collective-permute-done.48.refs_6_ = bf16[800,128]{1,0:T(8,128)(2,1)S(1)} collective-permute-done((bf16[800,128]{1,0:T(8,128)(2,1)S(1)}, bf16[800,128]{1,0:T(8,128)(2,1)S(1)}, u32[]{:S(2)}, u32[]{:S(2)}) %collective-permute-start.48) | collective-permute-done | bytes 204832 | tf_op jit(solution)/shard_map/ppermute | solution.py:562
  327.7 2.2 shard_map.85
  329.9 1.8 copy.70
  (185 shorter events, 58.1 us)
Async XLA Ops:
  3.0 12.6 %collective-permute-start.12 = (bf16[800,128]{1,0:T(8,128)(2,1)S(1)}, bf16[800,128]{1,0:T(8,128)(2,1)S(1)}, u32[]{:S(2)}, u32[]{:S(2)}) collective-permute-start(bf16[800,128]{1,0:T(8,128)(2,1)S(1)} %get-tuple-element.64), channel_id=1, source_target_pairs={{0,8},{1,9},{2,10},{3,11},{4,12},{5,13},{6,14},{7,15},{8,0},{9,1},... | collective-permute-start | bytes 614408 | tf_op jit(solution)/shard_map/ppermute | solution.py:562
  6.1 17.7 %collective-permute-start.13 = (bf16[800,128]{1,0:T(8,128)(2,1)S(1)}, bf16[800,128]{1,0:T(8,128)(2,1)S(1)}, u32[]{:S(2)}, u32[]{:S(2)}) collective-permute-start(bf16[800,128]{1,0:T(8,128)(2,1)S(1)} %get-tuple-element.64), channel_id=1, source_target_pairs={{0,16},{1,17},{2,18},{3,19},{4,20},{5,21},{6,22},{7,23},{8,24},{9,... | collective-permute-start | bytes 614408 | tf_op jit(solution)/shard_map/ppermute | solution.py:562
  8.7 15.8 %collective-permute-start.14 = (bf16[800,128]{1,0:T(8,128)(2,1)S(1)}, bf16[800,128]{1,0:T(8,128)(2,1)S(1)}, u32[]{:S(2)}, u32[]{:S(2)}) collective-permute-start(bf16[800,128]{1,0:T(8,128)(2,1)S(1)} %get-tuple-element.64), channel_id=1, source_target_pairs={{0,24},{1,25},{2,26},{3,27},{4,28},{5,29},{6,30},{7,31},{8,16},{9,... | collective-permute-start | bytes 614408 | tf_op jit(solution)/shard_map/ppermute | solution.py:562
  8.7 18.0 %collective-permute-start = (bf16[800,128]{1,0:T(8,128)(2,1)S(1)}, bf16[800,128]{1,0:T(8,128)(2,1)S(1)}, u32[]{:S(2)}, u32[]{:S(2)}) collective-permute-start(bf16[800,128]{1,0:T(8,128)(2,1)S(1)} %get-tuple-element.55), channel_id=1, source_target_pairs={{0,8},{1,9},{2,10},{3,11},{4,12},{5,13},{6,14},{7,15},{8,0},{9,1},... | collective-permute-start | bytes 614408 | tf_op jit(solution)/shard_map/ppermute | solution.py:562
  9.6 31.8 %collective-permute-start.1 = (bf16[800,128]{1,0:T(8,128)(2,1)S(1)}, bf16[800,128]{1,0:T(8,128)(2,1)S(1)}, u32[]{:S(2)}, u32[]{:S(2)}) collective-permute-start(bf16[800,128]{1,0:T(8,128)(2,1)S(1)} %get-tuple-element.55), channel_id=1, source_target_pairs={{0,16},{1,17},{2,18},{3,19},{4,20},{5,21},{6,22},{7,23},{8,24},{9,... | collective-permute-start | bytes 614408 | tf_op jit(solution)/shard_map/ppermute | solution.py:562
  15.6 25.8 %collective-permute-start.2 = (bf16[800,128]{1,0:T(8,128)(2,1)S(1)}, bf16[800,128]{1,0:T(8,128)(2,1)S(1)}, u32[]{:S(2)}, u32[]{:S(2)}) collective-permute-start(bf16[800,128]{1,0:T(8,128)(2,1)S(1)} %get-tuple-element.55), channel_id=1, source_target_pairs={{0,24},{1,25},{2,26},{3,27},{4,28},{5,29},{6,30},{7,31},{8,16},{9,... | collective-permute-start | bytes 614408 | tf_op jit(solution)/shard_map/ppermute | solution.py:562
  25.2 19.9 %collective-permute-start.16 = (bf16[3200,128]{1,0:T(8,128)(2,1)}, bf16[3200,128]{1,0:T(8,128)(2,1)}, u32[]{:S(2)}, u32[]{:S(2)}) collective-permute-start(bf16[3200,128]{1,0:T(8,128)(2,1)} %constant_dynamic-update-slice_fusion.4.refs_0_), channel_id=1, source_target_pairs={{0,4},{1,5},{2,6},{3,7},{4,0},{5,1},{6,2},{7,3},{8,12},{9,13},{10,... | collective-permute-start | bytes 2457608 | tf_op jit(solution)/shard_map/ppermute | solution.py:562
  41.4 21.4 %collective-permute-start.6 = (bf16[3200,128]{1,0:T(8,128)(2,1)S(1)}, bf16[3200,128]{1,0:T(8,128)(2,1)}, u32[]{:S(2)}, u32[]{:S(2)}) collective-permute-start(bf16[3200,128]{1,0:T(8,128)(2,1)S(1)} %constant_dynamic-update-slice_fusion.refs_0_), channel_id=1, source_target_pairs={{0,2},{1,3},{2,0},{3,1},{4,6},{5,7},{6,4},{7,5},{8,10},{9,11},{10,... | collective-permute-start | bytes 2457608 | tf_op jit(solution)/shard_map/ppermute | solution.py:562
  43.0 22.4 %collective-permute-start.4 = (bf16[3200,128]{1,0:T(8,128)(2,1)S(1)}, bf16[3200,128]{1,0:T(8,128)(2,1)}, u32[]{:S(2)}, u32[]{:S(2)}) collective-permute-start(bf16[3200,128]{1,0:T(8,128)(2,1)S(1)} %constant_dynamic-update-slice_fusion.refs_0_), channel_id=1, source_target_pairs={{0,4},{1,5},{2,6},{3,7},{4,0},{5,1},{6,2},{7,3},{8,12},{9,13},{10,... | collective-permute-start | bytes 2457608 | tf_op jit(solution)/shard_map/ppermute | solution.py:562
  44.5 35.8 %collective-permute-start.18 = (bf16[3200,128]{1,0:T(8,128)(2,1)}, bf16[3200,128]{1,0:T(8,128)(2,1)}, u32[]{:S(2)}, u32[]{:S(2)}) collective-permute-start(bf16[3200,128]{1,0:T(8,128)(2,1)} %constant_dynamic-update-slice_fusion.4.refs_0_), channel_id=1, source_target_pairs={{0,2},{1,3},{2,0},{3,1},{4,6},{5,7},{6,4},{7,5},{8,10},{9,11},{10,... | collective-permute-start | bytes 2457608 | tf_op jit(solution)/shard_map/ppermute | solution.py:562
  45.0 35.3 %collective-permute-start.3 = (bf16[3200,128]{1,0:T(8,128)(2,1)S(1)}, bf16[3200,128]{1,0:T(8,128)(2,1)S(1)}, u32[]{:S(2)}, u32[]{:S(2)}) collective-permute-start(bf16[3200,128]{1,0:T(8,128)(2,1)S(1)} %constant_dynamic-update-slice_fusion.refs_0_), channel_id=1, source_target_pairs={{0,1},{1,0},{2,3},{3,2},{4,5},{5,4},{6,7},{7,6},{8,9},{9,8},{10,11... | collective-permute-start | bytes 2457608 | tf_op jit(solution)/shard_map/ppermute | solution.py:562
  46.1 42.9 %collective-permute-start.20 = (bf16[1600,128]{1,0:T(8,128)(2,1)S(1)}, bf16[1600,128]{1,0:T(8,128)(2,1)S(1)}, u32[]{:S(2)}, u32[]{:S(2)}) collective-permute-start(bf16[1600,128]{1,0:T(8,128)(2,1)S(1)} %bitcast.198), channel_id=1, source_target_pairs={{0,2},{1,3},{2,0},{3,1},{4,6},{5,7},{6,4},{7,5},{8,10},{9,11},{10,... | collective-permute-start | bytes 1228808 | tf_op jit(solution)/shard_map/ppermute | solution.py:562
  63.8 26.7 %collective-permute-start.10 = (bf16[1600,128]{1,0:T(8,128)(2,1)S(1)}, bf16[1600,128]{1,0:T(8,128)(2,1)S(1)}, u32[]{:S(2)}, u32[]{:S(2)}) collective-permute-start(bf16[1600,128]{1,0:T(8,128)(2,1)S(1)} %bitcast.199), channel_id=1, source_target_pairs={{0,4},{1,5},{2,6},{3,7},{4,0},{5,1},{6,2},{7,3},{8,12},{9,13},{10,... | collective-permute-start | bytes 1228808 | tf_op jit(solution)/shard_map/ppermute | solution.py:562
  66.4 27.6 %collective-permute-start.8 = (bf16[1600,128]{1,0:T(8,128)(2,1)S(1)}, bf16[1600,128]{1,0:T(8,128)(2,1)S(1)}, u32[]{:S(2)}, u32[]{:S(2)}) collective-permute-start(bf16[1600,128]{1,0:T(8,128)(2,1)S(1)} %bitcast.200), channel_id=1, source_target_pairs={{0,2},{1,3},{2,0},{3,1},{4,6},{5,7},{6,4},{7,5},{8,10},{9,11},{10,... | collective-permute-start | bytes 1228808 | tf_op jit(solution)/shard_map/ppermute | solution.py:562
  80.3 17.7 %collective-permute-start.5 = (bf16[3200,128]{1,0:T(8,128)(2,1)}, bf16[3200,128]{1,0:T(8,128)(2,1)}, u32[]{:S(2)}, u32[]{:S(2)}) collective-permute-start(bf16[3200,128]{1,0:T(8,128)(2,1)} %collective-permute-done.4.refs_2_), channel_id=1, source_target_pairs={{0,1},{1,0},{2,3},{3,2},{4,5},{5,4},{6,7},{7,6},{8,9},{9,8},{10,11... | collective-permute-start | bytes 2457608 | tf_op jit(solution)/shard_map/ppermute | solution.py:562
  80.3 18.2 %collective-permute-start.7 = (bf16[3200,128]{1,0:T(8,128)(2,1)}, bf16[3200,128]{1,0:T(8,128)(2,1)}, u32[]{:S(2)}, u32[]{:S(2)}) collective-permute-start(bf16[3200,128]{1,0:T(8,128)(2,1)} %collective-permute-done.6.refs_4_), channel_id=1, source_target_pairs={{0,1},{1,0},{2,3},{3,2},{4,5},{5,4},{6,7},{7,6},{8,9},{9,8},{10,11... | collective-permute-start | bytes 2457608 | tf_op jit(solution)/shard_map/ppermute | solution.py:562
  89.0 8.0 %collective-permute-start.22 = (bf16[1600,128]{1,0:T(8,128)(2,1)S(1)}, bf16[1600,128]{1,0:T(8,128)(2,1)S(1)}, u32[]{:S(2)}, u32[]{:S(2)}) collective-permute-start(bf16[1600,128]{1,0:T(8,128)(2,1)S(1)} %bitcast.201), channel_id=1, source_target_pairs={{0,4},{1,5},{2,6},{3,7},{4,0},{5,1},{6,2},{7,3},{8,12},{9,13},{10,... | collective-permute-start | bytes 1228808 | tf_op jit(solution)/shard_map/ppermute | solution.py:562
  90.5 6.5 %collective-permute-start.11 = (bf16[1600,128]{1,0:T(8,128)(2,1)S(1)}, bf16[1600,128]{1,0:T(8,128)(2,1)S(1)}, u32[]{:S(2)}, u32[]{:S(2)}) collective-permute-start(bf16[1600,128]{1,0:T(8,128)(2,1)S(1)} %collective-permute-done.10.refs_8_), channel_id=1, source_target_pairs={{0,1},{1,0},{2,3},{3,2},{4,5},{5,4},{6,7},{7,6},{8,9},{9,8},{10,11... | collective-permute-start | bytes 1228808 | tf_op jit(solution)/shard_map/ppermute | solution.py:562
  97.0 28.0 %collective-permute-start.15 = (bf16[3200,128]{1,0:T(8,128)(2,1)}, bf16[3200,128]{1,0:T(8,128)(2,1)}, u32[]{:S(2)}, u32[]{:S(2)}) collective-permute-start(bf16[3200,128]{1,0:T(8,128)(2,1)} %constant_dynamic-update-slice_fusion.4.refs_0_), channel_id=1, source_target_pairs={{0,1},{1,0},{2,3},{3,2},{4,5},{5,4},{6,7},{7,6},{8,9},{9,8},{10,11... | collective-permute-start | bytes 2457608 | tf_op jit(solution)/shard_map/ppermute | solution.py:562
  97.0 28.1 %collective-permute-start.17 = (bf16[3200,128]{1,0:T(8,128)(2,1)}, bf16[3200,128]{1,0:T(8,128)(2,1)}, u32[]{:S(2)}, u32[]{:S(2)}) collective-permute-start(bf16[3200,128]{1,0:T(8,128)(2,1)} %collective-permute-done.16.refs_2_), channel_id=1, source_target_pairs={{0,1},{1,0},{2,3},{3,2},{4,5},{5,4},{6,7},{7,6},{8,9},{9,8},{10,11... | collective-permute-start | bytes 2457608 | tf_op jit(solution)/shard_map/ppermute | solution.py:562
  97.5 27.6 %collective-permute-start.19 = (bf16[3200,128]{1,0:T(8,128)(2,1)}, bf16[3200,128]{1,0:T(8,128)(2,1)}, u32[]{:S(2)}, u32[]{:S(2)}) collective-permute-start(bf16[3200,128]{1,0:T(8,128)(2,1)} %collective-permute-done.18.refs_4_), channel_id=1, source_target_pairs={{0,1},{1,0},{2,3},{3,2},{4,5},{5,4},{6,7},{7,6},{8,9},{9,8},{10,11... | collective-permute-start | bytes 2457608 | tf_op jit(solution)/shard_map/ppermute | solution.py:562
  98.1 26.9 %collective-permute-start.21 = (bf16[1600,128]{1,0:T(8,128)(2,1)S(1)}, bf16[1600,128]{1,0:T(8,128)(2,1)S(1)}, u32[]{:S(2)}, u32[]{:S(2)}) collective-permute-start(bf16[1600,128]{1,0:T(8,128)(2,1)S(1)} %collective-permute-done.20.refs_6_), channel_id=1, source_target_pairs={{0,1},{1,0},{2,3},{3,2},{4,5},{5,4},{6,7},{7,6},{8,9},{9,8},{10,11... | collective-permute-start | bytes 1228808 | tf_op jit(solution)/shard_map/ppermute | solution.py:562
  98.6 26.4 %collective-permute-start.23 = (bf16[1600,128]{1,0:T(8,128)(2,1)S(1)}, bf16[1600,128]{1,0:T(8,128)(2,1)S(1)}, u32[]{:S(2)}, u32[]{:S(2)}) collective-permute-start(bf16[1600,128]{1,0:T(8,128)(2,1)S(1)} %collective-permute-done.22.refs_8_), channel_id=1, source_target_pairs={{0,1},{1,0},{2,3},{3,2},{4,5},{5,4},{6,7},{7,6},{8,9},{9,8},{10,11... | collective-permute-start | bytes 1228808 | tf_op jit(solution)/shard_map/ppermute | solution.py:562
  194.2 28.2 %collective-permute-start.24 = (bf16[8,800,128]{2,1,0:T(8,128)(2,1)}, bf16[8,800,128]{2,1,0:T(8,128)(2,1)}, u32[]{:S(2)}, u32[]{:S(2)}) collective-permute-start(bf16[8,800,128]{2,1,0:T(8,128)(2,1)} %get-tuple-element.89), channel_id=1, source_target_pairs={{0,1},{1,0},{2,3},{3,2},{4,5},{5,4},{6,7},{7,6},{8,9},{9,8},{10,11... | collective-permute-start | bytes 4915208 | tf_op jit(solution)/shard_map/ppermute | solution.py:562
  212.9 13.5 %collective-permute-start.29 = (bf16[8,800,128]{2,1,0:T(8,128)(2,1)}, bf16[8,800,128]{2,1,0:T(8,128)(2,1)}, u32[]{:S(2)}, u32[]{:S(2)}) collective-permute-start(bf16[8,800,128]{2,1,0:T(8,128)(2,1)} %get-tuple-element.98), channel_id=1, source_target_pairs={{0,1},{1,0},{2,3},{3,2},{4,5},{5,4},{6,7},{7,6},{8,9},{9,8},{10,11... | collective-permute-start | bytes 4915208 | tf_op jit(solution)/shard_map/ppermute | solution.py:562
  216.7 13.8 %collective-permute-start.37 = (bf16[8,800,128]{2,1,0:T(8,128)(2,1)}, bf16[8,800,128]{2,1,0:T(8,128)(2,1)S(1)}, u32[]{:S(2)}, u32[]{:S(2)}) collective-permute-start(bf16[8,800,128]{2,1,0:T(8,128)(2,1)} %get-tuple-element.100), channel_id=1, source_target_pairs={{0,1},{1,0},{2,3},{3,2},{4,5},{5,4},{6,7},{7,6},{8,9},{9,8},{10,11... | collective-permute-start | bytes 4915208 | tf_op jit(solution)/shard_map/ppermute | solution.py:562
  216.7 14.5 %collective-permute-start.42 = (bf16[8,800,128]{2,1,0:T(8,128)(2,1)}, bf16[8,800,128]{2,1,0:T(8,128)(2,1)S(1)}, u32[]{:S(2)}, u32[]{:S(2)}) collective-permute-start(bf16[8,800,128]{2,1,0:T(8,128)(2,1)} %get-tuple-element.102), channel_id=1, source_target_pairs={{0,1},{1,0},{2,3},{3,2},{4,5},{5,4},{6,7},{7,6},{8,9},{9,8},{10,11... | collective-permute-start | bytes 4915208 | tf_op jit(solution)/shard_map/ppermute | solution.py:562
  218.9 87.5 %collective-permute-start.53 = (bf16[8,128]{1,0:T(8,128)(2,1)S(1)}, bf16[8,128]{1,0:T(8,128)(2,1)S(1)}, u32[]{:S(2)}, u32[]{:S(2)}) collective-permute-start(bf16[8,128]{1,0:T(8,128)(2,1)S(1)} %get-tuple-element.115), channel_id=1, source_target_pairs={{0,8},{1,9},{2,10},{3,11},{4,12},{5,13},{6,14},{7,15},{8,0},{9,1},... | collective-permute-start | bytes 6152 | tf_op jit(solution)/shard_map/ppermute | solution.py:562
  222.4 84.2 %collective-permute-start.54 = (bf16[8,128]{1,0:T(8,128)(2,1)S(1)}, bf16[8,128]{1,0:T(8,128)(2,1)S(1)}, u32[]{:S(2)}, u32[]{:S(2)}) collective-permute-start(bf16[8,128]{1,0:T(8,128)(2,1)S(1)} %get-tuple-element.114), channel_id=1, source_target_pairs={{0,16},{1,17},{2,18},{3,19},{4,20},{5,21},{6,22},{7,23},{8,24},{9,... | collective-permute-start | bytes 6152 | tf_op jit(solution)/shard_map/ppermute | solution.py:562
  226.3 82.7 %collective-permute-start.55 = (bf16[8,128]{1,0:T(8,128)(2,1)S(1)}, bf16[8,128]{1,0:T(8,128)(2,1)S(1)}, u32[]{:S(2)}, u32[]{:S(2)}) collective-permute-start(bf16[8,128]{1,0:T(8,128)(2,1)S(1)} %get-tuple-element.113), channel_id=1, source_target_pairs={{0,24},{1,25},{2,26},{3,27},{4,28},{5,29},{6,30},{7,31},{8,16},{9,... | collective-permute-start | bytes 6152 | tf_op jit(solution)/shard_map/ppermute | solution.py:562
  232.8 9.7 %collective-permute-start.25 = (bf16[2,2,400,128]{3,2,1,0:T(8,128)(2,1)S(1)}, bf16[2,2,400,128]{3,2,1,0:T(8,128)(2,1)S(1)}, u32[]{:S(2)}, u32[]{:S(2)}) collective-permute-start(bf16[2,2,400,128]{3,2,1,0:T(8,128)(2,1)S(1)} %fusion.10), channel_id=1, source_target_pairs={{0,4},{1,5},{2,6},{3,7},{4,0},{5,1},{6,2},{7,3},{8,12},{9,13},{10,... | collective-permute-start | bytes 1228808 | tf_op jit(solution)/shard_map/ppermute | solution.py:562
  234.5 9.7 %collective-permute-start.27 = (bf16[2,2,400,128]{3,2,1,0:T(8,128)(2,1)S(1)}, bf16[2,2,400,128]{3,2,1,0:T(8,128)(2,1)S(1)}, u32[]{:S(2)}, u32[]{:S(2)}) collective-permute-start(bf16[2,2,400,128]{3,2,1,0:T(8,128)(2,1)S(1)} %fusion.11), channel_id=1, source_target_pairs={{0,2},{1,3},{2,0},{3,1},{4,6},{5,7},{6,4},{7,5},{8,10},{9,11},{10,... | collective-permute-start | bytes 1228808 | tf_op jit(solution)/shard_map/ppermute | solution.py:562
  242.5 9.6 %collective-permute-start.30 = (bf16[2,2,400,128]{3,2,1,0:T(8,128)(2,1)S(1)}, bf16[2,2,400,128]{3,2,1,0:T(8,128)(2,1)S(1)}, u32[]{:S(2)}, u32[]{:S(2)}) collective-permute-start(bf16[2,2,400,128]{3,2,1,0:T(8,128)(2,1)S(1)} %fusion.12), channel_id=1, source_target_pairs={{0,4},{1,5},{2,6},{3,7},{4,0},{5,1},{6,2},{7,3},{8,12},{9,13},{10,... | collective-permute-start | bytes 1228808 | tf_op jit(solution)/shard_map/ppermute | solution.py:562
  244.2 9.7 %collective-permute-start.32 = (bf16[2,2,400,128]{3,2,1,0:T(8,128)(2,1)S(1)}, bf16[2,2,400,128]{3,2,1,0:T(8,128)(2,1)S(1)}, u32[]{:S(2)}, u32[]{:S(2)}) collective-permute-start(bf16[2,2,400,128]{3,2,1,0:T(8,128)(2,1)S(1)} %fusion.13), channel_id=1, source_target_pairs={{0,2},{1,3},{2,0},{3,1},{4,6},{5,7},{6,4},{7,5},{8,10},{9,11},{10,... | collective-permute-start | bytes 1228808 | tf_op jit(solution)/shard_map/ppermute | solution.py:562
  252.2 10.3 %collective-permute-start.38 = (bf16[2,2,400,128]{3,2,1,0:T(8,128)(2,1)S(1)}, bf16[2,2,400,128]{3,2,1,0:T(8,128)(2,1)S(1)}, u32[]{:S(2)}, u32[]{:S(2)}) collective-permute-start(bf16[2,2,400,128]{3,2,1,0:T(8,128)(2,1)S(1)} %fusion.14), channel_id=1, source_target_pairs={{0,4},{1,5},{2,6},{3,7},{4,0},{5,1},{6,2},{7,3},{8,12},{9,13},{10,... | collective-permute-start | bytes 1228808 | tf_op jit(solution)/shard_map/ppermute | solution.py:562
  253.8 10.5 %collective-permute-start.40 = (bf16[2,2,400,128]{3,2,1,0:T(8,128)(2,1)S(1)}, bf16[2,2,400,128]{3,2,1,0:T(8,128)(2,1)S(1)}, u32[]{:S(2)}, u32[]{:S(2)}) collective-permute-start(bf16[2,2,400,128]{3,2,1,0:T(8,128)(2,1)S(1)} %fusion.15), channel_id=1, source_target_pairs={{0,2},{1,3},{2,0},{3,1},{4,6},{5,7},{6,4},{7,5},{8,10},{9,11},{10,... | collective-permute-start | bytes 1228808 | tf_op jit(solution)/shard_map/ppermute | solution.py:562
  262.5 9.3 %collective-permute-start.43 = (bf16[2,2,400,128]{3,2,1,0:T(8,128)(2,1)S(1)}, bf16[2,2,400,128]{3,2,1,0:T(8,128)(2,1)S(1)}, u32[]{:S(2)}, u32[]{:S(2)}) collective-permute-start(bf16[2,2,400,128]{3,2,1,0:T(8,128)(2,1)S(1)} %fusion.16), channel_id=1, source_target_pairs={{0,4},{1,5},{2,6},{3,7},{4,0},{5,1},{6,2},{7,3},{8,12},{9,13},{10,... | collective-permute-start | bytes 1228808 | tf_op jit(solution)/shard_map/ppermute | solution.py:562
  264.3 11.1 %collective-permute-start.45 = (bf16[2,2,400,128]{3,2,1,0:T(8,128)(2,1)S(1)}, bf16[2,2,400,128]{3,2,1,0:T(8,128)(2,1)S(1)}, u32[]{:S(2)}, u32[]{:S(2)}) collective-permute-start(bf16[2,2,400,128]{3,2,1,0:T(8,128)(2,1)S(1)} %fusion.17), channel_id=1, source_target_pairs={{0,2},{1,3},{2,0},{3,1},{4,6},{5,7},{6,4},{7,5},{8,10},{9,11},{10,... | collective-permute-start | bytes 1228808 | tf_op jit(solution)/shard_map/ppermute | solution.py:562
  271.8 7.7 %collective-permute-start.26 = (bf16[2,400,128]{2,1,0:T(8,128)(2,1)S(1)}, bf16[2,400,128]{2,1,0:T(8,128)(2,1)S(1)}, u32[]{:S(2)}, u32[]{:S(2)}) collective-permute-start(bf16[2,400,128]{2,1,0:T(8,128)(2,1)S(1)} %fusion.26), channel_id=1, source_target_pairs={{0,2},{1,3},{2,0},{3,1},{4,6},{5,7},{6,4},{7,5},{8,10},{9,11},{10,... | collective-permute-start | bytes 614408 | tf_op jit(solution)/shard_map/ppermute | solution.py:562
  275.5 6.9 %collective-permute-start.28 = (bf16[2,400,128]{2,1,0:T(8,128)(2,1)S(1)}, bf16[2,400,128]{2,1,0:T(8,128)(2,1)S(1)}, u32[]{:S(2)}, u32[]{:S(2)}) collective-permute-start(bf16[2,400,128]{2,1,0:T(8,128)(2,1)S(1)} %fusion.27), channel_id=1, source_target_pairs={{0,4},{1,5},{2,6},{3,7},{4,0},{5,1},{6,2},{7,3},{8,12},{9,13},{10,... | collective-permute-start | bytes 614408 | tf_op jit(solution)/shard_map/ppermute | solution.py:562
  279.5 7.7 %collective-permute-start.31 = (bf16[2,400,128]{2,1,0:T(8,128)(2,1)S(1)}, bf16[2,400,128]{2,1,0:T(8,128)(2,1)S(1)}, u32[]{:S(2)}, u32[]{:S(2)}) collective-permute-start(bf16[2,400,128]{2,1,0:T(8,128)(2,1)S(1)} %fusion.28), channel_id=1, source_target_pairs={{0,2},{1,3},{2,0},{3,1},{4,6},{5,7},{6,4},{7,5},{8,10},{9,11},{10,... | collective-permute-start | bytes 614408 | tf_op jit(solution)/shard_map/ppermute | solution.py:562
  282.3 7.6 %collective-permute-start.33 = (bf16[2,400,128]{2,1,0:T(8,128)(2,1)S(1)}, bf16[2,400,128]{2,1,0:T(8,128)(2,1)S(1)}, u32[]{:S(2)}, u32[]{:S(2)}) collective-permute-start(bf16[2,400,128]{2,1,0:T(8,128)(2,1)S(1)} %fusion.29), channel_id=1, source_target_pairs={{0,4},{1,5},{2,6},{3,7},{4,0},{5,1},{6,2},{7,3},{8,12},{9,13},{10,... | collective-permute-start | bytes 614408 | tf_op jit(solution)/shard_map/ppermute | solution.py:562
  301.9 17.8 %collective-permute-start.35 = (bf16[800,128]{1,0:T(8,128)(2,1)S(1)}, bf16[800,128]{1,0:T(8,128)(2,1)S(1)}, u32[]{:S(2)}, u32[]{:S(2)}) collective-permute-start(bf16[800,128]{1,0:T(8,128)(2,1)S(1)} %get-tuple-element.112), channel_id=1, source_target_pairs={{0,16},{1,17},{2,18},{3,19},{4,20},{5,21},{6,22},{7,23},{8,24},{9,... | collective-permute-start | bytes 614408 | tf_op jit(solution)/shard_map/ppermute | solution.py:562
  304.9 15.6 %collective-permute-start.36 = (bf16[800,128]{1,0:T(8,128)(2,1)S(1)}, bf16[800,128]{1,0:T(8,128)(2,1)S(1)}, u32[]{:S(2)}, u32[]{:S(2)}) collective-permute-start(bf16[800,128]{1,0:T(8,128)(2,1)S(1)} %get-tuple-element.111), channel_id=1, source_target_pairs={{0,24},{1,25},{2,26},{3,27},{4,28},{5,29},{6,30},{7,31},{8,16},{9,... | collective-permute-start | bytes 614408 | tf_op jit(solution)/shard_map/ppermute | solution.py:562
  306.4 20.8 %collective-permute-start.48 = (bf16[800,128]{1,0:T(8,128)(2,1)S(1)}, bf16[800,128]{1,0:T(8,128)(2,1)S(1)}, u32[]{:S(2)}, u32[]{:S(2)}) collective-permute-start(bf16[800,128]{1,0:T(8,128)(2,1)S(1)} %get-tuple-element.110), channel_id=1, source_target_pairs={{0,16},{1,17},{2,18},{3,19},{4,20},{5,21},{6,22},{7,23},{8,24},{9,... | collective-permute-start | bytes 614408 | tf_op jit(solution)/shard_map/ppermute | solution.py:562
  306.6 20.6 %collective-permute-start.49 = (bf16[800,128]{1,0:T(8,128)(2,1)S(1)}, bf16[800,128]{1,0:T(8,128)(2,1)S(1)}, u32[]{:S(2)}, u32[]{:S(2)}) collective-permute-start(bf16[800,128]{1,0:T(8,128)(2,1)S(1)} %get-tuple-element.109), channel_id=1, source_target_pairs={{0,24},{1,25},{2,26},{3,27},{4,28},{5,29},{6,30},{7,31},{8,16},{9,... | collective-permute-start | bytes 614408 | tf_op jit(solution)/shard_map/ppermute | solution.py:562
  309.0 18.2 %collective-permute-start.34 = (bf16[800,128]{1,0:T(8,128)(2,1)S(1)}, bf16[800,128]{1,0:T(8,128)(2,1)S(1)}, u32[]{:S(2)}, u32[]{:S(2)}) collective-permute-start(bf16[800,128]{1,0:T(8,128)(2,1)S(1)} %fusion.30), channel_id=1, source_target_pairs={{0,8},{1,9},{2,10},{3,11},{4,12},{5,13},{6,14},{7,15},{8,0},{9,1},... | collective-permute-start | bytes 614408 | tf_op jit(solution)/shard_map/ppermute | solution.py:562
  319.7 8.0 %collective-permute-start.47 = (bf16[800,128]{1,0:T(8,128)(2,1)S(1)}, bf16[800,128]{1,0:T(8,128)(2,1)S(1)}, u32[]{:S(2)}, u32[]{:S(2)}) collective-permute-start(bf16[800,128]{1,0:T(8,128)(2,1)S(1)} %fusion.35), channel_id=1, source_target_pairs={{0,8},{1,9},{2,10},{3,11},{4,12},{5,13},{6,14},{7,15},{8,0},{9,1},... | collective-permute-start | bytes 614408 | tf_op jit(solution)/shard_map/ppermute | solution.py:562
  (22 other events, 293.5 us)

commit v2 on v1

--- a/solution.py
+++ b/solution.py
@@ -37,7 +37,7 @@
         self.param_rows = max(self.count(d, shard) for d in range(devices))
         self.embed_rows = max(self.count(d, embed_shard) for d in range(devices))
         self.embed_at = ceil_to(self.param_rows, 8)
-        self.rows = ceil_to(self.embed_at + 8, 16)
+        self.rows = ceil_to(max(self.embed_at + 8, self.param_rows + 2 * self.embed_rows), 16)
 
     @staticmethod
     def first(d, size):
@@ -48,7 +48,8 @@
         return -(-(d + 1) * size // LANES) - d * size // LANES
 
 
-def params(flops, nbytes):
+def params(flops, nbytes, weight=0):
+    flops, nbytes = max(flops * weight, 1000), max(nbytes * weight, 1000)
     return dict(
         compiler_params=pltpu.CompilerParams(vmem_limit_bytes=VMEM_BYTES),
         cost_estimate=pl.CostEstimate(flops=flops, bytes_accessed=nbytes, transcendentals=0),
@@ -110,25 +111,28 @@
     )(place, layers.reshape(2, geo.rows, LANES), table.reshape(8, LANES))
 
 
-def finish_kernel(geo, place_ref, *refs):
-    n_param, n_embed = 4, 4
-    firsts, seconds, tables = refs[:n_param], refs[n_param : 2 * n_param], refs[2 * n_param : 2 * n_param + n_embed]
+def finish_kernel(geo, fast, place_ref, *refs):
     grads_ref, embed_ref = refs[-2:]
-    for layer, parts in ((0, firsts), (1, seconds)):
-        total = parts[0][...].astype(F32)
-        for part in parts[1:]:
+    parts = refs[:-2]
+    count = 4 if fast else 1
+    for layer in range(2):
+        total = parts[layer * count][...].astype(F32)
+        for part in parts[layer * count + 1 : (layer + 1) * count]:
             total = total + part[...].astype(F32)
         grads_ref[layer] = shift_out(total, place_ref[1])
-    total = tables[0][...].astype(F32)
-    for part in tables[1:]:
-        total = total + part[...].astype(F32)
-    embed_ref[...] = shift_out(total, place_ref[2])
-
-
-def finish(geo, place, firsts, seconds, tables):
-    operands = list(firsts) + list(seconds) + list(tables)
+        if fast and layer == 0:
+            first, size = geo.param_rows, geo.embed_rows
+            lower, upper = total[first : first + size], total[first + size : first + 2 * size]
+            tail = jnp.where(place_ref[3] >= 2, upper, lower)
+            tail = jnp.concatenate([tail, jnp.zeros((8 - size, LANES), F32)], 0)
+    if not fast:
+        tail = parts[2][...]
+    embed_ref[...] = shift_out(tail, place_ref[2])
+
+
+def finish(geo, fast, place, operands):
     grads, table = pl.pallas_call(
-        functools.partial(finish_kernel, geo),
+        functools.partial(finish_kernel, geo, fast),
         out_shape=(
             jax.ShapeDtypeStruct((2, geo.rows, LANES), F32),
             jax.ShapeDtypeStruct((8, LANES), F32),
@@ -229,7 +233,7 @@
             pltpu.VMEM((4 * 32, LANES), F32),
             pltpu.SemaphoreType.DMA((sum(len(pieces) for pieces in plan),)),
         ],
-        **params(10**7, 4 * 6432768),
+        **params(10**7, 4 * 6432768, 1),
     )(place, *arrays)
 
 
@@ -266,15 +270,15 @@
     return one, two
 
 
-def forward_kernel(layer, seqs, *refs):
+def ahead_attn_kernel(layer, seqs, *refs):
     if layer == 0:
         chars, table = refs[:2]
         refs = refs[2:]
     else:
         stream_in = refs[0]
         refs = refs[1:]
-    emb, w_time, w_qkv, w_out, w_up, w_down, vectors = refs[:7]
-    stream_out, x_out, a_out, qkv_out, prob_out, o_out, x2_out, a2_out, gl_out, slope_out = refs[7:]
+    emb, w_time, w_qkv, w_out, vectors = refs[:5]
+    x_out, a_out, qkv_out, prob_out, o_out, x2_out, a2_out = refs[5:]
     tokens = x_out.shape[0]
     length = tokens // seqs
     time_vec = nn(emb[...], w_time[...]) + vectors[2:3, :D]
@@ -310,21 +314,11 @@
     x2_out[...] = x_out[...] + nn(o_out[...], w_out[...])
     unit, _ = norm_stats(x2_out[...])
     a2_out[...] = (unit * vectors[3:4, :D] + vectors[4:5, :D]).astype(BF16)
-    total = x2_out[...] + vectors[5:6, :D]
-    for c in range(4):
-        part = slice(c * D, (c + 1) * D)
-        u = nn(a2_out[...], w_up[:, part]) + vectors[6:7, part]
-        gl, slope = gelu_both(u)
-        gl_out[:, part] = gl.astype(BF16)
-        slope_out[:, part] = slope.astype(BF16)
-        total = total + nn(gl_out[:, part], w_down[part, :])
-    stream_out[...] = total.astype(stream_out.dtype)
-
-
-def forward(layer, seqs, tokens, first_inputs, emb, weights, out_dtype):
+
+
+def ahead_attn(layer, seqs, tokens, first_inputs, emb, weights):
     length = tokens // seqs
     shapes = (
-        jax.ShapeDtypeStruct((tokens, D), out_dtype),
         jax.ShapeDtypeStruct((tokens, D), F32),
         jax.ShapeDtypeStruct((tokens, D), BF16),
         jax.ShapeDtypeStruct((tokens, 3 * D), BF16),
@@ -332,22 +326,55 @@
         jax.ShapeDtypeStruct((tokens, D), BF16),
         jax.ShapeDtypeStruct((tokens, D), F32),
         jax.ShapeDtypeStruct((tokens, D), BF16),
+    )
+    operands = list(first_inputs) + [emb] + list(weights)
+    return pl.pallas_call(
+        functools.partial(ahead_attn_kernel, layer, seqs),
+        out_shape=shapes,
+        in_specs=[VM] * len(operands),
+        out_specs=(VM,) * len(shapes),
+        **params(2 * tokens * 1100000 * 2, 10**7, 1),
+    )(*operands)
+
+
+def ahead_mlp_kernel(x2, a2, w_up, w_down, vectors, stream_out, gl_out, slope_out):
+    total = x2[...] + vectors[5:6, :D]
+    for c in range(4):
+        part = slice(c * D, (c + 1) * D)
+        u = nn(a2[...], w_up[:, part]) + vectors[6:7, part]
+        gl, slope = gelu_both(u)
+        gl_out[:, part] = gl.astype(BF16)
+        slope_out[:, part] = slope.astype(BF16)
+        total = total + nn(gl_out[:, part], w_down[part, :])
+    stream_out[...] = total.astype(stream_out.dtype)
+
+
+def ahead_mlp(x2, a2, w_up, w_down, vectors, out_dtype):
+    tokens = x2.shape[0]
+    shapes = (
+        jax.ShapeDtypeStruct((tokens, D), out_dtype),
         jax.ShapeDtypeStruct((tokens, FF), BF16),
         jax.ShapeDtypeStruct((tokens, FF), BF16),
     )
-    operands = list(first_inputs) + [emb] + list(weights)
     return pl.pallas_call(
-        functools.partial(forward_kernel, layer, seqs),
+        ahead_mlp_kernel,
         out_shape=shapes,
-        in_specs=[VM] * len(operands),
-        out_specs=(VM,) * len(shapes),
-        **params(2 * tokens * 3216384 * 2, 3 * 10**7),
-    )(*operands)
-
-
-def place_chunks(geo, owners, flat, base, me, outs, fast):
+        in_specs=[VM] * 5,
+        out_specs=(VM,) * 3,
+        **params(2 * tokens * 2100000 * 2, 10**7, 1),
+    )(x2, a2, w_up, w_down, vectors)
+
+
+def place_chunks(geo, owners, flat, base, me, outs, fast, table=None):
     for d in owners:
-        block = flat[pl.ds(geo.first(d, geo.shard) - base, geo.rows), :].astype(BF16)
+        block = flat[pl.ds(geo.first(d, geo.shard) - base, geo.rows), :]
+        if table is not None:
+            first, size = geo.param_rows, geo.embed_rows
+            tails = [
+                table[pl.ds(geo.first(e, geo.embed_shard), size), :] for e in (d, d + geo.devices // 2)
+            ]
+            block = jnp.concatenate([block[:first], *tails, block[first + 2 * size :]], 0)
+        block = block.astype(BF16)
         if fast:
             keep, send = outs
             relative = lax.bitwise_xor(me, d)
@@ -430,7 +457,7 @@
         in_specs=[SM] + [VM] * 8,
         out_specs=(VM,) * (2 + len(chunks)),
         scratch_shapes=[pltpu.VMEM((ROW_END - ROW_GAIN_TWO + CHUNK_PAD, LANES), F32)],
-        **params(4 * tokens * 2100000 * 2, 2 * 10**7),
+        **params(4 * tokens * 2100000 * 2, 2 * 10**7, 1),
     )(place, grad, x2, a2, gl, slope, w_up, w_down, vectors)
 
 
@@ -440,8 +467,8 @@
         refs = refs[1:]
     n_chunks = 2 if fast else 1
     if layer == 0:
-        outs, embed_outs = refs[:n_chunks], refs[n_chunks : 2 * n_chunks]
-        flat, qkv_grad, heads_grad, flat_table = refs[2 * n_chunks :]
+        outs, embed_outs = refs[:n_chunks], refs[n_chunks:-4]
+        flat, qkv_grad, heads_grad, flat_table = refs[-4:]
     else:
         grad_out = refs[0]
         outs = refs[1 : 1 + n_chunks]
@@ -503,28 +530,16 @@
         flat[pl.ds(ROW_BIAS_ONE + c, 1), :] = grad_bias[:, cols]
         flat[pl.ds(ROW_B_TIME + c, 1), :] = bias_grad[:, cols]
         flat[pl.ds(ROW_W_TIME + c, TD, stride=4), :] = weight_grad[:, cols]
-    place_chunks(geo, list(range(geo.devices // 2)), flat, 0, me, outs, fast)
     if layer == 0:
         kind = lax.broadcasted_iota(jnp.int32, (32, tokens), 0)
         table_grad = nn((chars[...] == kind).astype(BF16), total.astype(BF16))
         for c in range(4):
             flat_table[pl.ds(c, 32, stride=4), :] = table_grad[:, c * LANES : (c + 1) * LANES]
+    owners = list(range(geo.devices // 2))
+    place_chunks(geo, owners, flat, 0, me, outs, fast, flat_table if layer == 0 and fast else None)
+    if layer == 0 and not fast:
         for d in range(geo.devices):
-            block = flat_table[pl.ds(geo.first(d, geo.embed_shard), 8), :]
-            if fast:
-                relative = lax.bitwise_xor(me, d)
-                row = lax.shift_right_logical(relative, 1)
-                core = lax.bitwise_and(relative, 1)
-
-                @pl.when(core == 0)
-                def _():
-                    embed_outs[0][row] = block
-
-                @pl.when(core == 1)
-                def _():
-                    embed_outs[1][row] = block
-            else:
-                embed_outs[0][d] = block
+            embed_outs[0][d] = flat_table[pl.ds(geo.first(d, geo.embed_shard), 8), :]
 
 
 def back_attn(geo, layer, fast, seqs, place, grad, kept, weights, emb_t, rest, chars_row):
@@ -542,11 +557,8 @@
     ]
     if layer == 0:
         operands.append(chars_row)
-        if fast:
-            tables = (jax.ShapeDtypeStruct((geo.devices // 2, 8, LANES), F32),) * 2
-        else:
-            tables = (jax.ShapeDtypeStruct((geo.devices, 8, LANES), F32),)
-        shapes = shapes + tables
+        if not fast:
+            shapes = shapes + (jax.ShapeDtypeStruct((geo.devices, 8, LANES), F32),)
         scratch.append(pltpu.VMEM((4 * 32, LANES), F32))
     return pl.pallas_call(
         functools.partial(back_attn_kernel, geo, layer, fast, seqs),
@@ -554,7 +566,7 @@
         in_specs=[SM] + [VM] * len(operands),
         out_specs=(VM,) * len(shapes),
         scratch_shapes=scratch,
-        **params(4 * tokens * 1100000 * 2, 2 * 10**7),
+        **params(4 * tokens * 1100000 * 2, 2 * 10**7, 1),
     )(place, *operands)
 
 
@@ -565,26 +577,97 @@
 Z1, Z2, Z3, X, Y, CORE = 8, 16, 24, 4, 2, 1
 
 
-def gather_fast(geo, chunk):
+def after(value, *others):
+    return lax.optimization_barrier((value, *others))[0]
+
+
+def sync(*values):
+    return lax.optimization_barrier(values)
+
+
+def gather_both(geo, first, second):
     n, rows = geo.devices, geo.rows
     half = ceil_to(rows // 2, 16)
-    column = jnp.concatenate([chunk] + [permute(chunk, k, n) for k in (Z1, Z2, Z3)], 0)
-    over_x, over_y = permute(column, X, n), permute(column, Y, n)
+
+    def sides(held):
+        return permute(held, X, n), permute(held, Y, n)
+
+    def corners(over_x, over_y):
+        return permute(over_x[:half], Y, n), permute(over_y[half:], X, n)
+
+    def other(*arrays):
+        return permute(jnp.concatenate(arrays, 0), CORE, n)
+
+    near, over = permute(first, Z1, n), permute(first, Z2, n)
+    sides_0 = sides(first)
+    sides_0 = sync(*sides_0)
+    corners_0 = corners(*sides_0)
+    near, _ = sync(near, sides_0[0])
+    sides_1 = sides(near)
+    over, _ = sync(over, near)
+    far = permute(over, Z1, n)
+    sides_2 = sides(over)
+    *sides_1, _ = sync(*sides_1, over)
+    corners_1 = corners(*sides_1)
+    far, *corners_0 = sync(far, *corners_0, sides_1[0])[:3]
+    sides_3 = sides(far)
+    other_0 = other(first, *sides_0, *corners_0)
+    second, _ = sync(second, far)
+    near_b, over_b = permute(second, Z1, n), permute(second, Z2, n)
+    *sides_2, _ = sync(*sides_2, far)
+    corners_2 = corners(*sides_2)
+    *corners_1, _ = sync(*corners_1, sides_2[0])
+    other_1 = other(near, *sides_1, *corners_1)
+    *sides_3, _ = sync(*sides_3, sides_2[0])
+    corners_3 = corners(*sides_3)
+    over_b, near_b, _ = sync(over_b, near_b, sides_3[0])
+    far_b = permute(over_b, Z1, n)
+    *corners_2, _ = sync(*corners_2, sides_3[0])
+    other_2 = other(over, *sides_2, *corners_2)
+    *corners_3, far_b, _ = sync(*corners_3, far_b, corners_2[0])
+    other_3 = other(far, *sides_3, *corners_3)
+    column = jnp.concatenate([second, near_b, over_b, far_b], 0)
+    found = []
+    for z, arrays, packed in (
+        (0, (first, *sides_0, *corners_0), other_0),
+        (Z1, (near, *sides_1, *corners_1), other_1),
+        (Z2, (over, *sides_2, *corners_2), other_2),
+        (Z3, (far, *sides_3, *corners_3), other_3),
+    ):
+        pieces = [
+            (0, z, None, 0, rows),
+            (rows, z + X, None, 0, rows),
+            (2 * rows, z + Y, None, 0, rows),
+            (3 * rows, z + X + Y, None, 0, half),
+            (3 * rows + half, z + X + Y, None, half, rows - half),
+        ]
+        for array, (_, relative, _, at, count) in zip(arrays, pieces):
+            found.append((array, [(0, relative, None, at, count)]))
+        found.append((packed, [(src, rel + CORE, None, at, count) for src, rel, _, at, count in pieces]))
+    return found, column
+
+
+def gather_sides(geo, column):
+    return permute(column, X, geo.devices), permute(column, Y, geo.devices)
+
+
+def gather_corners(geo, over_x, over_y):
+    n, rows = geo.devices, geo.rows
+    half = ceil_to(rows // 2, 16)
     cut_x = over_x.reshape(4, rows, LANES)[:, :half].reshape(-1, LANES)
     cut_y = over_y.reshape(4, rows, LANES)[:, half:].reshape(-1, LANES)
-    corner_one, corner_two = permute(cut_x, Y, n), permute(cut_y, X, n)
+    return permute(cut_x, Y, n), permute(cut_y, X, n)
+
+
+def gathered_pieces(geo, arrays, others):
+    rows = geo.rows
+    half = ceil_to(rows // 2, 16)
     found = []
-    for array, relative, at, count in (
-        (column, 0, 0, rows),
-        (over_x, X, 0, rows),
-        (over_y, Y, 0, rows),
-        (corner_one, X + Y, 0, half),
-        (corner_two, X + Y, half, rows - half),
-    ):
-        for core in (0, CORE):
-            held = permute(array, core, n) if core else array
-            pieces = [(z * count, relative + core + 8 * z, None, at, count) for z in range(4)]
-            found.append((held, pieces))
+    for core, group in ((0, arrays), (CORE, others)):
+        for array, (relative, at, count) in zip(
+            group, ((0, 0, rows), (X, 0, rows), (Y, 0, rows), (X + Y, 0, half), (X + Y, half, rows - half))
+        ):
+            found.append((array, [(z * count, relative + core + 8 * z, None, at, count) for z in range(4)]))
     return found
 
 
@@ -600,43 +683,41 @@
     return total
 
 
-def plane_sum(geo, keep, send):
-    n, rows = geo.devices, geo.rows
-    half = ceil_to(rows // 2, 16)
-    keep = keep.reshape(2, 2, 2, rows, LANES)
-    came = permute(send, CORE, n).reshape(2, 2, 2, rows, LANES)
-    one = add(keep[:, :, :, :half], came[:, :, :, :half])
-    two = add(keep[:, :, :, half:], came[:, :, :, half:])
-    from_x = permute(one[1].astype(BF16), X, n)
-    from_y = permute(two[:, 1].astype(BF16), Y, n)
-    one = add(one[0], from_x)
-    two = add(two[:, 0], from_y)
-    from_y = permute(one[1].astype(BF16), Y, n)
-    from_x = permute(two[1].astype(BF16), X, n)
-    return jnp.concatenate([add(one[0], from_y), add(two[0], from_x)], 1)
-
-
-def column_sum(geo, place, upper, lower):
+def plane_start(geo, keep, came):
+    shape = (2, 2, 2, geo.rows, LANES)
+    half = ceil_to(geo.rows // 2, 16)
+    keep, came = keep.reshape(shape), came.reshape(shape)
+    one = (keep[:, :, :, :half], came[:, :, :, :half])
+    two = (keep[:, :, :, half:], came[:, :, :, half:])
+    to_x = add(*(part[1] for part in one)).astype(BF16)
+    to_y = add(*(part[:, 1] for part in two)).astype(BF16)
+    return [part[0] for part in one], [part[:, 0] for part in two], to_x, to_y
+
+
+def plane_next(one, two, from_x, from_y):
+    one, two = one + [from_x], two + [from_y]
+    to_y = add(*(part[1] for part in one)).astype(BF16)
+    to_x = add(*(part[1] for part in two)).astype(BF16)
+    return [part[0] for part in one], [part[0] for part in two], to_y, to_x
+
+
+def plane_end(one, two, from_y, from_x):
+    return jnp.concatenate([add(*one, from_y), add(*two, from_x)], 1)
+
+
+def column_sum(geo, place, upper, lower, table):
     n = geo.devices
+    if table:
+        row = lax.broadcasted_iota(jnp.int32, (1, geo.rows, 1), 1)
+        upper = jnp.where(row < geo.param_rows, upper, lower)
     is_upper = place[3] >= 2
     near = jnp.where(is_upper, upper, lower)
     far = jnp.where(is_upper, lower, upper).astype(BF16)
     return [near[0], permute(near[1].astype(BF16), Z1, n), permute(far[0], Z2, n), permute(far[1], Z3, n)]
 
 
-def table_sum(geo, keep, send):
-    n = geo.devices
-    total = add(keep, permute(send.astype(BF16), CORE, n)).reshape(4, 2, 2, 8, LANES)
-    total = add(total[:, 0], permute(total[:, 1].astype(BF16), X, n))
-    total = add(total[:, 0], permute(total[:, 1].astype(BF16), Y, n))
-    low = total.astype(BF16)
-    return [total[0]] + [permute(low[k], 8 * k, n) for k in (1, 2, 3)]
-
-
 def sum_any(chunks):
-    total = lax.psum_scatter(chunks.astype(F32), AXES, scatter_dimension=0, tiled=True)[0]
-    zero = jnp.zeros_like(total)
-    return [total, zero, zero, zero]
+    return lax.psum_scatter(chunks.astype(F32), AXES, scatter_dimension=0, tiled=True)[0]
 
 
 def timestep_embed(step_ids):
@@ -654,61 +735,110 @@
     place = jnp.stack(
         [index, index * geo.shard % LANES, index * geo.embed_shard % LANES, index // 8]
     ).astype(jnp.int32)
-    gather = gather_fast if fast else gather_any
     chunks = pack_shards(geo, place, layer_params, embed)
     emb = timestep_embed(steps).astype(BF16)
     emb_rows = jnp.concatenate([emb, jnp.zeros((8 - seqs, TD), BF16)], 0) if seqs < 8 else emb
     emb_t = emb.astype(F32).T
-    gathered = [gather(geo, chunk) for chunk in chunks]
-
-    stream = None
-    kept, weights = [], []
-    for layer in range(2):
-        got = unpack(geo, layer, place, gathered[layer])
-        if layer == 0:
-            first_inputs = [chars.reshape(tokens, 1), got[6]]
-        else:
-            first_inputs = [stream]
-        stream, *saved = forward(
-            layer, seqs, tokens, first_inputs, emb_rows, got[:6], F32 if layer == 0 else BF16
-        )
-        kept.append(saved)
-        weights.append(got[:6])
+    chars_row, chars_col = chars.reshape(1, tokens), chars.reshape(tokens, 1)
+    n = geo.devices
+
+    def up(layer, gathered):
+        return unpack(geo, layer, place, gathered)
+
+    def ahead(layer, first_inputs, got):
+        w_time, w_qkv, w_out, _, _, vectors = got[:6]
+        return ahead_attn(layer, seqs, tokens, first_inputs, emb_rows, (w_time, w_qkv, w_out, vectors))
+
+    def ahead_rest(layer, saved, got):
+        x2, a2 = saved[5:]
+        stream, gl, slope = ahead_mlp(x2, a2, got[3], got[4], got[5], F32 if layer == 0 else BF16)
+        return stream, list(saved[:6]) + [a2, gl, slope]
+
+    def mlp(layer, grad, saved, got):
+        kept, weights = saved[5:], (got[3], got[4], got[5])
+        return back_mlp(geo, layer, fast, place, grad, kept, weights)
+
+    def attn(layer, grad, saved, got, rest):
+        weights = (got[1], got[2], got[5])
+        return back_attn(geo, layer, fast, seqs, place, grad, saved[:5], weights, emb_t, rest, chars_row)
+
+    grad = cotangent.reshape(tokens, D)
+    if not fast:
+        first = up(0, gather_any(geo, chunks[0]))
+        stream, saved_first = ahead_rest(0, ahead(0, [chars_col, first[6]], first), first)
+        second = up(1, gather_any(geo, chunks[1]))
+        stream, saved_second = ahead_rest(1, ahead(1, [stream], second), second)
+        grad, rest, upper_second = mlp(1, grad, saved_second, second)
+        grad, lower_second = attn(1, grad, saved_second, second, rest)
+        grad, rest, upper_first = mlp(0, grad, saved_first, first)
+        lower_first, tables = attn(0, grad, saved_first, first, rest)
+        firsts = sum_any(jnp.concatenate([lower_first, upper_first], 0))
+        seconds = sum_any(jnp.concatenate([lower_second, upper_second], 0))
+        grad_params, grad_embed = finish(geo, fast, place, [firsts, seconds, sum_any(tables)])
+        return (stream.reshape(seqs, length, D), grad_embed, grad_params)
+
+    gathered, column = gather_both(geo, *chunks)
+    sides = gather_sides(geo, column)
+    column_other = permute(column, CORE, n)
+    first = up(0, gathered)
+    saved_first = ahead(0, [chars_col, first[6]], first)
+    saved_first, sides, column_other = sync(saved_first, sides, column_other)
+    corners = gather_corners(geo, *sides)
+    sides_other = [permute(side, CORE, n) for side in sides]
+    stream, saved_first = ahead_rest(0, saved_first, first)
+    stream, corners, sides_other = sync(stream, corners, sides_other)
+    corners_other = [permute(corner, CORE, n) for corner in corners]
+    second = up(1, gathered_pieces(geo, [column, *sides, *corners], [column_other, *sides_other, *corners_other]))
+    stream, saved_second = ahead_rest(1, ahead(1, [stream], second), second)
     output = stream.reshape(seqs, length, D)
 
-    grad = cotangent.reshape(tokens, D)
-    sums = [None, None]
-    for layer in (1, 0):
-        x, a, qkv, prob, o, x2, a2, gl, slope = kept[layer]
-        w_time, w_qkv, w_out, w_up, w_down, vectors = weights[layer]
-        grad, rest, *upper = back_mlp(
-            geo, layer, fast, place, grad, (x2, a2, gl, slope), (w_up, w_down, vectors)
-        )
-        if fast:
-            upper = plane_sum(geo, *upper)
-        got = back_attn(
-            geo,
-            layer,
-            fast,
-            seqs,
-            place,
-            grad,
-            (x, a, qkv, prob, o),
-            (w_qkv, w_out, vectors),
-            emb_t,
-            rest,
-            chars.reshape(1, tokens),
-        )
-        if layer == 0:
-            lower, tables = (got[:2], got[2:]) if fast else (got[:1], got[1:])
-        else:
-            grad, *lower = got
-        if fast:
-            sums[layer] = column_sum(geo, place, upper, plane_sum(geo, *lower))
-        else:
-            sums[layer] = sum_any(jnp.concatenate([lower[0], upper[0]], 0))
-    tables = table_sum(geo, *tables) if fast else sum_any(tables[0])
-    grad_params, grad_embed = finish(geo, place, sums[0], sums[1], tables)
+    def cross(to_one, to_two, one, two):
+        return permute(to_one, one, n), permute(to_two, two, n)
+
+    grad, rest, keep_u, send_u = mlp(1, grad, saved_second, second)
+    came_u = permute(send_u, CORE, n)
+    grad, keep_l, send_l = attn(1, grad, saved_second, second, rest)
+    grad, keep_u, came_u, keep_l, send_l = sync(grad, keep_u, came_u, keep_l, send_l)
+    came_l = permute(send_l, CORE, n)
+    one_u, two_u, to_x, to_y = plane_start(geo, keep_u, came_u)
+    from_u = cross(to_x, to_y, X, Y)
+
+    grad, rest, keep, send = mlp(0, after(grad, to_x, to_y), saved_first, first)
+    grad, rest, keep, send, came_l, from_u = sync(grad, rest, keep, send, came_l, from_u)
+    came = permute(send, CORE, n)
+    one_u, two_u, to_y, to_x = plane_next(one_u, two_u, *from_u)
+    from_u = cross(to_y, to_x, Y, X)
+    one_l, two_l, to_x_l, to_y_l = plane_start(geo, keep_l, came_l)
+    from_l = cross(to_x_l, to_y_l, X, Y)
+
+    grad = after(grad, to_x, to_y, to_x_l, to_y_l)
+    low_keep, low_send = attn(0, grad, saved_first, first, rest)
+    low_keep, low_send, keep, came, from_u, from_l = sync(low_keep, low_send, keep, came, from_u, from_l)
+    low_came = permute(low_send, CORE, n)
+    one_l, two_l, to_y, to_x = plane_next(one_l, two_l, *from_l)
+    from_l = cross(to_y, to_x, Y, X)
+    one, two, to_x, to_y = plane_start(geo, keep, came)
+    from_up = cross(to_x, to_y, X, Y)
+    upper = plane_end(one_u, two_u, *from_u)
+
+    low_came, low_keep, upper, _, _ = sync(low_came, low_keep, upper, to_x, to_y)
+    low_one, low_two, to_x, to_y = plane_start(geo, low_keep, low_came)
+    from_low = cross(to_x, to_y, X, Y)
+
+    from_l, from_up, _, _ = sync(from_l, from_up, to_x, to_y)
+    lower = plane_end(one_l, two_l, *from_l)
+    seconds = column_sum(geo, place, upper, lower, False)
+    one, two, to_y, to_x = plane_next(one, two, *from_up)
+    from_up = cross(to_y, to_x, Y, X)
+
+    from_low, _, _ = sync(from_low, to_y, to_x)
+    low_one, low_two, to_y, to_x = plane_next(low_one, low_two, *from_low)
+    from_low = cross(to_y, to_x, Y, X)
+
+    from_low, from_up = sync(from_low, from_up)
+    upper, lower = plane_end(one, two, *from_up), plane_end(low_one, low_two, *from_low)
+    firsts = column_sum(geo, place, upper, lower, True)
+    grad_params, grad_embed = finish(geo, fast, place, firsts + seconds)
     return (output, grad_embed, grad_params)
 
 

time: 337 us -> 273 us (0.81)
  the two profiles are of different devices: /device:TPU:0 before, /device:TPU:16 now
where the time goes in v2:
time: 273 us; the launch traced here: 269 us
  Pallas kernels  118 us (43%)
  waiting for transfers between devices  56.1 us (21%)
  starting transfers between devices  54.7 us (20%)
  local copies, waits for them, and re-layouts  19.6 us (7%)
  other arithmetic  18.4 us (7%)
    ppermute x61, waiting for transfers between devices, permute(): lax.ppermute(value, AXES, [(d, d ^ distance) for d in range(devices)])  56.1 us
    ppermute x61, starting transfers between devices, permute(): lax.ppermute(value, AXES, [(d, d ^ distance) for d in range(devices)])  54.7 us
    pallas_call x2, Pallas kernels, back_attn(): pl.pallas_call(functools.partial(back_attn_kernel, geo, layer, fast, seqs...  29.8 us
    pallas_call x2, Pallas kernels, back_mlp(): pl.pallas_call(functools.partial(back_mlp_kernel, geo, layer, fast), out_...  26.9 us
    pallas_call x2, Pallas kernels, ahead_attn(): pl.pallas_call(functools.partial(ahead_attn_kernel, layer, seqs), out_sha...  21 us
    pallas_call x2, Pallas kernels, unpack(): pl.pallas_call(functools.partial(unpack_kernel, geo, layer, plan), out_sh...  19 us
    pallas_call x2, Pallas kernels, ahead_mlp(): pl.pallas_call(ahead_mlp_kernel, out_shape=shapes, in_specs=[VM] * 5, out...  18.2 us
    unnamed x92, local copies, waits for them, and re-layouts  13.6 us
  transfers between devices with their start and end apart: 61, of which 25 were waited for; matrix products, arithmetic and copies ran while one was open for 11% of the time, Pallas kernels for 27%

profile of v2, /device:TPU:16, one launch (start us, length us, event | category | flops | bytes accessed | tf_op | source)
XLA Modules:
  0.0 268.6 jit_solution(11153431168480132617)
XLA Ops:
  0.7 1.4 pad_bitcast_fusion
  3.0 1.6 collective-permute-start
  4.5 1.5 collective-permute-start.1
  6.1 1.6 collective-permute-start.3
  8.0 1.9 collective-permute-done.refs_1_
  11.1 3.5 %collective-permute-done.3.refs_6_ = bf16[800,128]{1,0:T(8,128)(2,1)S(1)} collective-permute-done((bf16[800,128]{1,0:T(8,128)(2,1)S(1)}, bf16[800,128]{1,0:T(8,128)(2,1)S(1)}, u32[]{:S(2)}, u32[]{:S(2)}) %collective-permute-start.3) | collective-permute-done | bytes 204832 | tf_op jit(solution)/shard_map/ppermute | solution.py:574
  16.7 2.7 %collective-permute-start.4 = (bf16[800,128]{1,0:T(8,128)(2,1)S(1)}, bf16[800,128]{1,0:T(8,128)(2,1)S(1)}, u32[]{:S(2)}, u32[]{:S(2)}) collective-permute-start(bf16[800,128]{1,0:T(8,128)(2,1)S(1)} %collective-permute-done.2.refs_12_), channel_id=1, source_target_pairs={{0,8},{1,9},{2,10},{3,11},{4,12},{5,13},{6,14},{7,15},{8,0},{9,1},... | collective-permute-start | bytes 614408 | tf_op jit(solution)/shard_map/ppermute | solution.py:574
  20.6 1.4 collective-permute-start.6
  22.9 1.5 collective-permute-start.13
  24.4 1.3 collective-permute-done.5.refs_3_
  29.5 1.2 collective-permute-done.12.refs_13_
  34.2 1.2 collective-permute-done.10.refs_9_
  35.4 2.6 collective-permute-start.23
  38.8 3.9 %collective-permute-done.15.refs_15_ = bf16[400,128]{1,0:T(8,128)(2,1)S(1)} collective-permute-done((bf16[400,128]{1,0:T(8,128)(2,1)S(1)}, bf16[400,128]{1,0:T(8,128)(2,1)S(1)}, u32[]{:S(2)}, u32[]{:S(2)}) %collective-permute-start.15) | collective-permute-done | bytes 102432 | tf_op jit(solution)/shard_map/ppermute | solution.py:574
  43.2 1.7 collective-permute-start.20
  45.0 2.0 collective-permute-start.24
  52.2 2.0 collective-permute-start.26
  56.6 10.0 %shard_map.77 = (bf16[128,512]{1,0:T(8,128)(2,1)S(1)}, bf16[512,1536]{1,0:T(8,128)(2,1)}, bf16[512,512]{1,0:T(8,128)(2,1)}, bf16[512,2048]{1,0:T(8,128)(2,1)}, b...) custom-call(s32[4]{0:T(128)S(1)} %pad_add_fusion.place_ref, ...), custom_call_target="tpu_custom_call" | custom-call | flops 10000000 | bytes 25731072 | tf_op jit(solution)/shard_map/pallas_call | solution.py:225
  66.7 10.1 %shard_map.78 = (f32[512,512]{1,0:T(8,128)}, bf16[512,512]{1,0:T(8,128)(2,1)S(1)}, bf16[512,1536]{1,0:T(8,128)(2,1)}, bf16[16,256,256]{2,1,0:T(8,128)(2,1)}, bf1...) custom-call(s32[512,1]{1,0:T(8,128)S(1)} %bitcast.151, ...), custom_call_target="tpu_custom_call" | custom-call | flops 2252800000 | bytes 10000000 | tf_op jit(solution)/shard_map/pallas_call | solution.py:331
  80.6 9.3 %shard_map.79 = (f32[512,512]{1,0:T(8,128)S(1)}, bf16[512,2048]{1,0:T(8,128)(2,1)}, bf16[512,2048]{1,0:T(8,128)(2,1)}) custom-call(f32[512,512]{1,0:T(8,128)} %get-tuple-element.163.x2, bf16[512,512]{1,0:T(8,128)(2,1)S(1)} %copy-done.6, bf16[512,2048]{1,0:T(8,128)(2,1)} %get-tuple-element.165.w_up, bf16[2048,512]{1,0:T(8,128)(2,1)} %get-tuple-element.166.w_down, ...), custom_call_target="tpu_custom_call" | custom-call | flops 4300800000 | bytes 10000000 | tf_op jit(solution)/shard_map/pallas_call | solution.py:359
  92.2 1.2 collective-permute-done.33.refs_8_
  94.1 9.0 %shard_map.80 = (bf16[128,512]{1,0:T(8,128)(2,1)S(1)}, bf16[512,1536]{1,0:T(8,128)(2,1)}, bf16[512,512]{1,0:T(8,128)(2,1)}, bf16[512,2048]{1,0:T(8,128)(2,1)}, b...) custom-call(s32[4]{0:T(128)S(1)} %pad_add_fusion.place_ref, bf16[3200,128]{1,0:T(8,128)(2,1)} %copy-done.12, ...), custom_call_target="tpu_custom_call" | custom-call | flops 10000000 | bytes 25731072 | tf_op jit(solution)/shard_map/pallas_call | solution.py:225
  103.1 10.9 %shard_map.81 = (f32[512,512]{1,0:T(8,128)}, bf16[512,512]{1,0:T(8,128)(2,1)S(1)}, bf16[512,1536]{1,0:T(8,128)(2,1)}, bf16[16,256,256]{2,1,0:T(8,128)(2,1)}, bf1...) custom-call(f32[512,512]{1,0:T(8,128)} %copy-done.3, ...), custom_call_target="tpu_custom_call" | custom-call | flops 2252800000 | bytes 10000000 | tf_op jit(solution)/shard_map/pallas_call | solution.py:331
  114.0 1.2 copy-done.4
  115.2 8.9 %shard_map.82 = (bf16[512,512]{1,0:T(8,128)(2,1)}, bf16[512,2048]{1,0:T(8,128)(2,1)}, bf16[512,2048]{1,0:T(8,128)(2,1)}) custom-call(f32[512,512]{1,0:T(8,128)S(1)} %copy-done.4, bf16[512,512]{1,0:T(8,128)(2,1)S(1)} %get-tuple-element.181.a2, bf16[512,2048]{1,0:T(8,128)(2,1)} %get-tuple-element.182.w_up, bf16[2048,512]{1,0:T(8,128)(2,1)} %get-tuple-element.183.w_down, ...), custom_call_target="tpu_custom_call" | custom-call | flops 4300800000 | bytes 10000000 | tf_op jit(solution)/shard_map/pallas_call | solution.py:359
  124.1 13.5 %shard_map.83 = (f32[512,512]{1,0:T(8,128)}, f32[4648,128]{1,0:T(8,128)}, bf16[8,800,128]{2,1,0:T(8,128)(2,1)}, bf16[8,800,128]{2,1,0:T(8,128)(2,1)}) custom-call(s32[4]{0:T(128)S(1)} %pad_add_fusion.place_ref, bf16[512,512]{1,0:T(8,128)(2,1)S(1)} %bitcast.157, f32[512,512]{1,0:T(8,128)} %get-tuple-element.180.x2, ...), custom_call_target="tpu_custom_call" | custom-call | flops 8601600000 | bytes 20000000 | tf_op jit(solution)/shard_map/pallas_call | solution.py:450
  137.9 15.0 %shard_map.84 = (f32[512,512]{1,0:T(8,128)}, bf16[8,800,128]{2,1,0:T(8,128)(2,1)}, bf16[8,800,128]{2,1,0:T(8,128)(2,1)}) custom-call(s32[4]{0:T(128)S(1)} %pad_add_fusion.place_ref, f32[512,512]{1,0:T(8,128)} %get-tuple-element.187.grad, f32[512,512]{1,0:T(8,128)} %get-tuple-element.188.x, bf16[512,512]{1,0:T(8,128)(2,1)S(1)} %get-tuple-element.189.a, ...), custom_call_target="tpu_custom_call" | custom-call | flops 4505600000 | bytes 20000000 | tf_op jit(solution)/shard_map/pallas_call | solution.py:563
  154.4 1.2 collective-permute-start.37
  157.9 13.3 %shard_map.85 = (f32[512,512]{1,0:T(8,128)S(1)}, f32[4648,128]{1,0:T(8,128)}, bf16[8,800,128]{2,1,0:T(8,128)(2,1)}, bf16[8,800,128]{2,1,0:T(8,128)(2,1)}) custom-call(s32[4]{0:T(128)S(1)} %pad_add_fusion.place_ref, f32[512,512]{1,0:T(8,128)} %get-tuple-element.202.grad, f32[512,512]{1,0:T(8,128)} %get-tuple-element.163.x2, bf16[512,512]{1,0:T(8,128)(2,1)S(1)} %copy-done.6, ...), custom_call_target="tpu_custom_call" | custom-call | flops 8601600000 | bytes 20000000 | tf_op jit(solution)/shard_map/pallas_call | solution.py:450
  172.0 2.2 fusion.24
  176.2 1.2 collective-permute-start.42
  178.8 14.8 %shard_map.86 = (bf16[8,800,128]{2,1,0:T(8,128)(2,1)}, bf16[8,800,128]{2,1,0:T(8,128)(2,1)}) custom-call(s32[4]{0:T(128)S(1)} %pad_add_fusion.place_ref, f32[512,512]{1,0:T(8,128)} %copy-done.5, f32[512,512]{1,0:T(8,128)} %get-tuple-element.216.x, bf16[512,512]{1,0:T(8,128)(2,1)S(1)} %get-tuple-element.217.a, bf16[512,1536]{1,0:T(8,128)(2,1)} %get-tuple-element.218.qkv, ...), custom_call_target="tpu_custom_call" | custom-call | flops 4505600000 | bytes 20000000 | tf_op jit(solution)/shard_map/pallas_call | solution.py:563
  194.3 1.4 fusion.22
  198.7 1.2 collective-permute-start.46
  202.3 1.5 fusion.21
  208.0 5.4 %collective-permute-done.46 = bf16[2,2,400,128]{3,2,1,0:T(8,128)(2,1)S(1)} collective-permute-done((bf16[2,2,400,128]{3,2,1,0:T(8,128)(2,1)S(1)}, bf16[2,2,400,128]{3,2,1,0:T(8,128)(2,1)S(1)}, u32[]{:S(2)}, u32[]{:S(2)}) %collective-permute-start.46) | collective-permute-done | bytes 409632 | tf_op jit(solution)/shard_map/ppermute | solution.py:574
  216.8 1.5 fusion.11
  220.4 1.8 collective-permute-done.49
  222.3 1.2 fusion.15
  226.9 1.7 collective-permute-start.60
  230.5 1.6 fusion.13
  234.5 1.6 collective-permute-start.57
  236.2 4.7 %collective-permute-done.59.refs_6_ = bf16[800,128]{1,0:T(8,128)(2,1)S(1)} collective-permute-done((bf16[800,128]{1,0:T(8,128)(2,1)S(1)}, bf16[800,128]{1,0:T(8,128)(2,1)S(1)}, u32[]{:S(2)}, u32[]{:S(2)}) %collective-permute-start.59) | collective-permute-done | bytes 204832 | tf_op jit(solution)/shard_map/ppermute | solution.py:574
  240.9 13.1 %collective-permute-done.60.refs_7_ = bf16[800,128]{1,0:T(8,128)(2,1)S(1)} collective-permute-done((bf16[800,128]{1,0:T(8,128)(2,1)S(1)}, bf16[800,128]{1,0:T(8,128)(2,1)S(1)}, u32[]{:S(2)}, u32[]{:S(2)}) %collective-permute-start.60) | collective-permute-done | bytes 204832 | tf_op jit(solution)/shard_map/ppermute | solution.py:574
  254.1 2.4 collective-permute-done.56.refs_2_
  256.4 6.1 %collective-permute-done.57.refs_3_ = bf16[800,128]{1,0:T(8,128)(2,1)S(1)} collective-permute-done((bf16[800,128]{1,0:T(8,128)(2,1)S(1)}, bf16[800,128]{1,0:T(8,128)(2,1)S(1)}, u32[]{:S(2)}, u32[]{:S(2)}) %collective-permute-start.57) | collective-permute-done | bytes 204832 | tf_op jit(solution)/shard_map/ppermute | solution.py:574
  262.6 2.2 shard_map.87
  265.4 1.8 copy.22
  (230 shorter events, 62.2 us)
Async XLA Ops:
  3.0 6.9 %collective-permute-start = (bf16[800,128]{1,0:T(8,128)(2,1)S(1)}, bf16[800,128]{1,0:T(8,128)(2,1)S(1)}, u32[]{:S(2)}, u32[]{:S(2)}) collective-permute-start(bf16[800,128]{1,0:T(8,128)(2,1)S(1)} %get-tuple-element.126.refs_0_), channel_id=1, source_target_pairs={{0,4},{1,5},{2,6},{3,7},{4,0},{5,1},{6,2},{7,3},{8,12},{9,13},{10,... | collective-permute-start | bytes 614408 | tf_op jit(solution)/shard_map/ppermute | solution.py:574
  4.5 6.5 %collective-permute-start.1 = (bf16[800,128]{1,0:T(8,128)(2,1)S(1)}, bf16[800,128]{1,0:T(8,128)(2,1)S(1)}, u32[]{:S(2)}, u32[]{:S(2)}) collective-permute-start(bf16[800,128]{1,0:T(8,128)(2,1)S(1)} %get-tuple-element.126.refs_0_), channel_id=1, source_target_pairs={{0,2},{1,3},{2,0},{3,1},{4,6},{5,7},{6,4},{7,5},{8,10},{9,11},{10,... | collective-permute-start | bytes 614408 | tf_op jit(solution)/shard_map/ppermute | solution.py:574
  6.1 8.5 %collective-permute-start.3 = (bf16[800,128]{1,0:T(8,128)(2,1)S(1)}, bf16[800,128]{1,0:T(8,128)(2,1)S(1)}, u32[]{:S(2)}, u32[]{:S(2)}) collective-permute-start(bf16[800,128]{1,0:T(8,128)(2,1)S(1)} %get-tuple-element.126.refs_0_), channel_id=1, source_target_pairs={{0,8},{1,9},{2,10},{3,11},{4,12},{5,13},{6,14},{7,15},{8,0},{9,1},... | collective-permute-start | bytes 614408 | tf_op jit(solution)/shard_map/ppermute | solution.py:574
  7.6 9.1 %collective-permute-start.2 = (bf16[800,128]{1,0:T(8,128)(2,1)S(1)}, bf16[800,128]{1,0:T(8,128)(2,1)S(1)}, u32[]{:S(2)}, u32[]{:S(2)}) collective-permute-start(bf16[800,128]{1,0:T(8,128)(2,1)S(1)} %get-tuple-element.126.refs_0_), channel_id=1, source_target_pairs={{0,16},{1,17},{2,18},{3,19},{4,20},{5,21},{6,22},{7,23},{8,24},{9,... | collective-permute-start | bytes 614408 | tf_op jit(solution)/shard_map/ppermute | solution.py:574
  14.6 7.5 %collective-permute-start.7 = (bf16[800,128]{1,0:T(8,128)(2,1)S(1)}, bf16[800,128]{1,0:T(8,128)(2,1)S(1)}, u32[]{:S(2)}, u32[]{:S(2)}) collective-permute-start(bf16[800,128]{1,0:T(8,128)(2,1)S(1)} %collective-permute-done.3.refs_6_), channel_id=1, source_target_pairs={{0,4},{1,5},{2,6},{3,7},{4,0},{5,1},{6,2},{7,3},{8,12},{9,13},{10,... | collective-permute-start | bytes 614408 | tf_op jit(solution)/shard_map/ppermute | solution.py:574
  15.1 7.8 %collective-permute-start.8 = (bf16[800,128]{1,0:T(8,128)(2,1)S(1)}, bf16[800,128]{1,0:T(8,128)(2,1)S(1)}, u32[]{:S(2)}, u32[]{:S(2)}) collective-permute-start(bf16[800,128]{1,0:T(8,128)(2,1)S(1)} %collective-permute-done.3.refs_6_), channel_id=1, source_target_pairs={{0,2},{1,3},{2,0},{3,1},{4,6},{5,7},{6,4},{7,5},{8,10},{9,11},{10,... | collective-permute-start | bytes 614408 | tf_op jit(solution)/shard_map/ppermute | solution.py:574
  16.7 9.7 %collective-permute-start.4 = (bf16[800,128]{1,0:T(8,128)(2,1)S(1)}, bf16[800,128]{1,0:T(8,128)(2,1)S(1)}, u32[]{:S(2)}, u32[]{:S(2)}) collective-permute-start(bf16[800,128]{1,0:T(8,128)(2,1)S(1)} %collective-permute-done.2.refs_12_), channel_id=1, source_target_pairs={{0,8},{1,9},{2,10},{3,11},{4,12},{5,13},{6,14},{7,15},{8,0},{9,1},... | collective-permute-start | bytes 614408 | tf_op jit(solution)/shard_map/ppermute | solution.py:574
  22.1 8.7 %collective-permute-start.12 = (bf16[800,128]{1,0:T(8,128)(2,1)S(1)}, bf16[800,128]{1,0:T(8,128)(2,1)S(1)}, u32[]{:S(2)}, u32[]{:S(2)}) collective-permute-start(bf16[800,128]{1,0:T(8,128)(2,1)S(1)} %collective-permute-done.2.refs_12_), channel_id=1, source_target_pairs={{0,4},{1,5},{2,6},{3,7},{4,0},{5,1},{6,2},{7,3},{8,12},{9,13},{10,... | collective-permute-start | bytes 614408 | tf_op jit(solution)/shard_map/ppermute | solution.py:574
  22.9 9.0 %collective-permute-start.13 = (bf16[800,128]{1,0:T(8,128)(2,1)S(1)}, bf16[800,128]{1,0:T(8,128)(2,1)S(1)}, u32[]{:S(2)}, u32[]{:S(2)}) collective-permute-start(bf16[800,128]{1,0:T(8,128)(2,1)S(1)} %collective-permute-done.2.refs_12_), channel_id=1, source_target_pairs={{0,2},{1,3},{2,0},{3,1},{4,6},{5,7},{6,4},{7,5},{8,10},{9,11},{10,... | collective-permute-start | bytes 614408 | tf_op jit(solution)/shard_map/ppermute | solution.py:574
  26.4 12.1 %collective-permute-start.17 = (bf16[800,128]{1,0:T(8,128)(2,1)S(1)}, bf16[800,128]{1,0:T(8,128)(2,1)S(1)}, u32[]{:S(2)}, u32[]{:S(2)}) collective-permute-start(bf16[800,128]{1,0:T(8,128)(2,1)S(1)} %collective-permute-done.4.refs_18_), channel_id=1, source_target_pairs={{0,4},{1,5},{2,6},{3,7},{4,0},{5,1},{6,2},{7,3},{8,12},{9,13},{10,... | collective-permute-start | bytes 614408 | tf_op jit(solution)/shard_map/ppermute | solution.py:574
  27.4 11.3 %collective-permute-start.18 = (bf16[800,128]{1,0:T(8,128)(2,1)S(1)}, bf16[800,128]{1,0:T(8,128)(2,1)S(1)}, u32[]{:S(2)}, u32[]{:S(2)}) collective-permute-start(bf16[800,128]{1,0:T(8,128)(2,1)S(1)} %collective-permute-done.4.refs_18_), channel_id=1, source_target_pairs={{0,2},{1,3},{2,0},{3,1},{4,6},{5,7},{6,4},{7,5},{8,10},{9,11},{10,... | collective-permute-start | bytes 614408 | tf_op jit(solution)/shard_map/ppermute | solution.py:574
  28.2 16.7 %collective-permute-start.22 = (bf16[800,128]{1,0:T(8,128)(2,1)S(1)}, bf16[800,128]{1,0:T(8,128)(2,1)S(1)}, u32[]{:S(2)}, u32[]{:S(2)}) collective-permute-start(bf16[800,128]{1,0:T(8,128)(2,1)S(1)} %get-tuple-element.145), channel_id=1, source_target_pairs={{0,16},{1,17},{2,18},{3,19},{4,20},{5,21},{6,22},{7,23},{8,24},{9,... | collective-permute-start | bytes 614408 | tf_op jit(solution)/shard_map/ppermute | solution.py:574
  35.4 9.5 %collective-permute-start.23 = (bf16[800,128]{1,0:T(8,128)(2,1)S(1)}, bf16[800,128]{1,0:T(8,128)(2,1)S(1)}, u32[]{:S(2)}, u32[]{:S(2)}) collective-permute-start(bf16[800,128]{1,0:T(8,128)(2,1)S(1)} %get-tuple-element.145), channel_id=1, source_target_pairs={{0,8},{1,9},{2,10},{3,11},{4,12},{5,13},{6,14},{7,15},{8,0},{9,1},... | collective-permute-start | bytes 614408 | tf_op jit(solution)/shard_map/ppermute | solution.py:574
  38.7 15.5 %collective-permute-start.9 = (bf16[3200,128]{1,0:T(8,128)(2,1)S(1)}, bf16[3200,128]{1,0:T(8,128)(2,1)S(1)}, u32[]{:S(2)}, u32[]{:S(2)}) collective-permute-start(bf16[3200,128]{1,0:T(8,128)(2,1)S(1)} %constant_dynamic-update-slice_fusion), channel_id=1, source_target_pairs={{0,1},{1,0},{2,3},{3,2},{4,5},{5,4},{6,7},{7,6},{8,9},{9,8},{10,11... | collective-permute-start | bytes 2457608 | tf_op jit(solution)/shard_map/ppermute | solution.py:574
  42.7 12.5 %collective-permute-start.14 = (bf16[3200,128]{1,0:T(8,128)(2,1)S(1)}, bf16[3200,128]{1,0:T(8,128)(2,1)S(1)}, u32[]{:S(2)}, u32[]{:S(2)}) collective-permute-start(bf16[3200,128]{1,0:T(8,128)(2,1)S(1)} %constant_dynamic-update-slice_fusion.5), channel_id=1, source_target_pairs={{0,1},{1,0},{2,3},{3,2},{4,5},{5,4},{6,7},{7,6},{8,9},{9,8},{10,11... | collective-permute-start | bytes 2457608 | tf_op jit(solution)/shard_map/ppermute | solution.py:574
  43.2 6.5 %collective-permute-start.20 = (bf16[400,128]{1,0:T(8,128)(2,1)S(1)}, bf16[400,128]{1,0:T(8,128)(2,1)S(1)}, u32[]{:S(2)}, u32[]{:S(2)}) collective-permute-start(bf16[400,128]{1,0:T(8,128)(2,1)S(1)} %slice.388), channel_id=1, source_target_pairs={{0,2},{1,3},{2,0},{3,1},{4,6},{5,7},{6,4},{7,5},{8,10},{9,11},{10,... | collective-permute-start | bytes 307208 | tf_op jit(solution)/shard_map/ppermute | solution.py:574
  49.7 6.9 %collective-permute-start.19 = (bf16[3200,128]{1,0:T(8,128)(2,1)}, bf16[3200,128]{1,0:T(8,128)(2,1)}, u32[]{:S(2)}, u32[]{:S(2)}) collective-permute-start(bf16[3200,128]{1,0:T(8,128)(2,1)} %constant_dynamic-update-slice_fusion.10), channel_id=1, source_target_pairs={{0,1},{1,0},{2,3},{3,2},{4,5},{5,4},{6,7},{7,6},{8,9},{9,8},{10,11... | collective-permute-start | bytes 2457608 | tf_op jit(solution)/shard_map/ppermute | solution.py:574
  52.2 24.6 %collective-permute-start.26 = (bf16[3200,128]{1,0:T(8,128)(2,1)S(1)}, bf16[3200,128]{1,0:T(8,128)(2,1)}, u32[]{:S(2)}, u32[]{:S(2)}) collective-permute-start(bf16[3200,128]{1,0:T(8,128)(2,1)S(1)} %constant_dynamic-update-slice_fusion.20.refs_0_), channel_id=1, source_target_pairs={{0,4},{1,5},{2,6},{3,7},{4,0},{5,1},{6,2},{7,3},{8,12},{9,13},{10,... | collective-permute-start | bytes 2457608 | tf_op jit(solution)/shard_map/ppermute | solution.py:574
  54.2 22.6 %collective-permute-start.27 = (bf16[3200,128]{1,0:T(8,128)(2,1)S(1)}, bf16[3200,128]{1,0:T(8,128)(2,1)}, u32[]{:S(2)}, u32[]{:S(2)}) collective-permute-start(bf16[3200,128]{1,0:T(8,128)(2,1)S(1)} %constant_dynamic-update-slice_fusion.20.refs_0_), channel_id=1, source_target_pairs={{0,2},{1,3},{2,0},{3,1},{4,6},{5,7},{6,4},{7,5},{8,10},{9,11},{10,... | collective-permute-start | bytes 2457608 | tf_op jit(solution)/shard_map/ppermute | solution.py:574
  55.3 21.5 %collective-permute-start.28 = (bf16[3200,128]{1,0:T(8,128)(2,1)S(1)}, bf16[3200,128]{1,0:T(8,128)(2,1)}, u32[]{:S(2)}, u32[]{:S(2)}) collective-permute-start(bf16[3200,128]{1,0:T(8,128)(2,1)S(1)} %constant_dynamic-update-slice_fusion.20.refs_0_), channel_id=1, source_target_pairs={{0,1},{1,0},{2,3},{3,2},{4,5},{5,4},{6,7},{7,6},{8,9},{9,8},{10,11... | collective-permute-start | bytes 2457608 | tf_op jit(solution)/shard_map/ppermute | solution.py:574
  76.7 14.9 %collective-permute-start.31 = (bf16[3200,128]{1,0:T(8,128)(2,1)}, bf16[3200,128]{1,0:T(8,128)(2,1)S(1)}, u32[]{:S(2)}, u32[]{:S(2)}) collective-permute-start(bf16[3200,128]{1,0:T(8,128)(2,1)} %collective-permute-done.26.refs_1_), channel_id=1, source_target_pairs={{0,1},{1,0},{2,3},{3,2},{4,5},{5,4},{6,7},{7,6},{8,9},{9,8},{10,11... | collective-permute-start | bytes 2457608 | tf_op jit(solution)/shard_map/ppermute | solution.py:574
  76.8 14.8 %collective-permute-start.32 = (bf16[3200,128]{1,0:T(8,128)(2,1)}, bf16[3200,128]{1,0:T(8,128)(2,1)S(1)}, u32[]{:S(2)}, u32[]{:S(2)}) collective-permute-start(bf16[3200,128]{1,0:T(8,128)(2,1)} %collective-permute-done.27.refs_2_), channel_id=1, source_target_pairs={{0,1},{1,0},{2,3},{3,2},{4,5},{5,4},{6,7},{7,6},{8,9},{9,8},{10,11... | collective-permute-start | bytes 2457608 | tf_op jit(solution)/shard_map/ppermute | solution.py:574
  78.4 12.6 %collective-permute-start.29 = (bf16[1600,128]{1,0:T(8,128)(2,1)S(1)}, bf16[1600,128]{1,0:T(8,128)(2,1)S(1)}, u32[]{:S(2)}, u32[]{:S(2)}) collective-permute-start(bf16[1600,128]{1,0:T(8,128)(2,1)S(1)} %bitcast.180), channel_id=1, source_target_pairs={{0,2},{1,3},{2,0},{3,1},{4,6},{5,7},{6,4},{7,5},{8,10},{9,11},{10,... | collective-permute-start | bytes 1228808 | tf_op jit(solution)/shard_map/ppermute | solution.py:574
  80.4 11.2 %collective-permute-start.30 = (bf16[1600,128]{1,0:T(8,128)(2,1)S(1)}, bf16[1600,128]{1,0:T(8,128)(2,1)S(1)}, u32[]{:S(2)}, u32[]{:S(2)}) collective-permute-start(bf16[1600,128]{1,0:T(8,128)(2,1)S(1)} %bitcast.181), channel_id=1, source_target_pairs={{0,4},{1,5},{2,6},{3,7},{4,0},{5,1},{6,2},{7,3},{8,12},{9,13},{10,... | collective-permute-start | bytes 1228808 | tf_op jit(solution)/shard_map/ppermute | solution.py:574
  137.7 15.3 %collective-permute-start.35 = (bf16[8,800,128]{2,1,0:T(8,128)(2,1)}, bf16[8,800,128]{2,1,0:T(8,128)(2,1)}, u32[]{:S(2)}, u32[]{:S(2)}) collective-permute-start(bf16[8,800,128]{2,1,0:T(8,128)(2,1)} %get-tuple-element.196), channel_id=1, source_target_pairs={{0,1},{1,0},{2,3},{3,2},{4,5},{5,4},{6,7},{7,6},{8,9},{9,8},{10,11... | collective-permute-start | bytes 4915208 | tf_op jit(solution)/shard_map/ppermute | solution.py:574
  152.9 18.4 %collective-permute-start.36 = (bf16[8,800,128]{2,1,0:T(8,128)(2,1)}, bf16[8,800,128]{2,1,0:T(8,128)(2,1)S(1)}, u32[]{:S(2)}, u32[]{:S(2)}) collective-permute-start(bf16[8,800,128]{2,1,0:T(8,128)(2,1)} %get-tuple-element.209), channel_id=1, source_target_pairs={{0,1},{1,0},{2,3},{3,2},{4,5},{5,4},{6,7},{7,6},{8,9},{9,8},{10,11... | collective-permute-start | bytes 4915208 | tf_op jit(solution)/shard_map/ppermute | solution.py:574
  154.4 16.9 %collective-permute-start.37 = (bf16[2,2,400,128]{3,2,1,0:T(8,128)(2,1)S(1)}, bf16[2,2,400,128]{3,2,1,0:T(8,128)(2,1)S(1)}, u32[]{:S(2)}, u32[]{:S(2)}) collective-permute-start(bf16[2,2,400,128]{3,2,1,0:T(8,128)(2,1)S(1)} %fusion.2), channel_id=1, source_target_pairs={{0,4},{1,5},{2,6},{3,7},{4,0},{5,1},{6,2},{7,3},{8,12},{9,13},{10,... | collective-permute-start | bytes 1228808 | tf_op jit(solution)/shard_map/ppermute | solution.py:574
  156.8 14.5 %collective-permute-start.38 = (bf16[2,2,400,128]{3,2,1,0:T(8,128)(2,1)S(1)}, bf16[2,2,400,128]{3,2,1,0:T(8,128)(2,1)S(1)}, u32[]{:S(2)}, u32[]{:S(2)}) collective-permute-start(bf16[2,2,400,128]{3,2,1,0:T(8,128)(2,1)S(1)} %fusion.3), channel_id=1, source_target_pairs={{0,2},{1,3},{2,0},{3,1},{4,6},{5,7},{6,4},{7,5},{8,10},{9,11},{10,... | collective-permute-start | bytes 1228808 | tf_op jit(solution)/shard_map/ppermute | solution.py:574
  171.3 22.9 %collective-permute-start.39 = (bf16[8,800,128]{2,1,0:T(8,128)(2,1)}, bf16[8,800,128]{2,1,0:T(8,128)(2,1)}, u32[]{:S(2)}, u32[]{:S(2)}) collective-permute-start(bf16[8,800,128]{2,1,0:T(8,128)(2,1)} %get-tuple-element.225), channel_id=1, source_target_pairs={{0,1},{1,0},{2,3},{3,2},{4,5},{5,4},{6,7},{7,6},{8,9},{9,8},{10,11... | collective-permute-start | bytes 4915208 | tf_op jit(solution)/shard_map/ppermute | solution.py:574
  174.3 19.3 %collective-permute-start.40 = (bf16[2,400,128]{2,1,0:T(8,128)(2,1)S(1)}, bf16[2,400,128]{2,1,0:T(8,128)(2,1)S(1)}, u32[]{:S(2)}, u32[]{:S(2)}) collective-permute-start(bf16[2,400,128]{2,1,0:T(8,128)(2,1)S(1)} %get-tuple-element.263), channel_id=1, source_target_pairs={{0,2},{1,3},{2,0},{3,1},{4,6},{5,7},{6,4},{7,5},{8,10},{9,11},{10,... | collective-permute-start | bytes 614408 | tf_op jit(solution)/shard_map/ppermute | solution.py:574
  175.3 18.3 %collective-permute-start.41 = (bf16[2,400,128]{2,1,0:T(8,128)(2,1)S(1)}, bf16[2,400,128]{2,1,0:T(8,128)(2,1)S(1)}, u32[]{:S(2)}, u32[]{:S(2)}) collective-permute-start(bf16[2,400,128]{2,1,0:T(8,128)(2,1)S(1)} %get-tuple-element.264), channel_id=1, source_target_pairs={{0,4},{1,5},{2,6},{3,7},{4,0},{5,1},{6,2},{7,3},{8,12},{9,13},{10,... | collective-permute-start | bytes 614408 | tf_op jit(solution)/shard_map/ppermute | solution.py:574
  176.2 17.4 %collective-permute-start.42 = (bf16[2,2,400,128]{3,2,1,0:T(8,128)(2,1)S(1)}, bf16[2,2,400,128]{3,2,1,0:T(8,128)(2,1)}, u32[]{:S(2)}, u32[]{:S(2)}) collective-permute-start(bf16[2,2,400,128]{3,2,1,0:T(8,128)(2,1)S(1)} %fusion.4), channel_id=1, source_target_pairs={{0,4},{1,5},{2,6},{3,7},{4,0},{5,1},{6,2},{7,3},{8,12},{9,13},{10,... | collective-permute-start | bytes 1228808 | tf_op jit(solution)/shard_map/ppermute | solution.py:574
  177.6 16.0 %collective-permute-start.43 = (bf16[2,2,400,128]{3,2,1,0:T(8,128)(2,1)S(1)}, bf16[2,2,400,128]{3,2,1,0:T(8,128)(2,1)}, u32[]{:S(2)}, u32[]{:S(2)}) collective-permute-start(bf16[2,2,400,128]{3,2,1,0:T(8,128)(2,1)S(1)} %fusion.5), channel_id=1, source_target_pairs={{0,2},{1,3},{2,0},{3,1},{4,6},{5,7},{6,4},{7,5},{8,10},{9,11},{10,... | collective-permute-start | bytes 1228808 | tf_op jit(solution)/shard_map/ppermute | solution.py:574
  194.3 9.5 %collective-permute-start.48 = (bf16[8,800,128]{2,1,0:T(8,128)(2,1)}, bf16[8,800,128]{2,1,0:T(8,128)(2,1)}, u32[]{:S(2)}, u32[]{:S(2)}) collective-permute-start(bf16[8,800,128]{2,1,0:T(8,128)(2,1)} %get-tuple-element.230), channel_id=1, source_target_pairs={{0,1},{1,0},{2,3},{3,2},{4,5},{5,4},{6,7},{7,6},{8,9},{9,8},{10,11... | collective-permute-start | bytes 4915208 | tf_op jit(solution)/shard_map/ppermute | solution.py:574
  195.7 11.2 %collective-permute-start.44 = (bf16[2,400,128]{2,1,0:T(8,128)(2,1)S(1)}, bf16[2,400,128]{2,1,0:T(8,128)(2,1)S(1)}, u32[]{:S(2)}, u32[]{:S(2)}) collective-permute-start(bf16[2,400,128]{2,1,0:T(8,128)(2,1)S(1)} %get-tuple-element.260), channel_id=1, source_target_pairs={{0,2},{1,3},{2,0},{3,1},{4,6},{5,7},{6,4},{7,5},{8,10},{9,11},{10,... | collective-permute-start | bytes 614408 | tf_op jit(solution)/shard_map/ppermute | solution.py:574
  196.7 11.3 %collective-permute-start.45 = (bf16[2,400,128]{2,1,0:T(8,128)(2,1)S(1)}, bf16[2,400,128]{2,1,0:T(8,128)(2,1)S(1)}, u32[]{:S(2)}, u32[]{:S(2)}) collective-permute-start(bf16[2,400,128]{2,1,0:T(8,128)(2,1)S(1)} %get-tuple-element.259), channel_id=1, source_target_pairs={{0,4},{1,5},{2,6},{3,7},{4,0},{5,1},{6,2},{7,3},{8,12},{9,13},{10,... | collective-permute-start | bytes 614408 | tf_op jit(solution)/shard_map/ppermute | solution.py:574
  198.7 14.7 %collective-permute-start.46 = (bf16[2,2,400,128]{3,2,1,0:T(8,128)(2,1)S(1)}, bf16[2,2,400,128]{3,2,1,0:T(8,128)(2,1)S(1)}, u32[]{:S(2)}, u32[]{:S(2)}) collective-permute-start(bf16[2,2,400,128]{3,2,1,0:T(8,128)(2,1)S(1)} %fusion.6), channel_id=1, source_target_pairs={{0,4},{1,5},{2,6},{3,7},{4,0},{5,1},{6,2},{7,3},{8,12},{9,13},{10,... | collective-permute-start | bytes 1228808 | tf_op jit(solution)/shard_map/ppermute | solution.py:574
  201.1 12.4 %collective-permute-start.47 = (bf16[2,2,400,128]{3,2,1,0:T(8,128)(2,1)S(1)}, bf16[2,2,400,128]{3,2,1,0:T(8,128)(2,1)S(1)}, u32[]{:S(2)}, u32[]{:S(2)}) collective-permute-start(bf16[2,2,400,128]{3,2,1,0:T(8,128)(2,1)S(1)} %fusion.7), channel_id=1, source_target_pairs={{0,2},{1,3},{2,0},{3,1},{4,6},{5,7},{6,4},{7,5},{8,10},{9,11},{10,... | collective-permute-start | bytes 1228808 | tf_op jit(solution)/shard_map/ppermute | solution.py:574
  204.9 17.3 %collective-permute-start.49 = (bf16[2,2,400,128]{3,2,1,0:T(8,128)(2,1)S(1)}, bf16[2,2,400,128]{3,2,1,0:T(8,128)(2,1)S(1)}, u32[]{:S(2)}, u32[]{:S(2)}) collective-permute-start(bf16[2,2,400,128]{3,2,1,0:T(8,128)(2,1)S(1)} %fusion.8), channel_id=1, source_target_pairs={{0,4},{1,5},{2,6},{3,7},{4,0},{5,1},{6,2},{7,3},{8,12},{9,13},{10,... | collective-permute-start | bytes 1228808 | tf_op jit(solution)/shard_map/ppermute | solution.py:574
  207.0 15.3 %collective-permute-start.50 = (bf16[2,2,400,128]{3,2,1,0:T(8,128)(2,1)S(1)}, bf16[2,2,400,128]{3,2,1,0:T(8,128)(2,1)S(1)}, u32[]{:S(2)}, u32[]{:S(2)}) collective-permute-start(bf16[2,2,400,128]{3,2,1,0:T(8,128)(2,1)S(1)} %fusion.9), channel_id=1, source_target_pairs={{0,2},{1,3},{2,0},{3,1},{4,6},{5,7},{6,4},{7,5},{8,10},{9,11},{10,... | collective-permute-start | bytes 1228808 | tf_op jit(solution)/shard_map/ppermute | solution.py:574
  214.8 11.1 %collective-permute-start.53 = (bf16[2,400,128]{2,1,0:T(8,128)(2,1)S(1)}, bf16[2,400,128]{2,1,0:T(8,128)(2,1)S(1)}, u32[]{:S(2)}, u32[]{:S(2)}) collective-permute-start(bf16[2,400,128]{2,1,0:T(8,128)(2,1)S(1)} %get-tuple-element.258), channel_id=1, source_target_pairs={{0,2},{1,3},{2,0},{3,1},{4,6},{5,7},{6,4},{7,5},{8,10},{9,11},{10,... | collective-permute-start | bytes 614408 | tf_op jit(solution)/shard_map/ppermute | solution.py:574
  215.9 11.0 %collective-permute-start.54 = (bf16[2,400,128]{2,1,0:T(8,128)(2,1)S(1)}, bf16[2,400,128]{2,1,0:T(8,128)(2,1)S(1)}, u32[]{:S(2)}, u32[]{:S(2)}) collective-permute-start(bf16[2,400,128]{2,1,0:T(8,128)(2,1)S(1)} %get-tuple-element.257), channel_id=1, source_target_pairs={{0,4},{1,5},{2,6},{3,7},{4,0},{5,1},{6,2},{7,3},{8,12},{9,13},{10,... | collective-permute-start | bytes 614408 | tf_op jit(solution)/shard_map/ppermute | solution.py:574
  218.3 16.2 %collective-permute-start.58 = (bf16[800,128]{1,0:T(8,128)(2,1)S(1)}, bf16[800,128]{1,0:T(8,128)(2,1)S(1)}, u32[]{:S(2)}, u32[]{:S(2)}) collective-permute-start(bf16[800,128]{1,0:T(8,128)(2,1)S(1)} %fusion.27), channel_id=1, source_target_pairs={{0,8},{1,9},{2,10},{3,11},{4,12},{5,13},{6,14},{7,15},{8,0},{9,1},... | collective-permute-start | bytes 614408 | tf_op jit(solution)/shard_map/ppermute | solution.py:574
  225.8 15.1 %collective-permute-start.59 = (bf16[800,128]{1,0:T(8,128)(2,1)S(1)}, bf16[800,128]{1,0:T(8,128)(2,1)S(1)}, u32[]{:S(2)}, u32[]{:S(2)}) collective-permute-start(bf16[800,128]{1,0:T(8,128)(2,1)S(1)} %get-tuple-element.266), channel_id=1, source_target_pairs={{0,16},{1,17},{2,18},{3,19},{4,20},{5,21},{6,22},{7,23},{8,24},{9,... | collective-permute-start | bytes 614408 | tf_op jit(solution)/shard_map/ppermute | solution.py:574
  226.9 27.2 %collective-permute-start.60 = (bf16[800,128]{1,0:T(8,128)(2,1)S(1)}, bf16[800,128]{1,0:T(8,128)(2,1)S(1)}, u32[]{:S(2)}, u32[]{:S(2)}) collective-permute-start(bf16[800,128]{1,0:T(8,128)(2,1)S(1)} %get-tuple-element.265), channel_id=1, source_target_pairs={{0,24},{1,25},{2,26},{3,27},{4,28},{5,29},{6,30},{7,31},{8,16},{9,... | collective-permute-start | bytes 614408 | tf_op jit(solution)/shard_map/ppermute | solution.py:574
  232.5 21.6 %collective-permute-start.55 = (bf16[800,128]{1,0:T(8,128)(2,1)S(1)}, bf16[800,128]{1,0:T(8,128)(2,1)S(1)}, u32[]{:S(2)}, u32[]{:S(2)}) collective-permute-start(bf16[800,128]{1,0:T(8,128)(2,1)S(1)} %fusion.26), channel_id=1, source_target_pairs={{0,8},{1,9},{2,10},{3,11},{4,12},{5,13},{6,14},{7,15},{8,0},{9,1},... | collective-permute-start | bytes 614408 | tf_op jit(solution)/shard_map/ppermute | solution.py:574
  233.7 22.7 %collective-permute-start.56 = (bf16[800,128]{1,0:T(8,128)(2,1)S(1)}, bf16[800,128]{1,0:T(8,128)(2,1)S(1)}, u32[]{:S(2)}, u32[]{:S(2)}) collective-permute-start(bf16[800,128]{1,0:T(8,128)(2,1)S(1)} %get-tuple-element.268), channel_id=1, source_target_pairs={{0,16},{1,17},{2,18},{3,19},{4,20},{5,21},{6,22},{7,23},{8,24},{9,... | collective-permute-start | bytes 614408 | tf_op jit(solution)/shard_map/ppermute | solution.py:574
  234.5 28.0 %collective-permute-start.57 = (bf16[800,128]{1,0:T(8,128)(2,1)S(1)}, bf16[800,128]{1,0:T(8,128)(2,1)S(1)}, u32[]{:S(2)}, u32[]{:S(2)}) collective-permute-start(bf16[800,128]{1,0:T(8,128)(2,1)S(1)} %get-tuple-element.267), channel_id=1, source_target_pairs={{0,24},{1,25},{2,26},{3,27},{4,28},{5,29},{6,30},{7,31},{8,16},{9,... | collective-permute-start | bytes 614408 | tf_op jit(solution)/shard_map/ppermute | solution.py:574
  (47 other events, 320.7 us)

commit v3 on v2

v3 whole, which is shorter than its diff:
```python
import functools
import math

import jax
import jax.numpy as jnp
from jax import lax
from jax.experimental import pallas as pl
from jax.experimental.pallas import tpu as pltpu
from jax.sharding import PartitionSpec as P

D = 512
HEADS = 8
FF = 2048
VOCAB = 27
TD = 128
HD = 64
LANES = 128
EPSILON = 1e-05
AXES = ("dp", "fsdp")
F32 = jnp.float32
BF16 = jnp.bfloat16
VMEM_BYTES = 52 * 2**20

ROW_GAIN_ONE, ROW_BIAS_ONE, ROW_W_TIME, ROW_B_TIME = 0, 4, 8, 520
ROW_QKV, ROW_OUT, ROW_GAIN_TWO, ROW_BIAS_TWO = 524, 6668, 8716, 8720
ROW_UP, ROW_B_UP, ROW_DOWN, ROW_B_DOWN, ROW_END = 8724, 16916, 16932, 25124, 25128
CHUNK_PAD = 832


def ceil_to(value, step):
    return -(-value // step) * step


class Geometry:
    def __init__(self, devices, shard, embed_shard):
        self.devices, self.shard, self.embed_shard = devices, shard, embed_shard
        self.param_rows = max(self.count(d, shard) for d in range(devices))
        self.embed_rows = max(self.count(d, embed_shard) for d in range(devices))
        self.embed_at = ceil_to(self.param_rows, 8)
        self.rows = ceil_to(max(self.embed_at + 8, self.param_rows + 2 * self.embed_rows), 16)

    @staticmethod
    def first(d, size):
        return d * size // LANES

    @staticmethod
    def count(d, size):
        return -(-(d + 1) * size // LANES) - d * size // LANES


def params(flops, nbytes, weight=0):
    flops, nbytes = max(flops * weight, 1000), max(nbytes * weight, 1000)
    return dict(
        compiler_params=pltpu.CompilerParams(vmem_limit_bytes=VMEM_BYTES),
        cost_estimate=pl.CostEstimate(flops=flops, bytes_accessed=nbytes, transcendentals=0),
    )


VM = pl.BlockSpec(memory_space=pltpu.VMEM)
SM = pl.BlockSpec(memory_space=pltpu.SMEM)
HBM = pl.BlockSpec(memory_space=pltpu.HBM)


def nn(left, right):
    return lax.dot_general(left, right, (((1,), (0,)), ((), ())), preferred_element_type=F32)


def nt(left, right):
    return lax.dot_general(left, right, (((1,), (1,)), ((), ())), preferred_element_type=F32)


def tn(left, right):
    return nn(left.T, right)


def shift_in(flat, offset):
    rolled = pltpu.roll(flat, offset, 1)
    above = jnp.concatenate([jnp.zeros((1, LANES), F32), rolled[:-1]], 0)
    lane = lax.broadcasted_iota(jnp.int32, flat.shape, 1)
    return jnp.where(lane >= offset, rolled, above)


def shift_out(flat, offset):
    rolled = pltpu.roll(flat, lax.rem(LANES - offset, LANES), 1)
    below = jnp.concatenate([rolled[1:], jnp.zeros((1, LANES), F32)], 0)
    lane = lax.broadcasted_iota(jnp.int32, flat.shape, 1)
    return jnp.where(lane < LANES - offset, rolled, below)


def pack_kernel(geo, place_ref, layers_ref, embed_ref, first_ref, second_ref):
    main = geo.embed_at
    for layer, out_ref in ((0, first_ref), (1, second_ref)):
        moved = shift_in(layers_ref[layer].astype(F32), place_ref[1])
        if layer == 0:
            tail = shift_in(embed_ref[...].astype(F32), place_ref[2])
            parts = [moved[:main], tail] + ([moved[main + 8 :]] if geo.rows > main + 8 else [])
            moved = jnp.concatenate(parts, 0)
        out_ref[...] = moved.astype(BF16)


def pack_shards(geo, place, layer_params, embed):
    layers = jnp.pad(layer_params, ((0, 0), (0, geo.rows * LANES - geo.shard)))
    table = jnp.pad(embed, (0, 8 * LANES - geo.embed_shard))
    out = jax.ShapeDtypeStruct((geo.rows, LANES), BF16)
    return pl.pallas_call(
        functools.partial(pack_kernel, geo),
        out_shape=(out, out),
        in_specs=[SM, VM, VM],
        out_specs=(VM, VM),
        **params(10**6, geo.rows * 1024),
    )(place, layers.reshape(2, geo.rows, LANES), table.reshape(8, LANES))


def finish_kernel(geo, fast, place_ref, *refs):
    grads_ref, embed_ref, moved = refs[-3:]
    parts = refs[:-3]
    count = 4 if fast else 1
    for layer in range(2):
        total = parts[layer * count][...].astype(F32)
        for part in parts[layer * count + 1 : (layer + 1) * count]:
            total = total + part[...].astype(F32)
        moved[pl.ds(layer * geo.rows, geo.rows), :] = shift_out(total, place_ref[1])
        if fast and layer == 0:
            first, size = geo.param_rows, geo.embed_rows
            lower, upper = total[first : first + size], total[first + size : first + 2 * size]
            tail = jnp.where(place_ref[3] >= 2, upper, lower)
            tail = jnp.concatenate([tail, jnp.zeros((8 - size, LANES), F32)], 0)
    if not fast:
        tail = parts[2][...]
    embed_ref[...] = shift_out(tail, place_ref[2])
    for r in range(ceil_to(geo.shard, LANES) // LANES):
        size = min(LANES, geo.shard - r * LANES)
        grads_ref[:, r * LANES : r * LANES + size] = moved[pl.ds(r, 2, stride=geo.rows), :][:, :size]


def finish(geo, fast, place, operands):
    grads, table = pl.pallas_call(
        functools.partial(finish_kernel, geo, fast),
        out_shape=(
            jax.ShapeDtypeStruct((2, geo.shard), F32),
            jax.ShapeDtypeStruct((8, LANES), F32),
        ),
        in_specs=[SM] + [VM] * len(operands),
        out_specs=(VM, VM),
        scratch_shapes=[pltpu.VMEM((2 * geo.rows, LANES), F32)],
        **params(10**6, geo.rows * 4096),
    )(place, *operands)
    return grads, table.reshape(-1)[: geo.embed_shard]


class Staged:
    def __init__(self, sources, targets, held, sems):
        self.held, self.pending, self.sent = held, {}, []
        self.targets, self.sems = targets, sems
        self.used = len(sources)
        for i, name in enumerate(sources):
            self.pending[name] = pltpu.make_async_copy(sources[name], held[name], sems.at[i])
            self.pending[name].start()

    def get(self, *names):
        for name in names:
            if name in self.pending:
                self.pending.pop(name).wait()
        found = [self.held[name] for name in names]
        return found[0] if len(found) == 1 else found

    def put(self, *names):
        for name in names:
            copy = pltpu.make_async_copy(self.held[name], self.targets[name], self.sems.at[self.used])
            copy.start()
            self.used += 1
            self.sent.append(copy)

    def close(self):
        for copy in list(self.pending.values()) + self.sent:
            copy.wait()


def staged_call(kernel, place, operands, results, scratch, flops, raw=(), semaphores=0, unheld=()):
    names, outs, temps = list(operands), list(results), list(scratch)

    held_outs = [name for name in outs if name not in unheld]

    def whole(place_ref, *refs):
        raws, refs = refs[: len(raw)], refs[len(raw) :]
        sources, refs = dict(zip(names, refs)), refs[len(names) :]
        targets, refs = dict(zip(outs, refs)), refs[len(outs) :]
        held, refs = dict(zip(names + held_outs, refs)), refs[len(names) + len(held_outs) :]
        extra, refs = dict(zip(temps, refs)), refs[len(temps) :]
        staged = Staged(sources, targets, held, refs[0])
        kernel(place_ref, raws, staged, extra, refs[-1])
        staged.close()

    buffers = [pltpu.VMEM(v.shape, v.dtype) for v in (*operands.values(), *(results[name] for name in held_outs))]
    sems = [pltpu.SemaphoreType.DMA((len(names) + len(outs),))]
    if semaphores:
        sems.append(pltpu.SemaphoreType.DMA((semaphores,)))
    found = pl.pallas_call(
        whole,
        out_shape=tuple(results.values()),
        in_specs=[SM] + [HBM] * (len(raw) + len(names)),
        out_specs=(HBM,) * len(outs),
        scratch_shapes=buffers + list(scratch.values()) + sems,
        **params(flops, 2 * 10**7, 1),
    )(place, *raw, *operands.values())
    return dict(zip(outs, found))


def like(dtype, *shape):
    return jax.ShapeDtypeStruct(shape, dtype)


def unpack(geo, layer, plan, me, chunk_refs, held, flat, flat_table, out, sems):
    copies = []
    for source, pieces in zip(chunk_refs, plan):
        for src_at, relative, absolute, dst_at, count in pieces:
            if absolute is None:
                target = held.at[lax.bitwise_xor(me, relative), pl.ds(dst_at, count)]
                origin = source.at[pl.ds(src_at, count)]
            else:
                target, origin = held, source
            copies.append(pltpu.make_async_copy(origin, target, sems.at[len(copies)]))
    for copy in copies:
        copy.start()
    for copy in copies:
        copy.wait()
    for d in range(geo.devices):
        block = held[d].astype(F32)
        start, rows = geo.first(d, geo.shard), geo.count(d, geo.shard)
        split = (d * geo.shard) % LANES != 0
        if split:
            shared = flat[pl.ds(start, 1), :] + block[:1]
        flat[pl.ds(start, rows), :] = block[:rows]
        if split:
            flat[pl.ds(start, 1), :] = shared
        if layer == 0:
            tail = block[geo.embed_at : geo.embed_at + 8]
            start, rows = geo.first(d, geo.embed_shard), geo.count(d, geo.embed_shard)
            split = (d * geo.embed_shard) % LANES != 0
            if split:
                shared = flat_table[pl.ds(start, 1), :] + tail[:1]
            flat_table[pl.ds(start, rows), :] = tail[:rows]
            if split:
                flat_table[pl.ds(start, 1), :] = shared
    vectors = out["vectors"]
    for row, start, width in (
        (0, ROW_GAIN_ONE, 4),
        (1, ROW_BIAS_ONE, 4),
        (2, ROW_B_TIME, 4),
        (3, ROW_GAIN_TWO, 4),
        (4, ROW_BIAS_TWO, 4),
        (5, ROW_B_DOWN, 4),
        (6, ROW_B_UP, 16),
    ):
        for c in range(width):
            vectors[row : row + 1, c * LANES : (c + 1) * LANES] = flat[pl.ds(start + c, 1), :]
    for name, start, rows, width in (
        ("w_time", ROW_W_TIME, TD, 4),
        ("w_qkv", ROW_QKV, D, 12),
        ("w_out", ROW_OUT, D, 4),
        ("w_up", ROW_UP, D, 16),
        ("w_down", ROW_DOWN, FF, 4),
    ):
        for c in range(width):
            out[name][:, c * LANES : (c + 1) * LANES] = flat[pl.ds(start + c, rows, stride=width), :].astype(BF16)
    if layer == 0:
        table = out["table"]
        table[...] = jnp.zeros(table.shape, BF16)
        for c in range(4):
            table[0:VOCAB, c * LANES : (c + 1) * LANES] = flat_table[pl.ds(c, VOCAB, stride=4), :].astype(BF16)


WEIGHTS = {
    "w_qkv": like(BF16, D, 3 * D),
    "w_out": like(BF16, D, D),
    "w_up": like(BF16, D, FF),
    "w_down": like(BF16, FF, D),
    "vectors": like(F32, 8, FF),
}


def unpack_scratch(geo, layer):
    scratch = {
        "chunks": pltpu.VMEM((geo.devices, geo.rows, LANES), BF16),
        "flat": pltpu.VMEM((ROW_END + CHUNK_PAD, LANES), F32),
        "flat_table": pltpu.VMEM((4 * 32, LANES), F32),
        "w_time": pltpu.VMEM((TD, D), BF16),
    }
    if layer == 0:
        scratch["table"] = pltpu.VMEM((32, D), BF16)
    return scratch


def split_gathered(gathered):
    plan = tuple(tuple(pieces) for array, pieces in gathered)
    return [array for array, pieces in gathered], plan, sum(len(pieces) for pieces in plan)


def norm_stats(values):
    mean = jnp.mean(values, -1, keepdims=True)
    centered = values - mean
    variance = jnp.mean(centered * centered, -1, keepdims=True)
    scale = lax.rsqrt(variance + EPSILON)
    return centered * scale, scale


ROW_BLOCK = 64


def norm_ahead(values, gain, bias, out):
    for r in range(0, values.shape[0], ROW_BLOCK):
        rows = slice(r, r + ROW_BLOCK)
        unit, _ = norm_stats(values[rows, :])
        out[rows, :] = (unit * gain + bias).astype(BF16)


def norm_back(grad, values, gain, passed, out):
    grad_gain, grad_bias = jnp.zeros((8, D), F32), jnp.zeros((8, D), F32)
    for r in range(0, values.shape[0], ROW_BLOCK):
        rows = slice(r, r + ROW_BLOCK)
        unit, scale = norm_stats(values[rows, :])
        block = grad[rows, :]
        grad_gain = grad_gain + jnp.sum((block * unit).reshape(-1, 8, D), 0)
        grad_bias = grad_bias + jnp.sum(block.reshape(-1, 8, D), 0)
        inner = block * gain
        shifted = inner - jnp.mean(inner, -1, keepdims=True)
        back = scale * (shifted - unit * jnp.mean(inner * unit, -1, keepdims=True))
        out[rows, :] = passed[rows, :].astype(F32) + back
    return jnp.sum(grad_gain, 0, keepdims=True), jnp.sum(grad_bias, 0, keepdims=True)


def gelu_both(u):
    root = math.sqrt(2.0 / math.pi)
    square = u * u
    t = jnp.tanh(root * (u + 0.044715 * (square * u)))
    half = 0.5 * (1.0 + t)
    slope = half + 0.5 * u * (1.0 - t * t) * (root * (1.0 + 3.0 * 0.044715 * square))
    return u * half, slope


def head_masks(shape, scale):
    lane = lax.broadcasted_iota(jnp.int32, shape, 1)
    one = jnp.where(lane < HD, scale, 0.0).astype(BF16)
    two = jnp.where(lane < HD, 0.0, scale).astype(BF16)
    return one, two


def ahead_attn(seqs, stream, emb, w_time, w_qkv, w_out, vectors, x, a, qkv, prob, o, x2, a2, done):
    tokens = x.shape[0]
    length = tokens // seqs
    time_vec = nn(emb[...], w_time[...]) + vectors[2:3, :D]
    for s in range(seqs):
        x[s * length : (s + 1) * length, :] = stream[s * length : (s + 1) * length] + time_vec[s : s + 1]
    done("x")
    norm_ahead(x, vectors[0:1, :D], vectors[1:2, :D], a)
    done("a")
    for c in range(3):
        part = slice(c * D, (c + 1) * D)
        qkv[:, part] = nn(a[...], w_qkv[:, part]).astype(BF16)
    done("qkv")
    masks = head_masks((length, LANES), 1.0 / math.sqrt(HD))
    for s in range(seqs):
        rows = slice(s * length, (s + 1) * length)
        for pair in range(HEADS // 2):
            cols = [slice(c * D + pair * LANES, c * D + (pair + 1) * LANES) for c in range(3)]
            q, k, v_t = qkv[rows, cols[0]], qkv[rows, cols[1]], qkv[rows, cols[2]].T
            mixed = []
            for h in range(2):
                scores = nt(k * masks[h], q)
                top = jnp.max(scores, 0, keepdims=True)
                expd = jnp.exp(scores - top)
                low = (expd * (1.0 / jnp.sum(expd, 0, keepdims=True))).astype(BF16)
                prob[s * HEADS + 2 * pair + h] = low
                mixed.append(nn(v_t[h * HD : (h + 1) * HD], low))
            o[rows, cols[0]] = jnp.concatenate(mixed, 0).T.astype(BF16)
    done("prob")
    done("o")
    x2[...] = x[...] + nn(o[...], w_out[...])
    done("x2")
    norm_ahead(x2, vectors[3:4, :D], vectors[4:5, :D], a2)
    done("a2")


def ahead_mlp(x2, a2, w_up, w_down, vectors, gl, slope):
    parts = [slice(c * D, (c + 1) * D) for c in range(FF // D)]

    def up(part):
        return nn(a2()[...], w_up()[:, part])

    total, u = None, up(parts[0])
    for c, part in enumerate(parts):
        value, rate = gelu_both(u + vectors()[6:7, part])
        low = value.astype(BF16)
        gl[:, part] = low
        slope[:, part] = rate.astype(BF16)
        if c + 1 < len(parts):
            u = up(parts[c + 1])
        step = nn(low, w_down()[part, :])
        total = step if total is None else total + step
    return x2()[...] + vectors()[5:6, :D] + total


class Chunks:
    def __init__(self, geo, fast, me, held, targets, sems):
        self.geo, self.fast, self.me, self.held, self.targets, self.sems = geo, fast, me, held, targets, sems
        self.copies = []

    def cut(self, d, flat, base, table=None):
        geo, slot = self.geo, d % (self.geo.devices // 2)
        block = flat[pl.ds(geo.first(d, geo.shard) - base, geo.rows), :]
        if table is not None:
            first, size = geo.param_rows, geo.embed_rows
            tails = [
                table[pl.ds(geo.first(e, geo.embed_shard), size), :] for e in (d, d + geo.devices // 2)
            ]
            block = jnp.concatenate([block[:first], *tails, block[first + 2 * size :]], 0)
        self.held[slot] = block.astype(BF16)
        source, sem = self.held.at[slot], self.sems.at[slot]
        if not self.fast:
            self.copies.append(pltpu.make_async_copy(source, self.targets[0].at[slot], sem))
            self.copies[-1].start()
            return
        relative = lax.bitwise_xor(self.me, d)
        row = lax.bitwise_and(relative, 4) + lax.bitwise_and(relative, 2)
        row = row + lax.bitwise_and(lax.shift_right_logical(relative, 3), 1)
        keep, send = (pltpu.make_async_copy(source, target.at[row], sem) for target in self.targets)
        core = lax.bitwise_and(relative, 1)

        @pl.when(core == 0)
        def _():
            keep.start()

        @pl.when(core == 1)
        def _():
            send.start()

        self.copies.append(keep)

    def close(self):
        for copy in self.copies:
            copy.wait()


def back_mlp(geo, chunks, grad_in, x2, a2, gl, slope, w_up, w_down, vectors, grad, rest, flat, base, normed, done):
    grad_low = grad_in()[...].astype(BF16)
    flat[pl.ds(ROW_END - base, CHUNK_PAD), :] = jnp.zeros((CHUNK_PAD, LANES), F32)
    grad_bias = jnp.sum(grad_low.astype(F32), 0, keepdims=True)
    for c in range(4):
        flat[pl.ds(ROW_B_DOWN - base + c, 1), :] = grad_bias[:, c * LANES : (c + 1) * LANES]
    parts = [slice(j * D, (j + 1) * D) for j in range(FF // D)]

    def hidden_grad(part):
        return nt(grad_low, w_down()[part, :])

    total, hidden = None, hidden_grad(parts[0])
    for j, part in enumerate(parts):
        up_grad = (hidden * slope()[:, part].astype(F32)).astype(BF16)
        bias_grad = jnp.sum(up_grad.astype(F32), 0, keepdims=True)
        if j + 1 < len(parts):
            hidden = hidden_grad(parts[j + 1])
        down = tn(gl()[:, part], grad_low)
        for c in range(4):
            cols = slice(c * LANES, (c + 1) * LANES)
            flat[pl.ds(ROW_B_UP - base + 4 * j + c, 1), :] = bias_grad[:, cols]
            flat[pl.ds(ROW_DOWN - base + 4 * D * j + c, D, stride=4), :] = down[:, cols]
        up = tn(a2()[...], up_grad)
        for c in range(4):
            cols = slice(c * LANES, (c + 1) * LANES)
            flat[pl.ds(ROW_UP - base + 4 * j + c, D, stride=16), :] = up[:, cols]
        step = nt(up_grad, w_up()[:, part])
        total = step if total is None else total + step
    normed[...] = total
    for d in range(geo.devices // 2, geo.devices):
        chunks.cut(d, flat, base)
    grad_gain, grad_bias = norm_back(normed, x2(), vectors()[3:4, :D], grad_in(), grad)
    done("grad")
    for c in range(4):
        cols = slice(c * LANES, (c + 1) * LANES)
        flat[pl.ds(ROW_GAIN_TWO - base + c, 1), :] = grad_gain[:, cols]
        flat[pl.ds(ROW_BIAS_TWO - base + c, 1), :] = grad_bias[:, cols]
    rest[...] = flat[pl.ds(ROW_GAIN_TWO - base, rest.shape[0]), :].astype(BF16)
    done("rest")


def back_attn(
    geo, seqs, chunks, table, embed_outs, grad_in, x, a, qkv, prob, o, w_qkv, w_out, vectors, emb_t, rest, total,
    flat, qkv_grad, heads_grad, normed, chars, done,
):
    tokens = normed.shape[0]
    length = tokens // seqs
    grad_low = grad_in()[...].astype(BF16)
    heads_grad[...] = nt(grad_low, w_out()[...]).astype(BF16)
    out_grad = tn(o()[...], grad_low)
    for c in range(4):
        flat[pl.ds(ROW_OUT + c, D, stride=4), :] = out_grad[:, c * LANES : (c + 1) * LANES]
    masks = head_masks((length, LANES), 1.0)
    scale = 1.0 / math.sqrt(HD)
    lane = lax.broadcasted_iota(jnp.int32, (length, LANES), 1)
    qkv, prob = qkv(), prob()
    for s in range(seqs):
        rows = slice(s * length, (s + 1) * length)
        for pair in range(HEADS // 2):
            cols = [slice(c * D + pair * LANES, c * D + (pair + 1) * LANES) for c in range(3)]
            q, k, v = qkv[rows, cols[0]], qkv[rows, cols[1]], qkv[rows, cols[2]]
            go = heads_grad[rows, cols[0]]
            k_t = k.T
            to_q, to_k, to_v = [], [], []
            for h in range(2):
                prob_low = prob[s * HEADS + 2 * pair + h]
                prob_full = prob_low.astype(F32)
                prob_grad = nt(v * masks[h], go)
                weighted = prob_full * prob_grad
                row_dot = jnp.sum(weighted, 0, keepdims=True)
                score_grad = (weighted - prob_full * row_dot).astype(BF16)
                to_q.append(nn(k_t[h * HD : (h + 1) * HD], score_grad))
                to_k.append(nn(score_grad, q))
                to_v.append(nn(prob_low, go))
            qkv_grad[rows, cols[0]] = (jnp.concatenate(to_q, 0).T * scale).astype(BF16)
            qkv_grad[rows, cols[1]] = (jnp.where(lane < HD, to_k[0], to_k[1]) * scale).astype(BF16)
            qkv_grad[rows, cols[2]] = jnp.where(lane < HD, to_v[0], to_v[1]).astype(BF16)
    a_t, steps = a()[...].T, None
    for part in range(3):
        cols = slice(part * D, (part + 1) * D)
        piece = nn(a_t, qkv_grad[:, cols])
        for c in range(4):
            flat[pl.ds(ROW_QKV + 4 * part + c, D, stride=12), :] = piece[:, c * LANES : (c + 1) * LANES]
        step = nt(qkv_grad[:, cols], w_qkv()[:, cols])
        steps = step if steps is None else steps + step
    normed[...] = steps
    flat[pl.ds(ROW_GAIN_TWO, rest().shape[0]), :] = rest()[...].astype(F32)
    middle = geo.devices // 2
    early = [d for d in range(middle) if geo.first(d, geo.shard) >= ROW_QKV] if table is None else []
    for d in early:
        chunks.cut(d, flat, 0)
    grad_gain, grad_bias = norm_back(normed, x(), vectors()[0:1, :D], grad_in(), total)
    done("grad")
    time_grad = [
        jnp.sum(total[s * length : (s + 1) * length, :], 0, keepdims=True).astype(BF16).astype(F32) for s in range(seqs)
    ]
    bias_grad = sum(time_grad[1:], time_grad[0])
    weight_grad = sum(emb_t()[:, s : s + 1] * time_grad[s] for s in range(seqs))
    for c in range(4):
        cols = slice(c * LANES, (c + 1) * LANES)
        flat[pl.ds(ROW_GAIN_ONE + c, 1), :] = grad_gain[:, cols]
        flat[pl.ds(ROW_BIAS_ONE + c, 1), :] = grad_bias[:, cols]
        flat[pl.ds(ROW_B_TIME + c, 1), :] = bias_grad[:, cols]
        flat[pl.ds(ROW_W_TIME + c, TD, stride=4), :] = weight_grad[:, cols]
    if table is not None:
        kind = lax.broadcasted_iota(jnp.int32, (32, tokens), 0)
        table_grad = nn((chars()[...] == kind).astype(BF16), total[...].astype(BF16))
        for c in range(4):
            table[pl.ds(c, 32, stride=4), :] = table_grad[:, c * LANES : (c + 1) * LANES]
    for d in range(middle):
        if d not in early:
            chunks.cut(d, flat, 0, table if chunks.fast else None)
    if table is not None and not chunks.fast:
        for d in range(geo.devices):
            embed_outs[d] = table[pl.ds(geo.first(d, geo.embed_shard), 8), :]


def kept_shapes(seqs, tokens):
    length = tokens // seqs
    return {
        "x": like(F32, tokens, D),
        "a": like(BF16, tokens, D),
        "qkv": like(BF16, tokens, 3 * D),
        "prob": like(BF16, seqs * HEADS, length, length),
        "o": like(BF16, tokens, D),
    }


def rest_rows(geo):
    middle = geo.first(geo.devices // 2, geo.shard)
    return ceil_to(middle + geo.rows - ROW_GAIN_TWO, 16)


def chunk_results(geo, fast):
    if fast:
        shape = like(BF16, geo.devices // 4, geo.rows, LANES)
        return {"keep": shape, "send": shape}
    return {"keep": like(BF16, geo.devices // 2, geo.rows, LANES)}


def chunk_targets(staged, fast):
    return [staged.targets[name] for name in (("keep", "send") if fast else ("keep",))]


def chunk_scratch(geo, tokens):
    return {
        "cuts": pltpu.VMEM((geo.devices // 2, geo.rows, LANES), BF16),
        "cut_sems": pltpu.SemaphoreType.DMA((geo.devices // 2,)),
        "normed": pltpu.VMEM((tokens, D), F32),
    }


def first_ahead(geo, seqs, place, gathered, chars, emb):
    tokens = chars.shape[0]
    arrays, plan, count = split_gathered(gathered)
    results = WEIGHTS | kept_shapes(seqs, tokens) | {"x2": like(F32, tokens, D), "a2": like(BF16, tokens, D)}

    def kernel(place_ref, chunk_refs, staged, extra, sems):
        held = staged.held
        unpack(
            geo, 0, plan, place_ref[0], chunk_refs, extra["chunks"], extra["flat"], extra["flat_table"], held | extra, sems
        )
        staged.put(*WEIGHTS)
        lane = lax.broadcasted_iota(jnp.int32, (tokens, 32), 1)
        stream = nn((staged.get("chars")[...] == lane).astype(BF16), extra["table"][...])
        weights = [extra["w_time"]] + [held[name] for name in ("w_qkv", "w_out", "vectors")]
        outs = [held[name] for name in ("x", "a", "qkv", "prob", "o", "x2", "a2")]
        ahead_attn(seqs, stream, staged.get("emb"), *weights, *outs, staged.put)

    operands = {"chars": chars, "emb": emb}
    scratch = unpack_scratch(geo, 0)
    return staged_call(kernel, place, operands, results, scratch, 4 * 10**9, arrays, count)


def first_ahead_rest(place, found):
    names = ("a2", "w_up", "vectors", "w_down", "x2")
    operands = {name: found[name] for name in names}
    tokens = found["x2"].shape[0]
    results = {"stream": like(F32, tokens, D), "gl": like(BF16, tokens, FF), "slope": like(BF16, tokens, FF)}

    def kernel(place_ref, _, staged, extra, sems):
        late = [functools.partial(staged.get, name) for name in ("x2", "a2", "w_up", "w_down", "vectors")]
        gl, slope, stream = (staged.held[name] for name in ("gl", "slope", "stream"))
        stream[...] = ahead_mlp(*late, gl, slope)
        staged.put("gl", "slope", "stream")

    return found | staged_call(kernel, place, operands, results, {}, 4 * 10**9)


def second_both(geo, fast, seqs, place, gathered, stream, emb, cotangent):
    tokens = stream.shape[0]
    arrays, plan, count = split_gathered(gathered)
    results = {name: WEIGHTS[name] for name in ("w_qkv", "w_out", "vectors")}
    results = results | kept_shapes(seqs, tokens)
    results = results | {
        "output": like(BF16, tokens, D),
        "grad": like(F32, tokens, D),
        "rest": like(BF16, rest_rows(geo), LANES),
    }
    results = results | chunk_results(geo, fast)
    scratch = unpack_scratch(geo, 1)
    scratch["w_up"], scratch["w_down"] = pltpu.VMEM((D, FF), BF16), pltpu.VMEM((FF, D), BF16)
    scratch["x2"], scratch["a2"] = pltpu.VMEM((tokens, D), F32), pltpu.VMEM((tokens, D), BF16)
    scratch["gl"], scratch["slope"] = pltpu.VMEM((tokens, FF), BF16), pltpu.VMEM((tokens, FF), BF16)
    scratch = scratch | chunk_scratch(geo, tokens)

    def kernel(place_ref, chunk_arrays, staged, extra, sems):
        every = staged.held | extra
        unpack(geo, 1, plan, place_ref[0], chunk_arrays, extra["chunks"], extra["flat"], extra["flat_table"], every, sems)
        staged.put("w_qkv", "w_out", "vectors")
        weights = [every[name] for name in ("w_time", "w_qkv", "w_out", "vectors")]
        outs = [every[name] for name in ("x", "a", "qkv", "prob", "o", "x2", "a2")]

        def done(name):
            if name in results:
                staged.put(name)

        ahead_attn(seqs, staged.get("stream")[...], staged.get("emb"), *weights, *outs, done)

        def ready(*names):
            return [functools.partial(every.get, name) for name in names]

        outputs = ahead_mlp(*ready("x2", "a2", "w_up", "w_down", "vectors"), every["gl"], every["slope"])
        every["output"][...] = outputs.astype(BF16)
        done("output")
        chunks = Chunks(geo, fast, place_ref[0], extra["cuts"], chunk_targets(staged, fast), extra["cut_sems"])
        back_mlp(
            geo, chunks, functools.partial(staged.get, "cotangent"),
            *ready("x2", "a2", "gl", "slope", "w_up", "w_down", "vectors"),
            every["grad"], every["rest"], extra["flat"], 0, extra["normed"], done,
        )
        chunks.close()

    operands = {"stream": stream, "emb": emb, "cotangent": cotangent}
    return staged_call(kernel, place, operands, results, scratch, 10**10, arrays, count, ("keep", "send"))


def first_back_mlp(geo, fast, place, grad, found):
    names = ("grad_in", "w_down", "slope", "gl", "a2", "w_up", "x2", "vectors")
    operands = {name: grad if name == "grad_in" else found[name] for name in names}
    tokens = grad.shape[0]
    results = {"grad": like(F32, tokens, D), "rest": like(BF16, rest_rows(geo), LANES)} | chunk_results(geo, fast)
    base = ROW_GAIN_TWO

    def kernel(place_ref, _, staged, extra, sems):
        late = [
            functools.partial(staged.get, name)
            for name in ("grad_in", "x2", "a2", "gl", "slope", "w_up", "w_down", "vectors")
        ]
        chunks = Chunks(geo, fast, place_ref[0], extra["cuts"], chunk_targets(staged, fast), extra["cut_sems"])
        back_mlp(
            geo, chunks, *late, staged.held["grad"], staged.held["rest"], extra["flat"], base, extra["normed"], staged.put
        )
        chunks.close()

    scratch = {"flat": pltpu.VMEM((ROW_END - base + CHUNK_PAD, LANES), F32)} | chunk_scratch(geo, tokens)
    return staged_call(kernel, place, operands, results, scratch, 6 * 10**9, unheld=("keep", "send"))


def both_back_attn(geo, fast, layer, seqs, place, grad, found, emb_t, rest, chars_row):
    names = ("grad_in", "w_out", "o", "qkv", "prob", "a", "w_qkv", "x", "vectors", "emb_t", "rest")
    given = {"grad_in": grad, "emb_t": emb_t, "rest": rest}
    operands = {name: given[name] if name in given else found[name] for name in names}
    tokens = grad.shape[0]
    results = {} if layer == 0 else {"grad": like(F32, tokens, D)}
    results = results | chunk_results(geo, fast)
    scratch = {
        "flat": pltpu.VMEM((ROW_GAIN_TWO + rest.shape[0], LANES), F32),
        "qkv_grad": pltpu.VMEM((tokens, 3 * D), BF16),
        "heads_grad": pltpu.VMEM((tokens, D), BF16),
    } | chunk_scratch(geo, tokens)
    if layer == 0:
        scratch["total"] = pltpu.VMEM((tokens, D), F32)
        operands["chars"] = chars_row
        scratch["table"] = pltpu.VMEM((4 * 32, LANES), F32)
        if not fast:
            results["table_out"] = like(F32, geo.devices, 8, LANES)

    def kernel(place_ref, _, staged, extra, sems):
        late = [functools.partial(staged.get, name) for name in ("grad_in", "x", "a", "qkv", "prob", "o", "w_qkv", "w_out")]
        tail = [functools.partial(staged.get, name) for name in ("vectors", "emb_t", "rest")]
        chunks = Chunks(geo, fast, place_ref[0], extra["cuts"], chunk_targets(staged, fast), extra["cut_sems"])

        def done(name):
            if name in results:
                staged.put(name)

        back_attn(
            geo, seqs, chunks, extra.get("table"), staged.held.get("table_out"), *late, *tail,
            extra["total"] if layer == 0 else staged.held["grad"], extra["flat"], extra["qkv_grad"], extra["heads_grad"],
            extra["normed"], functools.partial(staged.get, "chars"), done,
        )
        done("table_out")
        chunks.close()

    return staged_call(kernel, place, operands, results, scratch, 6 * 10**9, unheld=("keep", "send"))


def permute(value, distance, devices):
    return lax.ppermute(value, AXES, [(d, d ^ distance) for d in range(devices)])


Z1, Z2, Z3, X, Y, CORE = 8, 16, 24, 4, 2, 1


def after(value, *others):
    return lax.optimization_barrier((value, *others))[0]


def sync(*values):
    return lax.optimization_barrier(values)


def gather_both(geo, first, second):
    n, rows = geo.devices, geo.rows
    half = ceil_to(rows // 2, 16)

    def sides(held):
        return permute(held, X, n), permute(held, Y, n)

    def corners(over_x, over_y):
        return permute(over_x[:half], Y, n), permute(over_y[half:], X, n)

    def other(*arrays):
        return permute(jnp.concatenate(arrays, 0), CORE, n)

    near, over = permute(first, Z1, n), permute(first, Z2, n)
    sides_0 = sides(first)
    sides_0 = sync(*sides_0)
    corners_0 = corners(*sides_0)
    near, _ = sync(near, sides_0[0])
    sides_1 = sides(near)
    over, _ = sync(over, near)
    far = permute(over, Z1, n)
    sides_2 = sides(over)
    *sides_1, _ = sync(*sides_1, over)
    corners_1 = corners(*sides_1)
    far, *corners_0 = sync(far, *corners_0, sides_1[0])[:3]
    sides_3 = sides(far)
    other_0 = other(first, *sides_0, *corners_0)
    second, _ = sync(second, far)
    near_b, over_b = permute(second, Z1, n), permute(second, Z2, n)
    *sides_2, _ = sync(*sides_2, far)
    corners_2 = corners(*sides_2)
    *corners_1, _ = sync(*corners_1, sides_2[0])
    other_1 = other(near, *sides_1, *corners_1)
    *sides_3, _ = sync(*sides_3, sides_2[0])
    corners_3 = corners(*sides_3)
    over_b, near_b, _ = sync(over_b, near_b, sides_3[0])
    far_b = permute(over_b, Z1, n)
    *corners_2, _ = sync(*corners_2, sides_3[0])
    other_2 = other(over, *sides_2, *corners_2)
    *corners_3, far_b, _ = sync(*corners_3, far_b, corners_2[0])
    other_3 = other(far, *sides_3, *corners_3)
    column = jnp.concatenate([second, near_b, over_b, far_b], 0)
    found = []
    for z, arrays, packed in (
        (0, (first, *sides_0, *corners_0), other_0),
        (Z1, (near, *sides_1, *corners_1), other_1),
        (Z2, (over, *sides_2, *corners_2), other_2),
        (Z3, (far, *sides_3, *corners_3), other_3),
    ):
        pieces = [
            (0, z, None, 0, rows),
            (rows, z + X, None, 0, rows),
            (2 * rows, z + Y, None, 0, rows),
            (3 * rows, z + X + Y, None, 0, half),
            (3 * rows + half, z + X + Y, None, half, rows - half),
        ]
        for array, (_, relative, _, at, count) in zip(arrays, pieces):
            found.append((array, [(0, relative, None, at, count)]))
        found.append((packed, [(src, rel + CORE, None, at, count) for src, rel, _, at, count in pieces]))
    return found, column


def gather_sides(geo, column):
    return permute(column, X, geo.devices), permute(column, Y, geo.devices)


def gather_corners(geo, over_x, over_y):
    n, rows = geo.devices, geo.rows
    half = ceil_to(rows // 2, 16)
    cut_x = over_x.reshape(4, rows, LANES)[:, :half].reshape(-1, LANES)
    cut_y = over_y.reshape(4, rows, LANES)[:, half:].reshape(-1, LANES)
    return permute(cut_x, Y, n), permute(cut_y, X, n)


def gathered_pieces(geo, arrays, others):
    rows = geo.rows
    half = ceil_to(rows // 2, 16)
    found = []
    for core, group in ((0, arrays), (CORE, others)):
        for array, (relative, at, count) in zip(
            group, ((0, 0, rows), (X, 0, rows), (Y, 0, rows), (X + Y, 0, half), (X + Y, half, rows - half))
        ):
            found.append((array, [(z * count, relative + core + 8 * z, None, at, count) for z in range(4)]))
    return found


def gather_any(geo, chunk):
    gathered = lax.all_gather(chunk, AXES, axis=0)
    return [(gathered, [(0, 0, 0, 0, 0)])]


def add(*values):
    total = values[0].astype(F32)
    for value in values[1:]:
        total = total + value.astype(F32)
    return total


def plane_start(geo, keep, came):
    shape = (2, 2, 2, geo.rows, LANES)
    half = ceil_to(geo.rows // 2, 16)
    keep, came = keep.reshape(shape), came.reshape(shape)
    one = (keep[:, :, :, :half], came[:, :, :, :half])
    two = (keep[:, :, :, half:], came[:, :, :, half:])
    to_x = add(*(part[1] for part in one)).astype(BF16)
    to_y = add(*(part[:, 1] for part in two)).astype(BF16)
    return [part[0] for part in one], [part[:, 0] for part in two], to_x, to_y


def plane_next(one, two, from_x, from_y):
    one, two = one + [from_x], two + [from_y]
    to_y = add(*(part[1] for part in one)).astype(BF16)
    to_x = add(*(part[1] for part in two)).astype(BF16)
    return [part[0] for part in one], [part[0] for part in two], to_y, to_x


def plane_end(one, two, from_y, from_x):
    return jnp.concatenate([add(*one, from_y), add(*two, from_x)], 1)


def column_sum(geo, place, upper, lower, table):
    n = geo.devices
    if table:
        row = lax.broadcasted_iota(jnp.int32, (1, geo.rows, 1), 1)
        upper = jnp.where(row < geo.param_rows, upper, lower)
    is_upper = place[3] >= 2
    near = jnp.where(is_upper, upper, lower)
    far = jnp.where(is_upper, lower, upper).astype(BF16)
    return [near[0], permute(near[1].astype(BF16), Z1, n), permute(far[0], Z2, n), permute(far[1], Z3, n)]


def sum_any(chunks):
    return lax.psum_scatter(chunks.astype(F32), AXES, scatter_dimension=0, tiled=True)[0]


def timestep_embed(step_ids):
    half_dim = TD // 2
    freq_base = jnp.exp(jnp.arange(half_dim, dtype=F32) * (-math.log(10000.0) / half_dim))
    angle_grid = step_ids.astype(F32)[:, None] * freq_base[None, :]
    return jnp.concatenate([jnp.sin(angle_grid), jnp.cos(angle_grid)], axis=1)


def body(fast, chars, steps, embed, layer_params, cotangent):
    seqs, length = chars.shape
    tokens = seqs * length
    geo = Geometry(lax.axis_size(AXES), layer_params.shape[1], embed.shape[0])
    index = lax.axis_index(AXES).astype(jnp.int32)
    place = jnp.stack(
        [index, index * geo.shard % LANES, index * geo.embed_shard % LANES, index // 8]
    ).astype(jnp.int32)
    chunks = pack_shards(geo, place, layer_params, embed)
    emb = timestep_embed(steps).astype(BF16)
    emb_rows = jnp.concatenate([emb, jnp.zeros((8 - seqs, TD), BF16)], 0) if seqs < 8 else emb
    emb_t = emb.astype(F32).T
    chars_row, chars_col = chars.reshape(1, tokens), chars.reshape(tokens, 1)
    n = geo.devices

    cotangent = cotangent.reshape(tokens, D)
    if not fast:
        first = first_ahead(geo, seqs, place, gather_any(geo, chunks[0]), chars_col, emb_rows)
        first = first_ahead_rest(place, first)
        second = second_both(geo, fast, seqs, place, gather_any(geo, chunks[1]), first["stream"], emb_rows, cotangent)
        low_second = both_back_attn(geo, fast, 1, seqs, place, second["grad"], second, emb_t, second["rest"], chars_row)
        up_first = first_back_mlp(geo, fast, place, low_second["grad"], first)
        low_first = both_back_attn(geo, fast, 0, seqs, place, up_first["grad"], first, emb_t, up_first["rest"], chars_row)
        sums = [
            sum_any(jnp.concatenate([low_first["keep"], up_first["keep"]], 0)),
            sum_any(jnp.concatenate([low_second["keep"], second["keep"]], 0)),
            sum_any(low_first["table_out"]),
        ]
        grad_params, grad_embed = finish(geo, fast, place, sums)
        return (second["output"].reshape(seqs, length, D), grad_embed, grad_params)

    gathered, column = gather_both(geo, *chunks)
    sides = gather_sides(geo, column)
    column_other = permute(column, CORE, n)
    first = first_ahead(geo, seqs, place, gathered, chars_col, emb_rows)
    first, sides, column_other = sync(first, sides, column_other)
    corners = gather_corners(geo, *sides)
    sides_other = [permute(side, CORE, n) for side in sides]
    first = first_ahead_rest(place, first)
    first, corners, sides_other = sync(first, corners, sides_other)
    corners_other = [permute(corner, CORE, n) for corner in corners]
    pieces = gathered_pieces(geo, [column, *sides, *corners], [column_other, *sides_other, *corners_other])
    second = second_both(geo, fast, seqs, place, pieces, first["stream"], emb_rows, cotangent)
    output = second["output"].reshape(seqs, length, D)

    def cross(to_one, to_two, one, two):
        return permute(to_one, one, n), permute(to_two, two, n)

    def attn(layer, grad, found, rest):
        got = both_back_attn(geo, fast, layer, seqs, place, grad, found, emb_t, rest, chars_row)
        return (got["keep"], got["send"]) if layer == 0 else (got["grad"], got["keep"], got["send"])

    grad, rest, keep_u, send_u = (second[name] for name in ("grad", "rest", "keep", "send"))
    came_u = permute(send_u, CORE, n)
    grad, keep_l, send_l = attn(1, grad, second, rest)
    grad, keep_u, came_u, keep_l, send_l = sync(grad, keep_u, came_u, keep_l, send_l)
    came_l = permute(send_l, CORE, n)
    one_u, two_u, to_x, to_y = plane_start(geo, keep_u, came_u)
    from_u = cross(to_x, to_y, X, Y)

    got = first_back_mlp(geo, fast, place, after(grad, to_x, to_y), first)
    grad, rest, keep, send = (got[name] for name in ("grad", "rest", "keep", "send"))
    grad, rest, keep, send, came_l, from_u = sync(grad, rest, keep, send, came_l, from_u)
    came = permute(send, CORE, n)
    one_u, two_u, to_y, to_x = plane_next(one_u, two_u, *from_u)
    from_u = cross(to_y, to_x, Y, X)
    one_l, two_l, to_x_l, to_y_l = plane_start(geo, keep_l, came_l)
    from_l = cross(to_x_l, to_y_l, X, Y)

    grad = after(grad, to_x, to_y, to_x_l, to_y_l)
    low_keep, low_send = attn(0, grad, first, rest)
    low_keep, low_send, keep, came, from_u, from_l = sync(low_keep, low_send, keep, came, from_u, from_l)
    low_came = permute(low_send, CORE, n)
    one_l, two_l, to_y, to_x = plane_next(one_l, two_l, *from_l)
    from_l = cross(to_y, to_x, Y, X)
    one, two, to_x, to_y = plane_start(geo, keep, came)
    from_up = cross(to_x, to_y, X, Y)
    upper = plane_end(one_u, two_u, *from_u)

    low_came, low_keep, upper, _, _ = sync(low_came, low_keep, upper, to_x, to_y)
    low_one, low_two, to_x, to_y = plane_start(geo, low_keep, low_came)
    from_low = cross(to_x, to_y, X, Y)

    from_l, from_up, _, _ = sync(from_l, from_up, to_x, to_y)
    lower = plane_end(one_l, two_l, *from_l)
    seconds = column_sum(geo, place, upper, lower, False)
    one, two, to_y, to_x = plane_next(one, two, *from_up)
    from_up = cross(to_y, to_x, Y, X)

    from_low, _, _ = sync(from_low, to_y, to_x)
    low_one, low_two, to_y, to_x = plane_next(low_one, low_two, *from_low)
    from_low = cross(to_y, to_x, Y, X)

    from_low, from_up = sync(from_low, from_up)
    upper, lower = plane_end(one, two, *from_up), plane_end(low_one, low_two, *from_low)
    firsts = column_sum(geo, place, upper, lower, True)
    grad_params, grad_embed = finish(geo, fast, place, firsts + seconds)
    return (output, grad_embed, grad_params)


def solution(mesh):
    both = P(AXES)
    fast = dict(mesh.shape) == {"dp": 8, "fsdp": 4}
    return jax.shard_map(
        functools.partial(body, fast),
        mesh=mesh,
        in_specs=(P(AXES, None), both, both, P(None, AXES), P(AXES, None, None)),
        out_specs=(P(AXES, None, None), both, P(None, AXES)),
        check_vma=False,
    )
```

time: 273 us -> 240 us (0.88)
  the two profiles are of different devices: /device:TPU:16 before, /device:TPU:0 now
where the time goes in v3:
time: 240 us; the launch traced here: 236 us
  Pallas kernels  95.9 us (40%)
  starting transfers between devices  57.2 us (24%)
  waiting for transfers between devices  55.2 us (23%)
  other arithmetic  15.3 us (6%)
  local copies, waits for them, and re-layouts  10.3 us (4%)
    pallas_call x6, Pallas kernels, staged_call(): pl.pallas_call(whole, out_shape=tuple(results.values()), in_specs=[SM] +...  92.4 us
    ppermute x61, starting transfers between devices, permute(): lax.ppermute(value, AXES, [(d, d ^ distance) for d in range(devices)])  57.2 us
    ppermute x61, waiting for transfers between devices, permute(): lax.ppermute(value, AXES, [(d, d ^ distance) for d in range(devices)])  55.2 us
    unnamed x105, local copies, waits for them, and re-layouts  8.53 us
  transfers between devices with their start and end apart: 61, of which 23 were waited for; matrix products, arithmetic and copies ran while one was open for 8% of the time, Pallas kernels for 27%

profile of v3, /device:TPU:0, one launch (start us, length us, event | category | flops | bytes accessed | tf_op | source)
XLA Modules:
  0.0 235.9 jit_solution(5584457208775211690)
XLA Ops:
  0.7 1.4 pad_bitcast_fusion
  3.0 3.0 %collective-permute-start.2 = (bf16[800,128]{1,0:T(8,128)(2,1)S(1)}, bf16[800,128]{1,0:T(8,128)(2,1)S(1)}, u32[]{:S(2)}, u32[]{:S(2)}) collective-permute-start(bf16[800,128]{1,0:T(8,128)(2,1)S(1)} %get-tuple-element.137.refs_0_), channel_id=1, source_target_pairs={{0,4},{1,5},{2,6},{3,7},{4,0},{5,1},{6,2},{7,3},{8,12},{9,13},{10,... | collective-permute-start | bytes 614408 | tf_op jit(solution)/shard_map/ppermute | solution.py:743
  6.0 1.5 collective-permute-start.3
  7.5 1.6 collective-permute-start.1
  9.1 2.6 %collective-permute-start = (bf16[800,128]{1,0:T(8,128)(2,1)S(1)}, bf16[800,128]{1,0:T(8,128)(2,1)S(1)}, u32[]{:S(2)}, u32[]{:S(2)}) collective-permute-start(bf16[800,128]{1,0:T(8,128)(2,1)S(1)} %get-tuple-element.137.refs_0_), channel_id=1, source_target_pairs={{0,16},{1,17},{2,18},{3,19},{4,20},{5,21},{6,22},{7,23},{8,24},{9,... | collective-permute-start | bytes 614408 | tf_op jit(solution)/shard_map/ppermute | solution.py:743
  12.6 5.5 %collective-permute-done.1.refs_6_ = bf16[800,128]{1,0:T(8,128)(2,1)S(1)} collective-permute-done((bf16[800,128]{1,0:T(8,128)(2,1)S(1)}, bf16[800,128]{1,0:T(8,128)(2,1)S(1)}, u32[]{:S(2)}, u32[]{:S(2)}) %collective-permute-start.1) | collective-permute-done | bytes 204832 | tf_op jit(solution)/shard_map/ppermute | solution.py:743
  18.9 1.6 collective-permute-done.refs_12_
  22.4 3.6 %collective-permute-done.7.refs_7_ = bf16[800,128]{1,0:T(8,128)(2,1)S(1)} collective-permute-done((bf16[800,128]{1,0:T(8,128)(2,1)S(1)}, bf16[800,128]{1,0:T(8,128)(2,1)S(1)}, u32[]{:S(2)}, u32[]{:S(2)}) %collective-permute-start.7) | collective-permute-done | bytes 204832 | tf_op jit(solution)/shard_map/ppermute | solution.py:743
  26.5 1.4 collective-permute-start.6
  28.0 2.7 %collective-permute-done.5.refs_3_ = bf16[400,128]{1,0:T(8,128)(2,1)S(1)} collective-permute-done((bf16[400,128]{1,0:T(8,128)(2,1)S(1)}, bf16[400,128]{1,0:T(8,128)(2,1)S(1)}, u32[]{:S(2)}, u32[]{:S(2)}) %collective-permute-start.5) | collective-permute-done | bytes 102432 | tf_op jit(solution)/shard_map/ppermute | solution.py:743
  31.8 1.4 collective-permute-start.11
  34.0 1.3 collective-permute-start.18
  36.3 1.9 collective-permute-start.22
  38.3 2.8 %collective-permute-done.21.refs_9_ = bf16[400,128]{1,0:T(8,128)(2,1)S(1)} collective-permute-done((bf16[400,128]{1,0:T(8,128)(2,1)S(1)}, bf16[400,128]{1,0:T(8,128)(2,1)S(1)}, u32[]{:S(2)}, u32[]{:S(2)}) %collective-permute-start.21) | collective-permute-done | bytes 102432 | tf_op jit(solution)/shard_map/ppermute | solution.py:743
  41.8 3.0 %collective-permute-start.9 = (bf16[800,128]{1,0:T(8,128)(2,1)S(1)}, bf16[800,128]{1,0:T(8,128)(2,1)S(1)}, u32[]{:S(2)}, u32[]{:S(2)}) collective-permute-start(bf16[800,128]{1,0:T(8,128)(2,1)S(1)} %get-tuple-element.144), channel_id=1, source_target_pairs={{0,16},{1,17},{2,18},{3,19},{4,20},{5,21},{6,22},{7,23},{8,24},{9,... | collective-permute-start | bytes 614408 | tf_op jit(solution)/shard_map/ppermute | solution.py:743
  45.9 4.8 %collective-permute-done.10 = bf16[800,128]{1,0:T(8,128)(2,1)S(1)} collective-permute-done((bf16[800,128]{1,0:T(8,128)(2,1)S(1)}, bf16[800,128]{1,0:T(8,128)(2,1)S(1)}, u32[]{:S(2)}, u32[]{:S(2)}) %collective-permute-start.10) | collective-permute-done | bytes 204832 | tf_op jit(solution)/shard_map/ppermute | solution.py:743
  50.6 1.5 collective-permute-start.17
  52.2 2.4 %collective-permute-start.15 = (bf16[400,128]{1,0:T(8,128)(2,1)S(1)}, bf16[400,128]{1,0:T(8,128)(2,1)S(1)}, u32[]{:S(2)}, u32[]{:S(2)}) collective-permute-start(bf16[400,128]{1,0:T(8,128)(2,1)S(1)} %slice.381), channel_id=1, source_target_pairs={{0,2},{1,3},{2,0},{3,1},{4,6},{5,7},{6,4},{7,5},{8,10},{9,11},{10,... | collective-permute-start | bytes 307208 | tf_op jit(solution)/shard_map/ppermute | solution.py:743
  54.6 2.6 %collective-permute-done.15.refs_21_ = bf16[400,128]{1,0:T(8,128)(2,1)S(1)} collective-permute-done((bf16[400,128]{1,0:T(8,128)(2,1)S(1)}, bf16[400,128]{1,0:T(8,128)(2,1)S(1)}, u32[]{:S(2)}, u32[]{:S(2)}) %collective-permute-start.15) | collective-permute-done | bytes 102432 | tf_op jit(solution)/shard_map/ppermute | solution.py:743
  57.2 2.0 collective-permute-done.16.refs_22_
  62.6 18.2 %shard_map.77 = (bf16[512,1536]{1,0:T(8,128)(2,1)}, bf16[512,512]{1,0:T(8,128)(2,1)}, bf16[512,2048]{1,0:T(8,128)(2,1)}, bf16[2048,512]{1,0:T(8,128)(2,1)}, f32[...) custom-call(s32[4]{0:T(128)S(1)} %pad_add_fusion.place_ref, ...), custom_call_target="tpu_custom_call" | custom-call | flops 4000000000 | bytes 20000000 | tf_op jit(solution)/shard_map/pallas_call | solution.py:198
  82.6 1.5 collective-permute-start.30
  84.1 8.6 %shard_map.78 = (f32[512,512]{1,0:T(8,128)S(1)}, bf16[512,2048]{1,0:T(8,128)(2,1)}, bf16[512,2048]{1,0:T(8,128)(2,1)}) custom-call(s32[4]{0:T(128)S(1)} %pad_add_fusion.place_ref, bf16[512,512]{1,0:T(8,128)(2,1)S(1)} %copy-done.5, bf16[512,2048]{1,0:T(8,128)(2,1)} %get-tuple-element.220.refs_1_.refs_5_, ...), custom_call_target="tpu_custom_call" | custom-call | flops 4000000000 | bytes 20000000 | tf_op jit(solution)/shard_map/pallas_call | solution.py:198
  96.3 27.9 %shard_map.79 = (bf16[512,1536]{1,0:T(8,128)(2,1)}, bf16[512,512]{1,0:T(8,128)(2,1)}, f32[8,2048]{1,0:T(8,128)S(1)}, f32[512,512]{1,0:T(8,128)}, bf16[512,512]{1...) custom-call(s32[4]{0:T(128)S(1)} %pad_add_fusion.place_ref, ...), custom_call_target="tpu_custom_call" | custom-call | flops 10000000000 | bytes 20000000 | tf_op jit(solution)/shard_map/pallas_call | solution.py:198
  127.7 12.7 %shard_map.80 = (f32[512,512]{1,0:T(8,128)}, bf16[8,800,128]{2,1,0:T(8,128)(2,1)}, bf16[8,800,128]{2,1,0:T(8,128)(2,1)}) custom-call(s32[4]{0:T(128)S(1)} %pad_add_fusion.place_ref, f32[512,512]{1,0:T(8,128)} %get-tuple-element.197.refs_0_, bf16[512,512]{1,0:T(8,128)(2,1)S(1)} %copy-done.6, bf16[512,512]{1,0:T(8,128)(2,1)S(1)} %copy-done.8, ...), custom_call_target="tpu_custom_call" | custom-call | flops 6000000000 | bytes 20000000 | tf_op jit(solution)/shard_map/pallas_call | solution.py:198
  142.1 1.4 collective-permute-start.37
  143.6 11.6 %shard_map.81 = (f32[512,512]{1,0:T(8,128)S(1)}, bf16[4656,128]{1,0:T(8,128)(2,1)}, bf16[8,800,128]{2,1,0:T(8,128)(2,1)}, bf16[8,800,128]{2,1,0:T(8,128)(2,1)}) custom-call(s32[4]{0:T(128)S(1)} %pad_add_fusion.place_ref, f32[512,512]{1,0:T(8,128)} %get-tuple-element.215.refs_0_, bf16[2048,512]{1,0:T(8,128)(2,1)} %get-tuple-element.216.refs_3_.refs_1_, ...), custom_call_target="tpu_custom_call" | custom-call | flops 6000000000 | bytes 20000000 | tf_op jit(solution)/shard_map/pallas_call | solution.py:198
  155.5 1.4 collective-permute-start.43
  159.7 1.4 collective-permute-start.41
  161.2 13.5 %shard_map.82 = (bf16[8,800,128]{2,1,0:T(8,128)(2,1)}, bf16[8,800,128]{2,1,0:T(8,128)(2,1)}) custom-call(s32[4]{0:T(128)S(1)} %pad_add_fusion.place_ref, f32[512,512]{1,0:T(8,128)} %copy-done.1, bf16[512,512]{1,0:T(8,128)(2,1)S(1)} %copy-done.2, bf16[512,512]{1,0:T(8,128)(2,1)S(1)} %copy-done.4, bf16[512,1536]{1,0:T(8,128)(2,1)} %get-tuple-element.236.refs_3_, ...), custom_call_target="tpu_custom_call" | custom-call | flops 6000000000 | bytes 20000000 | tf_op jit(solution)/shard_map/pallas_call | solution.py:198
  175.4 1.4 fusion.22
  176.8 1.4 collective-permute-start.44
  181.8 1.5 collective-permute-start.46
  183.3 1.4 fusion.21
  186.0 1.4 collective-permute-start.50
  189.0 4.5 %collective-permute-done.47 = bf16[2,2,400,128]{3,2,1,0:T(8,128)(2,1)S(1)} collective-permute-done((bf16[2,2,400,128]{3,2,1,0:T(8,128)(2,1)S(1)}, bf16[2,2,400,128]{3,2,1,0:T(8,128)(2,1)S(1)}, u32[]{:S(2)}, u32[]{:S(2)}) %collective-permute-start.47) | collective-permute-done | bytes 409632 | tf_op jit(solution)/shard_map/ppermute | solution.py:743
  193.5 1.4 collective-permute-done.46
  194.9 1.5 fusion.11
  202.3 1.4 collective-permute-done.49
  205.6 1.5 collective-permute-start.52
  207.1 2.2 collective-permute-start.60
  209.3 1.4 collective-permute-done.51
  211.8 1.6 fusion.13
  214.6 1.8 collective-permute-start.57
  217.5 4.9 %collective-permute-done.58.refs_5_ = bf16[800,128]{1,0:T(8,128)(2,1)S(1)} collective-permute-done((bf16[800,128]{1,0:T(8,128)(2,1)S(1)}, bf16[800,128]{1,0:T(8,128)(2,1)S(1)}, u32[]{:S(2)}, u32[]{:S(2)}) %collective-permute-start.58) | collective-permute-done | bytes 204832 | tf_op jit(solution)/shard_map/ppermute | solution.py:743
  222.4 8.5 %collective-permute-done.56.refs_2_ = bf16[800,128]{1,0:T(8,128)(2,1)S(1)} collective-permute-done((bf16[800,128]{1,0:T(8,128)(2,1)S(1)}, bf16[800,128]{1,0:T(8,128)(2,1)S(1)}, u32[]{:S(2)}, u32[]{:S(2)}) %collective-permute-start.56) | collective-permute-done | bytes 204832 | tf_op jit(solution)/shard_map/ppermute | solution.py:743
  231.0 1.4 collective-permute-done.55.refs_1_
  232.4 2.7 %shard_map.83 = (f32[2,100512]{1,0:T(2,128)}, f32[8,128]{1,0:T(8,128)S(1)}) custom-call(s32[4]{0:T(128)S(1)} %pad_add_fusion.place_ref, f32[800,128]{1,0:T(8,128)S(1)} %slice_bitcast_fusion.1.refs_0_, bf16[800,128]{1,0:T(8,128)(2,1)S(1)} %collective-permute-done.55.refs_1_, bf16[800,128]{1,0:T(8,128)(2,1)S(1)} %collective-permute-done.56.refs_2_, ...), custom_call_target="tpu_custom_call" | custom-call | flops 1000 | bytes 1000 | tf_op jit(solution)/shard_map/pallas_call | solution.py:137
  (238 shorter events, 45.0 us)
Async XLA Ops:
  3.0 9.6 %collective-permute-start.2 = (bf16[800,128]{1,0:T(8,128)(2,1)S(1)}, bf16[800,128]{1,0:T(8,128)(2,1)S(1)}, u32[]{:S(2)}, u32[]{:S(2)}) collective-permute-start(bf16[800,128]{1,0:T(8,128)(2,1)S(1)} %get-tuple-element.137.refs_0_), channel_id=1, source_target_pairs={{0,4},{1,5},{2,6},{3,7},{4,0},{5,1},{6,2},{7,3},{8,12},{9,13},{10,... | collective-permute-start | bytes 614408 | tf_op jit(solution)/shard_map/ppermute | solution.py:743
  6.0 6.6 %collective-permute-start.3 = (bf16[800,128]{1,0:T(8,128)(2,1)S(1)}, bf16[800,128]{1,0:T(8,128)(2,1)S(1)}, u32[]{:S(2)}, u32[]{:S(2)}) collective-permute-start(bf16[800,128]{1,0:T(8,128)(2,1)S(1)} %get-tuple-element.137.refs_0_), channel_id=1, source_target_pairs={{0,2},{1,3},{2,0},{3,1},{4,6},{5,7},{6,4},{7,5},{8,10},{9,11},{10,... | collective-permute-start | bytes 614408 | tf_op jit(solution)/shard_map/ppermute | solution.py:743
  7.5 10.5 %collective-permute-start.1 = (bf16[800,128]{1,0:T(8,128)(2,1)S(1)}, bf16[800,128]{1,0:T(8,128)(2,1)S(1)}, u32[]{:S(2)}, u32[]{:S(2)}) collective-permute-start(bf16[800,128]{1,0:T(8,128)(2,1)S(1)} %get-tuple-element.137.refs_0_), channel_id=1, source_target_pairs={{0,8},{1,9},{2,10},{3,11},{4,12},{5,13},{6,14},{7,15},{8,0},{9,1},... | collective-permute-start | bytes 614408 | tf_op jit(solution)/shard_map/ppermute | solution.py:743
  9.1 11.4 %collective-permute-start = (bf16[800,128]{1,0:T(8,128)(2,1)S(1)}, bf16[800,128]{1,0:T(8,128)(2,1)S(1)}, u32[]{:S(2)}, u32[]{:S(2)}) collective-permute-start(bf16[800,128]{1,0:T(8,128)(2,1)S(1)} %get-tuple-element.137.refs_0_), channel_id=1, source_target_pairs={{0,16},{1,17},{2,18},{3,19},{4,20},{5,21},{6,22},{7,23},{8,24},{9,... | collective-permute-start | bytes 614408 | tf_op jit(solution)/shard_map/ppermute | solution.py:743
  18.1 8.0 %collective-permute-start.7 = (bf16[800,128]{1,0:T(8,128)(2,1)S(1)}, bf16[800,128]{1,0:T(8,128)(2,1)S(1)}, u32[]{:S(2)}, u32[]{:S(2)}) collective-permute-start(bf16[800,128]{1,0:T(8,128)(2,1)S(1)} %collective-permute-done.1.refs_6_), channel_id=1, source_target_pairs={{0,4},{1,5},{2,6},{3,7},{4,0},{5,1},{6,2},{7,3},{8,12},{9,13},{10,... | collective-permute-start | bytes 614408 | tf_op jit(solution)/shard_map/ppermute | solution.py:743
  18.6 7.9 %collective-permute-start.8 = (bf16[800,128]{1,0:T(8,128)(2,1)S(1)}, bf16[800,128]{1,0:T(8,128)(2,1)S(1)}, u32[]{:S(2)}, u32[]{:S(2)}) collective-permute-start(bf16[800,128]{1,0:T(8,128)(2,1)S(1)} %collective-permute-done.1.refs_6_), channel_id=1, source_target_pairs={{0,2},{1,3},{2,0},{3,1},{4,6},{5,7},{6,4},{7,5},{8,10},{9,11},{10,... | collective-permute-start | bytes 614408 | tf_op jit(solution)/shard_map/ppermute | solution.py:743
  20.5 11.2 %collective-permute-start.4 = (bf16[800,128]{1,0:T(8,128)(2,1)S(1)}, bf16[800,128]{1,0:T(8,128)(2,1)S(1)}, u32[]{:S(2)}, u32[]{:S(2)}) collective-permute-start(bf16[800,128]{1,0:T(8,128)(2,1)S(1)} %collective-permute-done.refs_12_), channel_id=1, source_target_pairs={{0,8},{1,9},{2,10},{3,11},{4,12},{5,13},{6,14},{7,15},{8,0},{9,1},... | collective-permute-start | bytes 614408 | tf_op jit(solution)/shard_map/ppermute | solution.py:743
  20.9 13.1 %collective-permute-start.13 = (bf16[800,128]{1,0:T(8,128)(2,1)S(1)}, bf16[800,128]{1,0:T(8,128)(2,1)S(1)}, u32[]{:S(2)}, u32[]{:S(2)}) collective-permute-start(bf16[800,128]{1,0:T(8,128)(2,1)S(1)} %collective-permute-done.refs_12_), channel_id=1, source_target_pairs={{0,4},{1,5},{2,6},{3,7},{4,0},{5,1},{6,2},{7,3},{8,12},{9,13},{10,... | collective-permute-start | bytes 614408 | tf_op jit(solution)/shard_map/ppermute | solution.py:743
  21.4 12.6 %collective-permute-start.14 = (bf16[800,128]{1,0:T(8,128)(2,1)S(1)}, bf16[800,128]{1,0:T(8,128)(2,1)S(1)}, u32[]{:S(2)}, u32[]{:S(2)}) collective-permute-start(bf16[800,128]{1,0:T(8,128)(2,1)S(1)} %collective-permute-done.refs_12_), channel_id=1, source_target_pairs={{0,2},{1,3},{2,0},{3,1},{4,6},{5,7},{6,4},{7,5},{8,10},{9,11},{10,... | collective-permute-start | bytes 614408 | tf_op jit(solution)/shard_map/ppermute | solution.py:743
  31.8 10.0 %collective-permute-start.11 = (bf16[800,128]{1,0:T(8,128)(2,1)S(1)}, bf16[800,128]{1,0:T(8,128)(2,1)S(1)}, u32[]{:S(2)}, u32[]{:S(2)}) collective-permute-start(bf16[800,128]{1,0:T(8,128)(2,1)S(1)} %collective-permute-done.4.refs_18_), channel_id=1, source_target_pairs={{0,4},{1,5},{2,6},{3,7},{4,0},{5,1},{6,2},{7,3},{8,12},{9,13},{10,... | collective-permute-start | bytes 614408 | tf_op jit(solution)/shard_map/ppermute | solution.py:743
  33.2 11.6 %collective-permute-start.12 = (bf16[800,128]{1,0:T(8,128)(2,1)S(1)}, bf16[800,128]{1,0:T(8,128)(2,1)S(1)}, u32[]{:S(2)}, u32[]{:S(2)}) collective-permute-start(bf16[800,128]{1,0:T(8,128)(2,1)S(1)} %collective-permute-done.4.refs_18_), channel_id=1, source_target_pairs={{0,2},{1,3},{2,0},{3,1},{4,6},{5,7},{6,4},{7,5},{8,10},{9,11},{10,... | collective-permute-start | bytes 614408 | tf_op jit(solution)/shard_map/ppermute | solution.py:743
  34.0 10.9 %collective-permute-start.18 = (bf16[400,128]{1,0:T(8,128)(2,1)S(1)}, bf16[400,128]{1,0:T(8,128)(2,1)S(1)}, u32[]{:S(2)}, u32[]{:S(2)}) collective-permute-start(bf16[400,128]{1,0:T(8,128)(2,1)S(1)} %slice.383), channel_id=1, source_target_pairs={{0,2},{1,3},{2,0},{3,1},{4,6},{5,7},{6,4},{7,5},{8,10},{9,11},{10,... | collective-permute-start | bytes 307208 | tf_op jit(solution)/shard_map/ppermute | solution.py:743
  41.8 8.9 %collective-permute-start.10 = (bf16[800,128]{1,0:T(8,128)(2,1)S(1)}, bf16[800,128]{1,0:T(8,128)(2,1)S(1)}, u32[]{:S(2)}, u32[]{:S(2)}) collective-permute-start(bf16[800,128]{1,0:T(8,128)(2,1)S(1)} %get-tuple-element.144), channel_id=1, source_target_pairs={{0,8},{1,9},{2,10},{3,11},{4,12},{5,13},{6,14},{7,15},{8,0},{9,1},... | collective-permute-start | bytes 614408 | tf_op jit(solution)/shard_map/ppermute | solution.py:743
  41.8 8.8 %collective-permute-start.9 = (bf16[800,128]{1,0:T(8,128)(2,1)S(1)}, bf16[800,128]{1,0:T(8,128)(2,1)S(1)}, u32[]{:S(2)}, u32[]{:S(2)}) collective-permute-start(bf16[800,128]{1,0:T(8,128)(2,1)S(1)} %get-tuple-element.144), channel_id=1, source_target_pairs={{0,16},{1,17},{2,18},{3,19},{4,20},{5,21},{6,22},{7,23},{8,24},{9,... | collective-permute-start | bytes 614408 | tf_op jit(solution)/shard_map/ppermute | solution.py:743
  44.8 14.8 %collective-permute-start.20 = (bf16[3200,128]{1,0:T(8,128)(2,1)S(1)}, bf16[3200,128]{1,0:T(8,128)(2,1)S(1)}, u32[]{:S(2)}, u32[]{:S(2)}) collective-permute-start(bf16[3200,128]{1,0:T(8,128)(2,1)S(1)} %constant_dynamic-update-slice_fusion.4), channel_id=1, source_target_pairs={{0,1},{1,0},{2,3},{3,2},{4,5},{5,4},{6,7},{7,6},{8,9},{9,8},{10,11... | collective-permute-start | bytes 2457608 | tf_op jit(solution)/shard_map/ppermute | solution.py:743
  44.9 15.8 %collective-permute-start.23 = (bf16[3200,128]{1,0:T(8,128)(2,1)S(1)}, bf16[3200,128]{1,0:T(8,128)(2,1)S(1)}, u32[]{:S(2)}, u32[]{:S(2)}) collective-permute-start(bf16[3200,128]{1,0:T(8,128)(2,1)S(1)} %constant_dynamic-update-slice_fusion.9), channel_id=1, source_target_pairs={{0,1},{1,0},{2,3},{3,2},{4,5},{5,4},{6,7},{7,6},{8,9},{9,8},{10,11... | collective-permute-start | bytes 2457608 | tf_op jit(solution)/shard_map/ppermute | solution.py:743
  50.6 8.6 %collective-permute-start.17 = (bf16[800,128]{1,0:T(8,128)(2,1)S(1)}, bf16[800,128]{1,0:T(8,128)(2,1)S(1)}, u32[]{:S(2)}, u32[]{:S(2)}) collective-permute-start(bf16[800,128]{1,0:T(8,128)(2,1)S(1)} %collective-permute-done.9), channel_id=1, source_target_pairs={{0,8},{1,9},{2,10},{3,11},{4,12},{5,13},{6,14},{7,15},{8,0},{9,1},... | collective-permute-start | bytes 614408 | tf_op jit(solution)/shard_map/ppermute | solution.py:743
  59.5 21.3 %collective-permute-start.26 = (bf16[3200,128]{1,0:T(8,128)(2,1)S(1)}, bf16[3200,128]{1,0:T(8,128)(2,1)S(1)}, u32[]{:S(2)}, u32[]{:S(2)}) collective-permute-start(bf16[3200,128]{1,0:T(8,128)(2,1)S(1)} %constant_dynamic-update-slice_fusion.refs_0_), channel_id=1, source_target_pairs={{0,4},{1,5},{2,6},{3,7},{4,0},{5,1},{6,2},{7,3},{8,12},{9,13},{10,... | collective-permute-start | bytes 2457608 | tf_op jit(solution)/shard_map/ppermute | solution.py:743
  59.6 21.2 %collective-permute-start.27 = (bf16[3200,128]{1,0:T(8,128)(2,1)S(1)}, bf16[3200,128]{1,0:T(8,128)(2,1)S(1)}, u32[]{:S(2)}, u32[]{:S(2)}) collective-permute-start(bf16[3200,128]{1,0:T(8,128)(2,1)S(1)} %constant_dynamic-update-slice_fusion.refs_0_), channel_id=1, source_target_pairs={{0,2},{1,3},{2,0},{3,1},{4,6},{5,7},{6,4},{7,5},{8,10},{9,11},{10,... | collective-permute-start | bytes 2457608 | tf_op jit(solution)/shard_map/ppermute | solution.py:743
  60.7 20.1 %collective-permute-start.28 = (bf16[3200,128]{1,0:T(8,128)(2,1)S(1)}, bf16[3200,128]{1,0:T(8,128)(2,1)S(1)}, u32[]{:S(2)}, u32[]{:S(2)}) collective-permute-start(bf16[3200,128]{1,0:T(8,128)(2,1)S(1)} %constant_dynamic-update-slice_fusion.refs_0_), channel_id=1, source_target_pairs={{0,1},{1,0},{2,3},{3,2},{4,5},{5,4},{6,7},{7,6},{8,9},{9,8},{10,11... | collective-permute-start | bytes 2457608 | tf_op jit(solution)/shard_map/ppermute | solution.py:743
  80.8 13.1 %collective-permute-start.31 = (bf16[3200,128]{1,0:T(8,128)(2,1)S(1)}, bf16[3200,128]{1,0:T(8,128)(2,1)S(1)}, u32[]{:S(2)}, u32[]{:S(2)}) collective-permute-start(bf16[3200,128]{1,0:T(8,128)(2,1)S(1)} %collective-permute-done.26.refs_1_), channel_id=1, source_target_pairs={{0,1},{1,0},{2,3},{3,2},{4,5},{5,4},{6,7},{7,6},{8,9},{9,8},{10,11... | collective-permute-start | bytes 2457608 | tf_op jit(solution)/shard_map/ppermute | solution.py:743
  81.0 12.9 %collective-permute-start.32 = (bf16[3200,128]{1,0:T(8,128)(2,1)S(1)}, bf16[3200,128]{1,0:T(8,128)(2,1)S(1)}, u32[]{:S(2)}, u32[]{:S(2)}) collective-permute-start(bf16[3200,128]{1,0:T(8,128)(2,1)S(1)} %collective-permute-done.27.refs_2_), channel_id=1, source_target_pairs={{0,1},{1,0},{2,3},{3,2},{4,5},{5,4},{6,7},{7,6},{8,9},{9,8},{10,11... | collective-permute-start | bytes 2457608 | tf_op jit(solution)/shard_map/ppermute | solution.py:743
  81.4 12.3 %collective-permute-start.29 = (bf16[1600,128]{1,0:T(8,128)(2,1)S(1)}, bf16[1600,128]{1,0:T(8,128)(2,1)S(1)}, u32[]{:S(2)}, u32[]{:S(2)}) collective-permute-start(bf16[1600,128]{1,0:T(8,128)(2,1)S(1)} %bitcast.176), channel_id=1, source_target_pairs={{0,2},{1,3},{2,0},{3,1},{4,6},{5,7},{6,4},{7,5},{8,10},{9,11},{10,... | collective-permute-start | bytes 1228808 | tf_op jit(solution)/shard_map/ppermute | solution.py:743
  82.6 11.3 %collective-permute-start.30 = (bf16[1600,128]{1,0:T(8,128)(2,1)S(1)}, bf16[1600,128]{1,0:T(8,128)(2,1)S(1)}, u32[]{:S(2)}, u32[]{:S(2)}) collective-permute-start(bf16[1600,128]{1,0:T(8,128)(2,1)S(1)} %bitcast.177), channel_id=1, source_target_pairs={{0,4},{1,5},{2,6},{3,7},{4,0},{5,1},{6,2},{7,3},{8,12},{9,13},{10,... | collective-permute-start | bytes 1228808 | tf_op jit(solution)/shard_map/ppermute | solution.py:743
  124.2 16.2 %collective-permute-start.35 = (bf16[8,800,128]{2,1,0:T(8,128)(2,1)}, bf16[8,800,128]{2,1,0:T(8,128)(2,1)S(1)}, u32[]{:S(2)}, u32[]{:S(2)}) collective-permute-start(bf16[8,800,128]{2,1,0:T(8,128)(2,1)} %get-tuple-element.209), channel_id=1, source_target_pairs={{0,1},{1,0},{2,3},{3,2},{4,5},{5,4},{6,7},{7,6},{8,9},{9,8},{10,11... | collective-permute-start | bytes 4915208 | tf_op jit(solution)/shard_map/ppermute | solution.py:743
  140.4 14.8 %collective-permute-start.36 = (bf16[8,800,128]{2,1,0:T(8,128)(2,1)}, bf16[8,800,128]{2,1,0:T(8,128)(2,1)S(1)}, u32[]{:S(2)}, u32[]{:S(2)}) collective-permute-start(bf16[8,800,128]{2,1,0:T(8,128)(2,1)} %get-tuple-element.227), channel_id=1, source_target_pairs={{0,1},{1,0},{2,3},{3,2},{4,5},{5,4},{6,7},{7,6},{8,9},{9,8},{10,11... | collective-permute-start | bytes 4915208 | tf_op jit(solution)/shard_map/ppermute | solution.py:743
  141.0 14.2 %collective-permute-start.38 = (bf16[2,2,400,128]{3,2,1,0:T(8,128)(2,1)S(1)}, bf16[2,2,400,128]{3,2,1,0:T(8,128)(2,1)S(1)}, u32[]{:S(2)}, u32[]{:S(2)}) collective-permute-start(bf16[2,2,400,128]{3,2,1,0:T(8,128)(2,1)S(1)} %fusion.3), channel_id=1, source_target_pairs={{0,2},{1,3},{2,0},{3,1},{4,6},{5,7},{6,4},{7,5},{8,10},{9,11},{10,... | collective-permute-start | bytes 1228808 | tf_op jit(solution)/shard_map/ppermute | solution.py:743
  142.1 13.1 %collective-permute-start.37 = (bf16[2,2,400,128]{3,2,1,0:T(8,128)(2,1)S(1)}, bf16[2,2,400,128]{3,2,1,0:T(8,128)(2,1)S(1)}, u32[]{:S(2)}, u32[]{:S(2)}) collective-permute-start(bf16[2,2,400,128]{3,2,1,0:T(8,128)(2,1)S(1)} %fusion.2), channel_id=1, source_target_pairs={{0,4},{1,5},{2,6},{3,7},{4,0},{5,1},{6,2},{7,3},{8,12},{9,13},{10,... | collective-permute-start | bytes 1228808 | tf_op jit(solution)/shard_map/ppermute | solution.py:743
  155.2 20.1 %collective-permute-start.39 = (bf16[8,800,128]{2,1,0:T(8,128)(2,1)}, bf16[8,800,128]{2,1,0:T(8,128)(2,1)}, u32[]{:S(2)}, u32[]{:S(2)}) collective-permute-start(bf16[8,800,128]{2,1,0:T(8,128)(2,1)} %get-tuple-element.245), channel_id=1, source_target_pairs={{0,1},{1,0},{2,3},{3,2},{4,5},{5,4},{6,7},{7,6},{8,9},{9,8},{10,11... | collective-permute-start | bytes 4915208 | tf_op jit(solution)/shard_map/ppermute | solution.py:743
  155.5 19.1 %collective-permute-start.43 = (bf16[2,2,400,128]{3,2,1,0:T(8,128)(2,1)S(1)}, bf16[2,2,400,128]{3,2,1,0:T(8,128)(2,1)}, u32[]{:S(2)}, u32[]{:S(2)}) collective-permute-start(bf16[2,2,400,128]{3,2,1,0:T(8,128)(2,1)S(1)} %fusion.5), channel_id=1, source_target_pairs={{0,2},{1,3},{2,0},{3,1},{4,6},{5,7},{6,4},{7,5},{8,10},{9,11},{10,... | collective-permute-start | bytes 1228808 | tf_op jit(solution)/shard_map/ppermute | solution.py:743
  157.1 17.6 %collective-permute-start.42 = (bf16[2,2,400,128]{3,2,1,0:T(8,128)(2,1)S(1)}, bf16[2,2,400,128]{3,2,1,0:T(8,128)(2,1)}, u32[]{:S(2)}, u32[]{:S(2)}) collective-permute-start(bf16[2,2,400,128]{3,2,1,0:T(8,128)(2,1)S(1)} %fusion.4), channel_id=1, source_target_pairs={{0,4},{1,5},{2,6},{3,7},{4,0},{5,1},{6,2},{7,3},{8,12},{9,13},{10,... | collective-permute-start | bytes 1228808 | tf_op jit(solution)/shard_map/ppermute | solution.py:743
  158.7 16.0 %collective-permute-start.40 = (bf16[2,400,128]{2,1,0:T(8,128)(2,1)S(1)}, bf16[2,400,128]{2,1,0:T(8,128)(2,1)S(1)}, u32[]{:S(2)}, u32[]{:S(2)}) collective-permute-start(bf16[2,400,128]{2,1,0:T(8,128)(2,1)S(1)} %get-tuple-element.283), channel_id=1, source_target_pairs={{0,2},{1,3},{2,0},{3,1},{4,6},{5,7},{6,4},{7,5},{8,10},{9,11},{10,... | collective-permute-start | bytes 614408 | tf_op jit(solution)/shard_map/ppermute | solution.py:743
  159.7 14.9 %collective-permute-start.41 = (bf16[2,400,128]{2,1,0:T(8,128)(2,1)S(1)}, bf16[2,400,128]{2,1,0:T(8,128)(2,1)S(1)}, u32[]{:S(2)}, u32[]{:S(2)}) collective-permute-start(bf16[2,400,128]{2,1,0:T(8,128)(2,1)S(1)} %get-tuple-element.284), channel_id=1, source_target_pairs={{0,4},{1,5},{2,6},{3,7},{4,0},{5,1},{6,2},{7,3},{8,12},{9,13},{10,... | collective-permute-start | bytes 614408 | tf_op jit(solution)/shard_map/ppermute | solution.py:743
  175.3 9.5 %collective-permute-start.48 = (bf16[8,800,128]{2,1,0:T(8,128)(2,1)}, bf16[8,800,128]{2,1,0:T(8,128)(2,1)}, u32[]{:S(2)}, u32[]{:S(2)}) collective-permute-start(bf16[8,800,128]{2,1,0:T(8,128)(2,1)} %get-tuple-element.250), channel_id=1, source_target_pairs={{0,1},{1,0},{2,3},{3,2},{4,5},{5,4},{6,7},{7,6},{8,9},{9,8},{10,11... | collective-permute-start | bytes 4915208 | tf_op jit(solution)/shard_map/ppermute | solution.py:743
  176.8 11.7 %collective-permute-start.44 = (bf16[2,400,128]{2,1,0:T(8,128)(2,1)S(1)}, bf16[2,400,128]{2,1,0:T(8,128)(2,1)S(1)}, u32[]{:S(2)}, u32[]{:S(2)}) collective-permute-start(bf16[2,400,128]{2,1,0:T(8,128)(2,1)S(1)} %get-tuple-element.280), channel_id=1, source_target_pairs={{0,2},{1,3},{2,0},{3,1},{4,6},{5,7},{6,4},{7,5},{8,10},{9,11},{10,... | collective-permute-start | bytes 614408 | tf_op jit(solution)/shard_map/ppermute | solution.py:743
  178.2 10.8 %collective-permute-start.45 = (bf16[2,400,128]{2,1,0:T(8,128)(2,1)S(1)}, bf16[2,400,128]{2,1,0:T(8,128)(2,1)S(1)}, u32[]{:S(2)}, u32[]{:S(2)}) collective-permute-start(bf16[2,400,128]{2,1,0:T(8,128)(2,1)S(1)} %get-tuple-element.279), channel_id=1, source_target_pairs={{0,4},{1,5},{2,6},{3,7},{4,0},{5,1},{6,2},{7,3},{8,12},{9,13},{10,... | collective-permute-start | bytes 614408 | tf_op jit(solution)/shard_map/ppermute | solution.py:743
  179.6 13.9 %collective-permute-start.47 = (bf16[2,2,400,128]{3,2,1,0:T(8,128)(2,1)S(1)}, bf16[2,2,400,128]{3,2,1,0:T(8,128)(2,1)S(1)}, u32[]{:S(2)}, u32[]{:S(2)}) collective-permute-start(bf16[2,2,400,128]{3,2,1,0:T(8,128)(2,1)S(1)} %fusion.7), channel_id=1, source_target_pairs={{0,2},{1,3},{2,0},{3,1},{4,6},{5,7},{6,4},{7,5},{8,10},{9,11},{10,... | collective-permute-start | bytes 1228808 | tf_op jit(solution)/shard_map/ppermute | solution.py:743
  181.8 13.1 %collective-permute-start.46 = (bf16[2,2,400,128]{3,2,1,0:T(8,128)(2,1)S(1)}, bf16[2,2,400,128]{3,2,1,0:T(8,128)(2,1)S(1)}, u32[]{:S(2)}, u32[]{:S(2)}) collective-permute-start(bf16[2,2,400,128]{3,2,1,0:T(8,128)(2,1)S(1)} %fusion.6), channel_id=1, source_target_pairs={{0,4},{1,5},{2,6},{3,7},{4,0},{5,1},{6,2},{7,3},{8,12},{9,13},{10,... | collective-permute-start | bytes 1228808 | tf_op jit(solution)/shard_map/ppermute | solution.py:743
  186.0 16.3 %collective-permute-start.50 = (bf16[2,2,400,128]{3,2,1,0:T(8,128)(2,1)S(1)}, bf16[2,2,400,128]{3,2,1,0:T(8,128)(2,1)S(1)}, u32[]{:S(2)}, u32[]{:S(2)}) collective-permute-start(bf16[2,2,400,128]{3,2,1,0:T(8,128)(2,1)S(1)} %fusion.9), channel_id=1, source_target_pairs={{0,2},{1,3},{2,0},{3,1},{4,6},{5,7},{6,4},{7,5},{8,10},{9,11},{10,... | collective-permute-start | bytes 1228808 | tf_op jit(solution)/shard_map/ppermute | solution.py:743
  188.5 15.2 %collective-permute-start.49 = (bf16[2,2,400,128]{3,2,1,0:T(8,128)(2,1)S(1)}, bf16[2,2,400,128]{3,2,1,0:T(8,128)(2,1)S(1)}, u32[]{:S(2)}, u32[]{:S(2)}) collective-permute-start(bf16[2,2,400,128]{3,2,1,0:T(8,128)(2,1)S(1)} %fusion.8), channel_id=1, source_target_pairs={{0,4},{1,5},{2,6},{3,7},{4,0},{5,1},{6,2},{7,3},{8,12},{9,13},{10,... | collective-permute-start | bytes 1228808 | tf_op jit(solution)/shard_map/ppermute | solution.py:743
  196.5 19.9 %collective-permute-start.59 = (bf16[800,128]{1,0:T(8,128)(2,1)S(1)}, bf16[800,128]{1,0:T(8,128)(2,1)S(1)}, u32[]{:S(2)}, u32[]{:S(2)}) collective-permute-start(bf16[800,128]{1,0:T(8,128)(2,1)S(1)} %get-tuple-element.286), channel_id=1, source_target_pairs={{0,16},{1,17},{2,18},{3,19},{4,20},{5,21},{6,22},{7,23},{8,24},{9,... | collective-permute-start | bytes 614408 | tf_op jit(solution)/shard_map/ppermute | solution.py:743
  198.6 8.5 %collective-permute-start.53 = (bf16[2,400,128]{2,1,0:T(8,128)(2,1)S(1)}, bf16[2,400,128]{2,1,0:T(8,128)(2,1)S(1)}, u32[]{:S(2)}, u32[]{:S(2)}) collective-permute-start(bf16[2,400,128]{2,1,0:T(8,128)(2,1)S(1)} %get-tuple-element.278), channel_id=1, source_target_pairs={{0,2},{1,3},{2,0},{3,1},{4,6},{5,7},{6,4},{7,5},{8,10},{9,11},{10,... | collective-permute-start | bytes 614408 | tf_op jit(solution)/shard_map/ppermute | solution.py:743
  199.5 9.8 %collective-permute-start.54 = (bf16[2,400,128]{2,1,0:T(8,128)(2,1)S(1)}, bf16[2,400,128]{2,1,0:T(8,128)(2,1)S(1)}, u32[]{:S(2)}, u32[]{:S(2)}) collective-permute-start(bf16[2,400,128]{2,1,0:T(8,128)(2,1)S(1)} %get-tuple-element.277), channel_id=1, source_target_pairs={{0,4},{1,5},{2,6},{3,7},{4,0},{5,1},{6,2},{7,3},{8,12},{9,13},{10,... | collective-permute-start | bytes 614408 | tf_op jit(solution)/shard_map/ppermute | solution.py:743
  207.1 10.3 %collective-permute-start.60 = (bf16[800,128]{1,0:T(8,128)(2,1)S(1)}, bf16[800,128]{1,0:T(8,128)(2,1)S(1)}, u32[]{:S(2)}, u32[]{:S(2)}) collective-permute-start(bf16[800,128]{1,0:T(8,128)(2,1)S(1)} %get-tuple-element.285), channel_id=1, source_target_pairs={{0,24},{1,25},{2,26},{3,27},{4,28},{5,29},{6,30},{7,31},{8,16},{9,... | collective-permute-start | bytes 614408 | tf_op jit(solution)/shard_map/ppermute | solution.py:743
  209.3 13.1 %collective-permute-start.58 = (bf16[800,128]{1,0:T(8,128)(2,1)S(1)}, bf16[800,128]{1,0:T(8,128)(2,1)S(1)}, u32[]{:S(2)}, u32[]{:S(2)}) collective-permute-start(bf16[800,128]{1,0:T(8,128)(2,1)S(1)} %fusion.27), channel_id=1, source_target_pairs={{0,8},{1,9},{2,10},{3,11},{4,12},{5,13},{6,14},{7,15},{8,0},{9,1},... | collective-permute-start | bytes 614408 | tf_op jit(solution)/shard_map/ppermute | solution.py:743
  213.8 17.2 %collective-permute-start.56 = (bf16[800,128]{1,0:T(8,128)(2,1)S(1)}, bf16[800,128]{1,0:T(8,128)(2,1)S(1)}, u32[]{:S(2)}, u32[]{:S(2)}) collective-permute-start(bf16[800,128]{1,0:T(8,128)(2,1)S(1)} %get-tuple-element.288), channel_id=1, source_target_pairs={{0,16},{1,17},{2,18},{3,19},{4,20},{5,21},{6,22},{7,23},{8,24},{9,... | collective-permute-start | bytes 614408 | tf_op jit(solution)/shard_map/ppermute | solution.py:743
  214.6 16.4 %collective-permute-start.57 = (bf16[800,128]{1,0:T(8,128)(2,1)S(1)}, bf16[800,128]{1,0:T(8,128)(2,1)S(1)}, u32[]{:S(2)}, u32[]{:S(2)}) collective-permute-start(bf16[800,128]{1,0:T(8,128)(2,1)S(1)} %get-tuple-element.287), channel_id=1, source_target_pairs={{0,24},{1,25},{2,26},{3,27},{4,28},{5,29},{6,30},{7,31},{8,16},{9,... | collective-permute-start | bytes 614408 | tf_op jit(solution)/shard_map/ppermute | solution.py:743
  216.4 16.0 %collective-permute-start.55 = (bf16[800,128]{1,0:T(8,128)(2,1)S(1)}, bf16[800,128]{1,0:T(8,128)(2,1)S(1)}, u32[]{:S(2)}, u32[]{:S(2)}) collective-permute-start(bf16[800,128]{1,0:T(8,128)(2,1)S(1)} %fusion.26), channel_id=1, source_target_pairs={{0,8},{1,9},{2,10},{3,11},{4,12},{5,13},{6,14},{7,15},{8,0},{9,1},... | collective-permute-start | bytes 614408 | tf_op jit(solution)/shard_map/ppermute | solution.py:743
  (54 other events, 331.3 us)
